TPU v7x, 32 devices: a whole 2x2x4 slice. The times are simulated.
32 devices in a mesh: rows: 8 (over y, x, core), chan: 4 (over z).
Axes of the slice: x: 2, y: 2, z: 4, core: 2. Of those that a mesh axis runs over, the one named last changes fastest.
Arguments:
- features: bfloat16 [4, 8192, 256], P('chan', 'rows'), may hold values from -6 to 6
- indices: int32 [4, 8192], P('chan', 'rows'), may hold values from 0 to 16383
- img_width: int32 [4, 32], P('chan'), may hold values from 0 to 32, as said below
- img_start: int32 [4, 32], P('chan'), may hold values from 0 to 8192, as said below
- codebook: bfloat16 [16384, 256], P('chan'), may hold values from -6 to 6
- w_in: bfloat16 [256, 512], replicated, may hold values from -0.375 to 0.375
- b_in: float32 [512], replicated, may hold values from -1.8 to 1.8
- gn1_gain: float32 [512], replicated, may hold values from 0.5 to 1.5
- gn1_bias: float32 [512], replicated, may hold values from -1.8 to 1.8
- conv1_w: bfloat16 [3, 3, 512, 512], replicated, may hold values from -0.09375 to 0.09375
- conv1_b: float32 [512], replicated, may hold values from -1.8 to 1.8
- gn2_gain: float32 [512], replicated, may hold values from 0.5 to 1.5
- gn2_bias: float32 [512], replicated, may hold values from -1.8 to 1.8
- conv2_w: bfloat16 [3, 3, 512, 512], replicated, may hold values from -0.1875 to 0.1875
- conv2_b: float32 [512], replicated, may hold values from -1.8 to 1.8
- gn3_gain: float32 [512], replicated, may hold values from 0.5 to 1.5
- gn3_bias: float32 [512], replicated, may hold values from -1.8 to 1.8
- w_query: bfloat16 [512, 512], replicated, may hold values from -0.5 to 0.5
- b_query: float32 [512], replicated, may hold values from -1.8 to 1.8
- w_key: bfloat16 [512, 512], replicated, may hold values from -0.25 to 0.25
- w_value: bfloat16 [512, 512], replicated, may hold values from -0.25 to 0.25
- b_value: float32 [512], replicated, may hold values from -1.8 to 1.8
- w_proj: bfloat16 [512, 512], replicated, may hold values from -3 to 3
- b_proj: float32 [512], replicated, may hold values from -1.8 to 1.8
- cotangent: bfloat16 [4, 8192, 512], P('chan', 'rows'), may hold values from -6 to 6
Outputs:
- output: bfloat16 [4, 8192, 512], P('chan', 'rows')
- feature_grad: bfloat16 [4, 8192, 256], P('chan', 'rows')
- codebook_grad: float32 [16384, 256], P('chan')
- grad_w_in: float32 [256, 512], replicated
- grad_b_in: float32 [512], replicated
- grad_gn1_gain: float32 [512], replicated
- grad_gn1_bias: float32 [512], replicated
- grad_conv1_w: float32 [3, 3, 512, 512], replicated
- grad_conv1_b: float32 [512], replicated
- grad_gn2_gain: float32 [512], replicated
- grad_gn2_bias: float32 [512], replicated
- grad_conv2_w: float32 [3, 3, 512, 512], replicated
- grad_conv2_b: float32 [512], replicated
- grad_gn3_gain: float32 [512], replicated
- grad_gn3_bias: float32 [512], replicated
- grad_w_query: float32 [512, 512], replicated
- grad_b_query: float32 [512], replicated
- grad_w_key: float32 [512, 512], replicated
- grad_w_value: float32 [512, 512], replicated
- grad_b_value: float32 [512], replicated
- grad_w_proj: float32 [512, 512], replicated
- grad_b_proj: float32 [512], replicated
Inputs may be any that keep to these rules, and one draw needn't show every extreme that they name: `img_width`: each group's images in slot order have sides half of 32, three quarters of 32 or 32; the first has three quarters of 32, the second 32; slots after the last image hold 0. `img_start`: images follow one another without gaps from pixel 0 and fill the group's 8192 pixels; no image but the last ends at a multiple of 1024 pixels; unused slots hold 8192.
All inputs are finite; a program needn't handle non-finite values.
Results may differ from a plain program's by a relative error of at most 0.02.
Values may be sent and summed in bfloat16 or wider, within the bound.
No kernel may reach another device: no remote copies, remote signals or barrier semaphores. Data moves between devices by JAX's collectives and lax.ppermute only.
A program may use at most 256 MiB of HBM per device.

v0:
```python
import math

import jax
import jax.numpy as jnp
from jax import lax
from jax.sharding import PartitionSpec as P

GN_GROUPS = 32
GRID = 32
QBLOCK = 512


epsilon = 1e-06
highest = lax.Precision.HIGHEST
masked_score = -1e30


def padded(block, sides, width):
    for axis, dim in sides:
        count = lax.axis_size(axis)
        forward = [(i, i + 1) for i in range(count - 1)]
        backward = [(target, source) for source, target in forward]
        low = lax.ppermute(
            lax.slice_in_dim(block, block.shape[dim] - width, None, axis=dim), axis, forward
        )
        high = lax.ppermute(lax.slice_in_dim(block, 0, width, axis=dim), axis, backward)
        block = jnp.concatenate([low, block, high], axis=dim)
    return block


def from_behind(array, axis, by):
    length = lax.axis_size(axis)
    pairs = [(i, i + by) for i in range(length) if 0 <= i + by < length]
    return lax.ppermute(array, axis, pairs)


def layout(positions, widths, starts, stream_len):
    before = (starts[None, :] <= positions[:, None]).astype(jnp.int32)
    image_id = jnp.sum(before, axis=1) - 1
    inside = (positions >= 0) & (positions < stream_len)
    image_id = jnp.where(inside, image_id, -1)
    slot_ids = jnp.arange(widths.shape[0], dtype=jnp.int32)
    choose = (image_id[:, None] == slot_ids[None, :]).astype(jnp.int32)
    side_len = jnp.sum(choose * widths[None, :], axis=1)
    begin_at = jnp.sum(choose * starts[None, :], axis=1)
    offset = positions - begin_at
    safe_side = jnp.maximum(side_len, 1)
    return (image_id, side_len, offset // safe_side, offset % safe_side)


def tap_table(side_len, row_at, col_at, rim_len):
    pixel_count = side_len.shape[0]
    centre = jnp.arange(pixel_count, dtype=jnp.int32) + rim_len
    index_list = []
    valid_list = []
    for delta_r in (-1, 0, 1):
        for delta_c in (-1, 0, 1):
            index_list.append(centre + delta_r * side_len + delta_c)
            valid_list.append(
                (row_at + delta_r >= 0)
                & (row_at + delta_r < side_len)
                & (col_at + delta_c >= 0)
                & (col_at + delta_c < side_len)
            )
    return (jnp.stack(index_list, axis=1), jnp.stack(valid_list, axis=1))


def gather_taps(extended, tap_index, tap_valid):
    picked = jnp.take(extended, tap_index, axis=0)
    picked = jnp.where(tap_valid[:, :, None], picked, jnp.zeros((), extended.dtype))
    return picked.reshape(tap_index.shape[0], -1)


def extend_rows(values, rim_len):
    return padded(values, (("rows", 0),), rim_len)


def flip_taps(weight):
    taps_in = weight.reshape(9, weight.shape[2], weight.shape[3])
    return jnp.transpose(taps_in[::-1], (0, 2, 1)).reshape(9 * weight.shape[3], weight.shape[2])


def group_sums(values, onehot):
    sum_rows = jnp.dot(onehot.T, values, precision=highest)
    return sum_rows.reshape(sum_rows.shape[0], GN_GROUPS, -1).sum(axis=2)


def expand(stat_rows, onehot, channels):
    per_pixel = jnp.dot(onehot, stat_rows, precision=highest)
    return jnp.repeat(per_pixel, channels // stat_rows.shape[1], axis=1)


def add_beside(extended, slots):
    return extended[:slots] + extended[slots : 2 * slots] + extended[2 * slots :]


def norm_forward(values, onehot, counts):
    slots = onehot.shape[1]
    stacked = jnp.stack([group_sums(values, onehot), group_sums(values * values, onehot)], axis=1)
    extended = padded(stacked, (("rows", 0),), slots)
    totals = add_beside(extended, slots)
    first_sum = totals[:, 0]
    second_sum = totals[:, 1]
    mean_val = first_sum / counts[:, None]
    variance = second_sum / counts[:, None] - mean_val * mean_val
    inv_std = lax.rsqrt(variance + epsilon)
    channels = values.shape[1]
    mean_full = expand(mean_val, onehot, channels)
    inv_full = expand(inv_std, onehot, channels)
    return ((values - mean_full) * inv_full, inv_full)


def norm_backward(upstream, normed, inv_full, gain, onehot, counts):
    slots = onehot.shape[1]
    scaled = upstream * gain
    stacked = jnp.stack([group_sums(scaled, onehot), group_sums(scaled * normed, onehot)], axis=1)
    extended = padded(stacked, (("rows", 0),), slots)
    totals = add_beside(extended, slots)
    mean_grad = totals[:, 0]
    mean_cross = totals[:, 1]
    channels = upstream.shape[1]
    grad_full = expand(mean_grad / counts[:, None], onehot, channels)
    cross_full = expand(mean_cross / counts[:, None], onehot, channels)
    grad_in = inv_full * (scaled - grad_full - normed * cross_full)
    return (grad_in, jnp.sum(upstream * normed, axis=0), jnp.sum(upstream, axis=0))


def pass_rim(rim_rows, step_by):
    return from_behind(rim_rows.astype(jnp.bfloat16), "rows", step_by).astype(rim_rows.dtype)


def per_device(
    features,
    indices,
    img_width,
    img_start,
    codebook,
    w_in,
    b_in,
    gn1_gain,
    gn1_bias,
    conv1_w,
    conv1_b,
    gn2_gain,
    gn2_bias,
    conv2_w,
    conv2_b,
    gn3_gain,
    gn3_bias,
    w_query,
    b_query,
    w_key,
    w_value,
    b_value,
    w_proj,
    b_proj,
    cotangent,
):
    pixels = features.shape[1]
    chans = w_in.shape[1]
    widths = img_width[0]
    starts = img_start[0]
    stream_len = pixels * lax.axis_size("rows")
    first_pos = lax.axis_index("rows") * pixels
    conv_rim = 2 * GRID
    key_rim = GRID * GRID
    window = QBLOCK + 2 * key_rim
    score_scale = 1.0 / math.sqrt(chans)
    positions = first_pos + jnp.arange(pixels, dtype=jnp.int32)
    image_id, side_len, row_at, col_at = layout(positions, widths, starts, stream_len)
    key_pos = first_pos - key_rim + jnp.arange(pixels + 2 * key_rim, dtype=jnp.int32)
    key_ids = layout(key_pos, widths, starts, stream_len)[0]
    tap_index, tap_valid = tap_table(side_len, row_at, col_at, conv_rim)
    onehot = (image_id[:, None] == jnp.arange(widths.shape[0], dtype=jnp.int32)[None, :]).astype(
        jnp.float32
    )
    counts = (jnp.maximum(widths * widths, 1) * (chans // GN_GROUPS)).astype(jnp.float32)
    key_shard = codebook.shape[0]
    shard_at = lax.axis_index("chan") * key_shard
    own_index = indices[0]
    all_index, full_book = (
        lax.all_gather(own_index, "chan", axis=0, tiled=True),
        lax.all_gather(codebook, "chan", axis=0, tiled=True),
    )
    code_rows = jnp.take(full_book, own_index, axis=0).astype(jnp.float32)
    quant_rows = (features[0].astype(jnp.float32) + code_rows).astype(jnp.bfloat16)
    resid_in = jnp.dot(quant_rows, w_in, preferred_element_type=jnp.float32) + b_in
    norm_one, inv_one = norm_forward(resid_in, onehot, counts)
    pre_one = norm_one * gn1_gain + gn1_bias
    sig_one = jax.nn.sigmoid(pre_one)
    act_one = (pre_one * sig_one).astype(jnp.bfloat16)
    patch_one = gather_taps(extend_rows(act_one, conv_rim), tap_index, tap_valid)
    hid_one = (
        jnp.dot(patch_one, conv1_w.reshape(-1, chans), preferred_element_type=jnp.float32) + conv1_b
    )
    norm_two, inv_two = norm_forward(hid_one, onehot, counts)
    pre_two = norm_two * gn2_gain + gn2_bias
    sig_two = jax.nn.sigmoid(pre_two)
    act_two = (pre_two * sig_two).astype(jnp.bfloat16)
    patch_two = gather_taps(extend_rows(act_two, conv_rim), tap_index, tap_valid)
    hid_two = (
        jnp.dot(patch_two, conv2_w.reshape(-1, chans), preferred_element_type=jnp.float32) + conv2_b
    )
    resid_mid = resid_in + hid_two
    norm_three, inv_three = norm_forward(resid_mid, onehot, counts)
    normed_low = (norm_three * gn3_gain + gn3_bias).astype(jnp.bfloat16)
    query_rows = (
        jnp.dot(normed_low, w_query, preferred_element_type=jnp.float32) + b_query
    ).astype(jnp.bfloat16)
    kv_weight = jnp.concatenate([w_key, w_value], axis=1)
    kv_bias = jnp.concatenate([jnp.zeros_like(b_value), b_value])
    kv_rows = (jnp.dot(normed_low, kv_weight, preferred_element_type=jnp.float32) + kv_bias).astype(
        jnp.bfloat16
    )
    kv_ext = padded(kv_rows, (("rows", 0),), key_rim)
    block_starts = jnp.arange(pixels // QBLOCK, dtype=jnp.int32) * QBLOCK

    def block_scores(block_at):
        query_blk = lax.dynamic_slice_in_dim(query_rows, block_at, QBLOCK)
        kv_blk = lax.dynamic_slice_in_dim(kv_ext, block_at, window)
        key_blk = kv_blk[:, :chans]
        value_blk = kv_blk[:, chans:]
        id_query = lax.dynamic_slice_in_dim(image_id, block_at, QBLOCK)
        id_key = lax.dynamic_slice_in_dim(key_ids, block_at, window)
        scores = (
            jnp.einsum("qc,kc->qk", query_blk, key_blk, preferred_element_type=jnp.float32)
            * score_scale
        )
        keep_mask = (id_query[:, None] == id_key[None, :]) & (id_key[None, :] >= 0)
        return (jnp.where(keep_mask, scores, masked_score), query_blk, key_blk, value_blk)

    def block_forward(block_at):
        scores, query_blk, key_blk, value_blk = block_scores(block_at)
        row_max = jnp.max(scores, axis=1, keepdims=True)
        exp_val = jnp.exp(scores - row_max)
        row_total = jnp.sum(exp_val, axis=1, keepdims=True)
        prob_rows = (exp_val / row_total).astype(jnp.bfloat16)
        mixed_rows = jnp.dot(prob_rows, value_blk, preferred_element_type=jnp.float32)
        return (mixed_rows.astype(jnp.bfloat16), row_max[:, 0] + jnp.log(row_total[:, 0]))

    attn_blocks, lse_blocks = lax.map(block_forward, block_starts)
    attn_rows = attn_blocks.reshape(pixels, chans)
    log_norm = lse_blocks.reshape(pixels)
    output = (
        resid_mid + jnp.dot(attn_rows, w_proj, preferred_element_type=jnp.float32) + b_proj
    ).astype(jnp.bfloat16)
    d_out = cotangent[0]
    d_out_f = d_out.astype(jnp.float32)
    g_w_proj = jnp.einsum("nk,nc->kc", attn_rows, d_out, preferred_element_type=jnp.float32)
    g_b_proj = jnp.sum(d_out_f, axis=0)
    d_attn = jnp.einsum("nc,kc->nk", d_out, w_proj, preferred_element_type=jnp.float32).astype(
        jnp.bfloat16
    )

    def block_backward(grad_ext, block_at):
        scores, query_blk, key_blk, value_blk = block_scores(block_at)
        lse_blk = lax.dynamic_slice_in_dim(log_norm, block_at, QBLOCK)
        prob_rows = jnp.exp(scores - lse_blk[:, None])
        dout_blk = lax.dynamic_slice_in_dim(d_attn, block_at, QBLOCK)
        d_probs = jnp.einsum("qc,kc->qk", dout_blk, value_blk, preferred_element_type=jnp.float32)
        delta_row = jnp.sum(prob_rows * d_probs, axis=1, keepdims=True)
        d_scores = (prob_rows * (d_probs - delta_row)).astype(jnp.bfloat16)
        d_query_blk = jnp.dot(d_scores, key_blk, preferred_element_type=jnp.float32) * score_scale
        d_key_blk = (
            jnp.einsum("qk,qc->kc", d_scores, query_blk, preferred_element_type=jnp.float32)
            * score_scale
        )
        d_value_blk = jnp.einsum(
            "qk,qc->kc",
            prob_rows.astype(jnp.bfloat16),
            dout_blk,
            preferred_element_type=jnp.float32,
        )
        current = lax.dynamic_slice_in_dim(grad_ext, block_at, window)
        grad_ext = lax.dynamic_update_slice_in_dim(
            grad_ext, current + jnp.concatenate([d_key_blk, d_value_blk], axis=1), block_at, 0
        )
        return (grad_ext, d_query_blk)

    grad_init = jnp.zeros((pixels + 2 * key_rim, 2 * chans), jnp.float32)
    grad_ext, d_query_blocks = lax.scan(block_backward, grad_init, block_starts)
    from_next = pass_rim(grad_ext[:key_rim], -1)
    from_prev = pass_rim(grad_ext[pixels + key_rim :], 1)
    own_grad = grad_ext[key_rim : key_rim + pixels]
    own_grad = own_grad.at[:key_rim].add(from_prev)
    own_grad = own_grad.at[pixels - key_rim :].add(from_next)
    d_kv = own_grad.astype(jnp.bfloat16)
    d_query = d_query_blocks.reshape(pixels, chans).astype(jnp.bfloat16)
    g_w_query = jnp.einsum("nk,nc->kc", normed_low, d_query, preferred_element_type=jnp.float32)
    g_b_query = jnp.sum(d_query.astype(jnp.float32), axis=0)
    g_w_kv = jnp.einsum("nk,nc->kc", normed_low, d_kv, preferred_element_type=jnp.float32)
    g_b_value = jnp.sum(d_kv[:, chans:].astype(jnp.float32), axis=0)
    d_normed = jnp.einsum("nc,kc->nk", d_query, w_query, preferred_element_type=jnp.float32)
    d_normed = d_normed + jnp.einsum(
        "nc,kc->nk", d_kv, kv_weight, preferred_element_type=jnp.float32
    )
    d_mid_norm, g_gain_three, g_bias_three = norm_backward(
        d_normed, norm_three, inv_three, gn3_gain, onehot, counts
    )
    d_mid = d_out_f + d_mid_norm
    err_two = d_mid.astype(jnp.bfloat16)
    g_conv2_b = jnp.sum(err_two.astype(jnp.float32), axis=0)
    g_conv2_w = jnp.einsum(
        "nk,nc->kc", patch_two, err_two, preferred_element_type=jnp.float32
    ).reshape(conv2_w.shape)
    d_act_two = jnp.dot(
        gather_taps(extend_rows(err_two, conv_rim), tap_index, tap_valid),
        flip_taps(conv2_w),
        preferred_element_type=jnp.float32,
    )
    d_pre_two = d_act_two * sig_two * (1.0 + pre_two * (1.0 - sig_two))
    d_hid_one, g_gain_two, g_bias_two = norm_backward(
        d_pre_two, norm_two, inv_two, gn2_gain, onehot, counts
    )
    err_one = d_hid_one.astype(jnp.bfloat16)
    g_conv1_b = jnp.sum(err_one.astype(jnp.float32), axis=0)
    g_conv1_w = jnp.einsum(
        "nk,nc->kc", patch_one, err_one, preferred_element_type=jnp.float32
    ).reshape(conv1_w.shape)
    d_act_one = jnp.dot(
        gather_taps(extend_rows(err_one, conv_rim), tap_index, tap_valid),
        flip_taps(conv1_w),
        preferred_element_type=jnp.float32,
    )
    d_pre_one = d_act_one * sig_one * (1.0 + pre_one * (1.0 - sig_one))
    d_in_norm, g_gain_one, g_bias_one = norm_backward(
        d_pre_one, norm_one, inv_one, gn1_gain, onehot, counts
    )
    err_in = (d_mid + d_in_norm).astype(jnp.bfloat16)
    g_w_in = jnp.einsum("nk,nc->kc", quant_rows, err_in, preferred_element_type=jnp.float32)
    g_b_in = jnp.sum(err_in.astype(jnp.float32), axis=0)
    feature_grad = jnp.einsum("nc,kc->nk", err_in, w_in, preferred_element_type=jnp.float32).astype(
        jnp.bfloat16
    )
    all_grad = lax.all_gather(feature_grad, "chan", axis=0, tiled=True)
    local_code = all_index - shard_at
    segment = jnp.where((local_code >= 0) & (local_code < key_shard), local_code, key_shard)
    book_grad = jax.ops.segment_sum(
        all_grad.astype(jnp.float32), segment, num_segments=key_shard + 1
    )[:key_shard]
    book_grad = lax.psum(book_grad.astype(jnp.bfloat16), "rows").astype(jnp.float32)
    (
        g_w_in,
        g_b_in,
        g_gain_one,
        g_bias_one,
        g_conv1_w,
        g_conv1_b,
        g_gain_two,
        g_bias_two,
        g_conv2_w,
        g_conv2_b,
        g_gain_three,
        g_bias_three,
        g_w_query,
        g_b_query,
        g_w_kv,
        g_b_value,
        g_w_proj,
        g_b_proj,
    ) = lax.psum(
        (
            g_w_in,
            g_b_in,
            g_gain_one,
            g_bias_one,
            g_conv1_w,
            g_conv1_b,
            g_gain_two,
            g_bias_two,
            g_conv2_w,
            g_conv2_b,
            g_gain_three,
            g_bias_three,
            g_w_query,
            g_b_query,
            g_w_kv,
            g_b_value,
            g_w_proj,
            g_b_proj,
        ),
        ("rows", "chan"),
    )
    return (
        output[None],
        feature_grad[None],
        book_grad,
        g_w_in,
        g_b_in,
        g_gain_one,
        g_bias_one,
        g_conv1_w,
        g_conv1_b,
        g_gain_two,
        g_bias_two,
        g_conv2_w,
        g_conv2_b,
        g_gain_three,
        g_bias_three,
        g_w_query,
        g_b_query,
        g_w_kv[:, :chans],
        g_w_kv[:, chans:],
        g_b_value,
        g_w_proj,
        g_b_proj,
    )


def solution(mesh):
    placed = (
        P("chan", "rows", None),
        P("chan", "rows"),
        P("chan", None),
        P("chan", None),
        P("chan", None),
        P(),
        P(),
        P(),
        P(),
        P(),
        P(),
        P(),
        P(),
        P(),
        P(),
        P(),
        P(),
        P(),
        P(),
        P(),
        P(),
        P(),
        P(),
        P(),
        P("chan", "rows", None),
    )
    return jax.shard_map(
        per_device,
        mesh=mesh,
        in_specs=placed,
        out_specs=(
            P("chan", "rows", None),
            P("chan", "rows", None),
            P("chan", None),
            P(),
            P(),
            P(),
            P(),
            P(),
            P(),
            P(),
            P(),
            P(),
            P(),
            P(),
            P(),
            P(),
            P(),
            P(),
            P(),
            P(),
            P(),
            P(),
        ),
        check_vma=False,
    )
```

profile of v0, /device:TPU:0, one launch (start us, length us, event | category | flops | bytes accessed | tf_op | source)
XLA Modules:
  0.0 1615.5 jit_solution(11150770772238900393)
XLA Ops:
  9.8 152.2 %all-gather.4.cloned.1.call-done = bf16[16384,256]{1,0:T(8,128)(2,1)} async-done(((bf16[4096,256]{1,0:T(8,128)(2,1)}), bf16[16384,256]{1,0:T(8,128)(2,1)}) %all-gather.4.cloned.1.call-update) | async-done | bytes 8388624 | tf_op jit(solution)/shard_map/all_gather | solution.py:183
  162.0 9.1 gather_fusion
  192.0 4.4 multiply_convert_fusion.3
  197.4 4.5 collective-permute-start.2
  206.4 37.8 %gather_fusion.1 = bf16[9216,512]{1,0:T(8,128)(2,1)} fusion(bf16[1152,512]{1,0:T(8,128)(2,1)S(1)} %pad_maximum_fusion.1, s32[9216]{0:T(1024)S(1)} %broadcast_clamp_fusion), kind=kCustom, calls=%fused_computation.clone | custom fusion | bytes 18911232 | tf_op jit(solution)/shard_map/jit(_take)/gather | solution.py:69
  244.2 17.6 %reshape.728 = bf16[1024,9,512]{2,1,0:T(8,128)(2,1)} reshape(bf16[9216,512]{1,0:T(8,128)(2,1)} %gather_fusion.1) | data formatting | bytes 18874368 | tf_op jit(solution)/shard_map/jit(_take)/gather | solution.py:69
  261.8 12.1 select_select_fusion.3
  273.9 21.8 %copy.190 = bf16[1024,9,512]{0,2,1:T(8,128)(2,1)} copy(bf16[1024,9,512]{2,1,0:T(8,128)(2,1)} %select_select_fusion.3) | data formatting | bytes 18874368 | tf_op jit(solution)/shard_map/jit(_where)/select_n | solution.py:70
  295.7 9.0 fusion.233
  308.4 5.1 collective-permute-start.4
  322.7 5.2 multiply_convert_fusion.2
  328.0 5.0 collective-permute-start.6
  336.2 37.8 %gather_fusion.2 = bf16[9216,512]{1,0:T(8,128)(2,1)} fusion(bf16[1152,512]{1,0:T(8,128)(2,1)S(1)} %pad_maximum_fusion.2, s32[9216]{0:T(1024)S(1)} %broadcast_clamp_fusion), kind=kCustom, calls=%fused_computation.1.clone | custom fusion | bytes 18911232 | tf_op jit(solution)/shard_map/jit(_take)/gather | solution.py:69
  374.0 17.6 %reshape.732 = bf16[1024,9,512]{2,1,0:T(8,128)(2,1)} reshape(bf16[9216,512]{1,0:T(8,128)(2,1)} %gather_fusion.2) | data formatting | bytes 18874368 | tf_op jit(solution)/shard_map/jit(_take)/gather | solution.py:69
  391.6 12.1 select_select_fusion.2
  403.7 21.9 %copy.196 = bf16[1024,9,512]{0,2,1:T(8,128)(2,1)} copy(bf16[1024,9,512]{2,1,0:T(8,128)(2,1)} %select_select_fusion.2) | data formatting | bytes 18874368 | tf_op jit(solution)/shard_map/jit(_where)/select_n | solution.py:70
  425.6 9.1 add_add_fusion
  438.4 5.3 collective-permute-start.8
  452.9 5.1 add_convert_fusion.5
  459.4 6.3 collective-permute-start.10
  472.3 5.4 pad_maximum_fusion
  477.7 34.4 %while.28 = (s32[]{:T(128)}, bf16[2,512,512]{2,1,0:T(8,128)(2,1)}, f32[2,512]{1,0:T(2,128)S(1)}, s32[2]{0:T(128)S(1)}, s32[1024]{0:T(1024)S(1)}, /*index=5*/s32[...) while((s32[]{:T(128)}, bf16[2,512,512]{2,1,0:T(8,128)(2,1)}, ...), condition=%wide.region_13.15_spmd, body=%wide.region_10.14_spmd.sunk | while | flops 2697725952 | bytes 51443520 | solution.py:241
  481.7 4.3 fusion.282
  488.3 5.6 fusion.284
  498.9 4.3 fusion.282
  505.5 5.6 fusion.284
  512.1 6.1 broadcast_in_dim.189
  518.3 150.2 %while.29 = (s32[]{:T(128)}, f32[3072,1024]{0,1:T(8,128)}, bf16[2,512,512]{2,1,0:T(8,128)(2,1)}, s32[2]{0:T(128)S(1)}, s32[1024]{0:T(1024)S(1)}, /*index=5*/s32[...) while((s32[]{:T(128)}, f32[3072,1024]{0,1:T(8,128)}, ...), condition=%wide.region_16.18_spmd, body=%wide.region_14.17_spmd.sunk | while | flops 6732122112 | bytes 113299216 | solution.py:281
  526.4 5.0 multiply_reduce_fusion.5
  537.2 11.2 maximum_add_fusion.2
  548.5 41.2 %dynamic_update_slice.24 = f32[3072,1024]{0,1:T(8,128)} dynamic-update-slice(f32[3072,1024]{0,1:T(8,128)} %get-tuple-element.469, f32[2560,1024]{0,1:T(8,128)} %maximum_add_fusion.2, s32[]{:T(128)S(6)} %select_n.276, s32[]{:T(128)} %constant.186.clone.1..sunk.1) | dynamic-update-slice | bytes 20971524 | tf_op jit(solution)/shard_map/while/body/eval_jaxpr/dynamic_update_slice | solution.py:275
  589.7 4.1 fusion.295
  601.5 5.0 multiply_reduce_fusion.5
  612.3 11.1 maximum_add_fusion.2
  623.5 40.7 %dynamic_update_slice.24 = f32[3072,1024]{0,1:T(8,128)} dynamic-update-slice(f32[3072,1024]{0,1:T(8,128)} %get-tuple-element.469, f32[2560,1024]{0,1:T(8,128)} %maximum_add_fusion.2, s32[]{:T(128)S(6)} %select_n.276, s32[]{:T(128)} %constant.186.clone.1..sunk.1) | dynamic-update-slice | bytes 20971524 | tf_op jit(solution)/shard_map/while/body/eval_jaxpr/dynamic_update_slice | solution.py:275
  664.2 4.1 fusion.295
  668.4 8.2 convert.8
  679.4 42.3 %collective-permute-start.12 = (bf16[1024,1024]{0,1:T(8,128)(2,1)S(1)}, bf16[1024,1024]{0,1:T(8,128)(2,1)S(1)}, u32[]{:S(2)}, u32[]{:S(2)}) collective-permute-start(bf16[1024,1024]{0,1:T(8,128)(2,1)S(1)} %get-tuple-element.251), channel_id=1, source_target_pairs={{0,4},{4,8},{8,12},{12,16},{16,20},{20,24},{24,28},{1,5},{5,9},{9,... | collective-permute-start | bytes 6291464 | tf_op jit(solution)/shard_map/ppermute | solution.py:34
  736.4 41.9 %collective-permute-start.14 = (f32[32,2,32]{0,2,1:T(8,128)S(1)}, f32[32,2,32]{0,2,1:T(8,128)S(1)}, u32[]{:S(2)}, u32[]{:S(2)}) collective-permute-start(f32[32,2,32]{0,2,1:T(8,128)S(1)} %pad_maximum_fusion.8), channel_id=1, source_target_pairs={{0,4},{4,8},{8,12},{12,16},{16,20},{20,24},{24,28},{1,5},{5,9},{9,... | collective-permute-start | bytes 24584 | tf_op jit(solution)/shard_map/ppermute | solution.py:23
  790.9 7.1 fusion.223
  799.0 4.1 collective-permute-start.16
  804.4 6.8 copy.209
  811.2 4.8 rev.6
  816.8 37.6 %gather_fusion.3 = bf16[9216,512]{1,0:T(8,128)(2,1)} fusion(bf16[1152,512]{1,0:T(8,128)(2,1)S(1)} %pad_maximum_fusion.3, s32[9216]{0:T(1024)S(1)} %copy-done.3), kind=kCustom, calls=%fused_computation.2.clone | custom fusion | bytes 18911232 | tf_op jit(solution)/shard_map/jit(_take)/gather | solution.py:69
  854.4 17.6 %reshape.736 = bf16[1024,9,512]{2,1,0:T(8,128)(2,1)} reshape(bf16[9216,512]{1,0:T(8,128)(2,1)} %gather_fusion.3) | data formatting | bytes 18874368 | tf_op jit(solution)/shard_map/jit(_take)/gather | solution.py:69
  872.1 7.9 select_select_fusion.1
  880.1 23.6 %fusion.50 = f32[1024,512]{1,0:T(8,128)S(1)} fusion(f32[1024,512]{1,0:T(8,128)S(1)} %copy-done.8, bf16[9,512,512]{1,2,0:T(8,128)(2,1)} %rev.6, bf16[1024,9,512]{2,1,0:T(8,128)(2,1)S(1)} %select_select_fusion.1, f32[512]{0:T(512)S(1)} %copy-done.74, f32[512]{0:T(512)S(1)} %copy-done.58), kind=kOutput, calls=%fused_computation.67 | convolution fusion | flops 4837081088 | bytes 18354176 | tf_op jit(solution)/shard_map/dot_general | solution.py:306
  921.4 4.6 fusion.224
  927.0 4.5 collective-permute-start.20
  932.8 6.6 copy.217
  939.4 4.8 rev.7
  944.4 37.6 %gather_fusion.4 = bf16[9216,512]{1,0:T(8,128)(2,1)} fusion(bf16[1152,512]{1,0:T(8,128)(2,1)S(1)} %pad_maximum_fusion.4, s32[9216]{0:T(1024)S(1)} %copy-done.3), kind=kCustom, calls=%fused_computation.3.clone | custom fusion | bytes 18911232 | tf_op jit(solution)/shard_map/jit(_take)/gather | solution.py:69
  982.0 17.6 %reshape.740 = bf16[1024,9,512]{2,1,0:T(8,128)(2,1)} reshape(bf16[9216,512]{1,0:T(8,128)(2,1)} %gather_fusion.4) | data formatting | bytes 18874368 | tf_op jit(solution)/shard_map/jit(_take)/gather | solution.py:69
  999.6 8.0 select_select_fusion
  1007.6 23.5 %fusion.49 = f32[1024,512]{1,0:T(8,128)S(1)} fusion(f32[1024,512]{1,0:T(8,128)S(1)} %copy-done.12, bf16[9,512,512]{1,2,0:T(8,128)(2,1)} %rev.7, bf16[1024,9,512]{2,1,0:T(8,128)(2,1)S(1)} %select_select_fusion, f32[512]{0:T(512)S(1)} %copy-done.76, f32[512]{0:T(512)S(1)} %copy-done.60), kind=kOutput, calls=%fused_computation.65 | convolution fusion | flops 4837081088 | bytes 18354176 | tf_op jit(solution)/shard_map/dot_general | solution.py:320
  1039.2 13.1 all-gather
  1059.4 5.5 fusion.225
  1074.8 7.8 fusion.87
  1082.7 32.4 %all-gather.6.cloned.1.call-done = bf16[4096,256]{1,0:T(8,128)(2,1)} async-done(((bf16[1024,256]{1,0:T(8,128)(2,1)}), bf16[4096,256]{1,0:T(8,128)(2,1)}) %all-gather.6.cloned.1.call-update) | async-done | bytes 2097168 | tf_op jit(solution)/shard_map/all_gather | solution.py:335
  1115.0 25.1 %scatter_custom_fusion = f32[4097,256]{1,0:T(8,128)} fusion(s32[4096]{0:T(1024)S(1)} %and_select_fusion, bf16[4096,256]{1,0:T(8,128)(2,1)} %all-gather.6.cloned.1.call-done, f32[]{:T(128)} %constant.196.clone.1), kind=kCustom, calls=%fused_computation.57 | custom fusion | flops 2097152 | bytes 6292484 | tf_op jit(solution)/shard_map/scatter-add | solution.py:338
  1145.2 11.7 fusion.89
  1163.9 39.5 %all-reduce.1 = (f32[512]{0:T(512)}, f32[512]{0:T(512)}, f32[512]{0:T(512)}, f32[512]{0:T(512)}, f32[512]{0:T(512)}, /*index=5*/f32[512]{0:T(512)}, f32[512]{0:T...) all-reduce(f32[512]{0:T(512)S(1)} %get-tuple-element.258, ...), channel_id=1, replica_groups=mesh['rows'=8,'chan'=4] {'rows','chan'}, use_global_device_ids=true, to_apply=%region_27.29 | all-reduce | flops 6144 | bytes 49152 | tf_op jit(solution)/shard_map/psum | solution.py:361
  1208.8 380.3 %all-reduce.8.cloned.1.call-done = (f32[256,512]{1,0:T(8,128)}, f32[3,3,512,512]{3,2,1,0:T(8,128)}, f32[3,3,512,512]{3,2,1,0:T(8,128)}, f32[512,512]{1,0:T(8,128...) async-done(((f32[256,512]{1,0:T(8,128)}, f32[3,3,512,512]{3,2,1,0:T(8,128)}, f32[3,3,512,512]{3,2,1,0:T(8,128)}, f32[512,512]{1,0:T(8,128)}, f32[512,1024]{1,0:T(8,128)}, ...) | async-done | bytes 23592976 | tf_op jit(solution)/shard_map/psum | solution.py:361
  1593.0 9.2 copy.278
  (394 shorter events, 199.5 us)
Async XLA Ops:
  7.2 463.4 %copy-start = (bf16[512,512]{1,0:T(8,128)(2,1)S(1)}, bf16[512,512]{1,0:T(8,128)(2,1)}, u32[]{:S(2)}) copy-start(bf16[512,512]{1,0:T(8,128)(2,1)} %param.56) | copy-start | bytes 1572868
  7.2 154.8 %all-gather.4.cloned.1.call-start = ((), (), s32[]{:S(2)}) async-start(), calls=%async_computation | async-start | bytes 10485760 | tf_op jit(solution)/shard_map/all_gather | solution.py:183
  8.0 1107.1 %all-gather.6.cloned.1.call-start = ((), (), s32[]{:S(2)}) async-start(), calls=%async_computation.1 | async-start | bytes 2621440 | tf_op jit(solution)/shard_map/all_gather | solution.py:335
  9.0 162.1 %copy-start.71 = (pred[1024]{0:T(1024)(128)(4,1)}, pred[1024]{0:T(1024)(128)(4,1)S(1)}, u32[]{:S(2)}) copy-start(pred[1024]{0:T(1024)(128)(4,1)S(1)} %compare_and_fusion.4) | copy-start | bytes 3076
  9.8 326.3 %copy-start.2 = (s32[9216]{0:T(1024)}, s32[9216]{0:T(1024)S(1)}, u32[]{:S(2)}) copy-start(s32[9216]{0:T(1024)S(1)} %broadcast_clamp_fusion) | copy-start | bytes 110596
  9.8 161.3 %copy-start.41 = (bf16[256,512]{1,0:T(8,128)(2,1)S(1)}, bf16[256,512]{1,0:T(8,128)(2,1)}, u32[]{:S(2)}) copy-start(bf16[256,512]{1,0:T(8,128)(2,1)} %param.44) | copy-start | bytes 786436
  172.8 19.2 %copy-start.4 = (f32[1024,512]{1,0:T(8,128)}, f32[1024,512]{1,0:T(8,128)S(1)}, u32[]{:S(2)}) copy-start(f32[1024,512]{1,0:T(8,128)S(1)} %fusion.221) | copy-start | bytes 6291460
  176.5 3.3 collective-permute-start
  178.5 4.1 collective-permute-start.1
  179.8 267.2 %copy-start.53 = (f32[32]{0:T(128)}, f32[32]{0:T(128)S(1)}, u32[]{:S(2)}) copy-start(f32[32]{0:T(128)S(1)} %multiply_convert_fusion.4) | copy-start | bytes 388
  197.4 7.1 collective-permute-start.2
  202.0 3.1 collective-permute-start.3
  204.3 187.3 %copy-start.32 = (pred[1024,9]{1,0:T(8,128)(4,1)}, pred[1024,9]{1,0:T(8,128)(4,1)S(1)}, u32[]{:S(2)}) copy-start(pred[1024,9]{1,0:T(8,128)(4,1)S(1)} %copy.182) | copy-start | bytes 27652
  204.5 187.0 %copy-start.34 = (pred[1024,9]{1,0:T(8,128)(4,1)}, pred[1024,9]{1,0:T(8,128)(4,1)S(1)}, u32[]{:S(2)}) copy-start(pred[1024,9]{1,0:T(8,128)(4,1)S(1)} %copy.183) | copy-start | bytes 27652
  295.7 9.1 copy-start.63
  308.4 6.4 collective-permute-start.4
  313.5 3.1 collective-permute-start.5
  322.7 11.7 copy-start.46
  328.0 7.3 collective-permute-start.6
  332.9 3.1 collective-permute-start.7
  403.7 21.9 %copy-start.5 = (f32[1024,512]{1,0:T(8,128)S(1)}, f32[1024,512]{1,0:T(8,128)}, u32[]{:S(2)}) copy-start(f32[1024,512]{1,0:T(8,128)} %copy-done.4) | copy-start | bytes 6291460
  403.7 21.9 %copy-start.80 = (f32[512]{0:T(512)S(1)}, f32[512]{0:T(512)}, u32[]{:S(2)}) copy-start(f32[512]{0:T(512)} %param.53) | copy-start | bytes 6148
  434.7 10.3 copy-start.47
  434.7 10.3 copy-start.49
  436.5 8.5 copy-start.77
  438.4 6.7 collective-permute-start.8
  443.7 3.1 collective-permute-start.9
  458.1 9.2 copy-start.70
  459.4 11.3 copy-start.81
  459.4 12.9 collective-permute-start.10
  465.7 6.6 collective-permute-start.11
  676.6 46.4 %copy-start.30 = (bf16[2,512,512]{2,1,0:T(8,128)(2,1)S(1)}, bf16[2,512,512]{2,1,0:T(8,128)(2,1)}, u32[]{:S(2)}) copy-start(bf16[2,512,512]{2,1,0:T(8,128)(2,1)} %get-tuple-element.161) | copy-start | bytes 3145732
  679.4 45.9 %collective-permute-start.12 = (bf16[1024,1024]{0,1:T(8,128)(2,1)S(1)}, bf16[1024,1024]{0,1:T(8,128)(2,1)S(1)}, u32[]{:S(2)}, u32[]{:S(2)}) collective-permute-start(bf16[1024,1024]{0,1:T(8,128)(2,1)S(1)} %get-tuple-element.251), channel_id=1, source_target_pairs={{0,4},{4,8},{8,12},{12,16},{16,20},{20,24},{24,28},{1,5},{5,9},{9,... | collective-permute-start | bytes 6291464 | tf_op jit(solution)/shard_map/ppermute | solution.py:34
  721.7 6.1 collective-permute-start.13
  723.7 7.5 copy-start.52
  734.5 46.9 %copy-start.54 = (f32[32]{0:T(128)S(1)}, f32[32]{0:T(128)}, u32[]{:S(2)}) copy-start(f32[32]{0:T(128)} %copy-done.53) | copy-start | bytes 388
  736.4 43.2 %collective-permute-start.14 = (f32[32,2,32]{0,2,1:T(8,128)S(1)}, f32[32,2,32]{0,2,1:T(8,128)S(1)}, u32[]{:S(2)}, u32[]{:S(2)}) collective-permute-start(f32[32,2,32]{0,2,1:T(8,128)S(1)} %pad_maximum_fusion.8), channel_id=1, source_target_pairs={{0,4},{4,8},{8,12},{12,16},{16,20},{20,24},{24,28},{1,5},{5,9},{9,... | collective-permute-start | bytes 24584 | tf_op jit(solution)/shard_map/ppermute | solution.py:23
  778.2 3.1 collective-permute-start.15
  799.0 17.0 %collective-permute-start.16 = (bf16[64,512]{1,0:T(8,128)(2,1)S(1)}, bf16[64,512]{1,0:T(8,128)(2,1)S(1)}, u32[]{:S(2)}, u32[]{:S(2)}) collective-permute-start(bf16[64,512]{1,0:T(8,128)(2,1)S(1)} %get-tuple-element.265), channel_id=1, source_target_pairs={{0,4},{4,8},{8,12},{12,16},{16,20},{20,24},{24,28},{1,5},{5,9},{9,... | collective-permute-start | bytes 196616 | tf_op jit(solution)/shard_map/ppermute | solution.py:23
  803.1 13.0 collective-permute-start.17
  854.4 17.6 %copy-start.33 = (pred[1024,9]{1,0:T(8,128)(4,1)S(1)}, pred[1024,9]{1,0:T(8,128)(4,1)}, u32[]{:S(2)}) copy-start(pred[1024,9]{1,0:T(8,128)(4,1)} %copy-done.32) | copy-start | bytes 27652
  854.4 17.6 %copy-start.35 = (pred[1024,9]{1,0:T(8,128)(4,1)S(1)}, pred[1024,9]{1,0:T(8,128)(4,1)}, u32[]{:S(2)}) copy-start(pred[1024,9]{1,0:T(8,128)(4,1)} %copy-done.34) | copy-start | bytes 27652
  872.1 8.0 copy-start.8
  872.1 8.0 copy-start.58
  872.1 8.0 copy-start.74
  907.3 4.3 collective-permute-start.18
  910.4 3.9 collective-permute-start.19
  927.0 17.3 %collective-permute-start.20 = (bf16[64,512]{1,0:T(8,128)(2,1)S(1)}, bf16[64,512]{1,0:T(8,128)(2,1)S(1)}, u32[]{:S(2)}, u32[]{:S(2)}) collective-permute-start(bf16[64,512]{1,0:T(8,128)(2,1)S(1)} %get-tuple-element.263), channel_id=1, source_target_pairs={{0,4},{4,8},{8,12},{12,16},{16,20},{20,24},{24,28},{1,5},{5,9},{9,... | collective-permute-start | bytes 196616 | tf_op jit(solution)/shard_map/ppermute | solution.py:23
  931.5 12.8 collective-permute-start.21
  999.6 8.0 copy-start.12
  999.6 8.0 copy-start.60
  999.6 8.0 copy-start.76
  1034.8 17.5 %collective-permute-start.22 = (f32[32,2,32]{0,2,1:T(8,128)S(1)}, f32[32,2,32]{0,2,1:T(8,128)S(1)}, u32[]{:S(2)}, u32[]{:S(2)}) collective-permute-start(f32[32,2,32]{0,2,1:T(8,128)S(1)} %pad_maximum_fusion.10), channel_id=1, source_target_pairs={{0,4},{4,8},{8,12},{12,16},{16,20},{20,24},{24,28},{1,5},{5,9},{9,... | collective-permute-start | bytes 24584 | tf_op jit(solution)/shard_map/ppermute | solution.py:23
  1037.9 14.5 collective-permute-start.23
  1067.2 137.7 %all-reduce.6.cloned.1.call-start = ((), (), s32[]{:S(2)}) async-start(), calls=%async_computation.2 | async-start | bytes 4194304 | tf_op jit(solution)/shard_map/psum | solution.py:341
  1067.3 7.5 slice-start
  1144.0 445.1 %all-reduce.8.cloned.1.call-start = ((), (), s32[]{:S(2)}) async-start(), calls=%async_computation.3 | async-start | bytes 47185920 | tf_op jit(solution)/shard_map/psum | solution.py:361
  1145.2 11.7 copy-start.29
  1145.2 11.7 copy-start.36
  1145.2 11.7 copy-start.45
  1145.2 11.7 copy-start.72
  1592.2 10.0 slice-start.3
  1593.0 9.2 slice-start.4
  1593.0 9.2 slice-start.5
  (59 other events, 164.1 us)
Sparse Core Ops, SparseCore 0:
  9.6 152.3 all-gather.3
  1067.3 47.6 all-gather.5
  1144.1 60.7 all-reduce.5
  1211.7 377.3 all-reduce.7
where the time goes:
time: 1630 us; the launch traced here: 1620 us
  waiting for transfers between devices  583 us (36%)
  local copies, waits for them, and re-layouts  470 us (29%)
  matrix products  188 us (12%)
  other arithmetic  148 us (9%)
  starting transfers between devices  143 us (9%)
  blocking collectives  52.6 us (3%)
    psum x1, waiting for transfers between devices, per_device(): lax.psum((g_w_in, g_b_in, g_gain_one, g_bias_one, g_conv1_w, g_conv1_b, g...  380 us
    gather x8, local copies, waits for them, and re-layouts, gather_taps(): picked = jnp.take(extended, tap_index, axis=0)  221 us
    all_gather x1, waiting for transfers between devices, per_device(): lax.all_gather(codebook, 'chan', axis=0, tiled=True)  152 us
    ppermute x11, starting transfers between devices, padded(): lax.ppermute(lax.slice_in_dim(block, block.shape[dim] - width, None, axis...  84.7 us
    dynamic_update_slice x2, local copies, waits for them, and re-layouts, block_backward(): lax.dynamic_update_slice_in_dim(grad_ext, current + jnp.concatenate([d_ke...  81.9 us
    select_n x2, local copies, waits for them, and re-layouts, gather_taps(): jnp.where(tap_valid[:, :, None], picked, jnp.zeros((), extended.dtype))  43.7 us
    ppermute x2, starting transfers between devices, from_behind(): return lax.ppermute(array, axis, pairs)  43.6 us
    select_n x4, other arithmetic, gather_taps(): jnp.where(tap_valid[:, :, None], picked, jnp.zeros((), extended.dtype))  40.1 us
  transfers between devices with their start and end apart: 28, of which 13 were waited for; matrix products, arithmetic and copies ran while one was open for 4% of the time, Pallas kernels for 0%

commit v1 on v0

v1 whole, which is shorter than its diff:
```python
import functools
import math

import jax
import jax.numpy as jnp
from jax import lax
from jax.experimental import pallas as pl
from jax.experimental.pallas import tpu as pltpu
from jax.sharding import PartitionSpec as P

GN_GROUPS = 32
GRID = 32
BLK = (GRID // 4) ** 2
HALO = 64
CHUNK = 256
STAT = 16
epsilon = 1e-06
masked_score = -1e30
f32 = jnp.float32
bf16 = jnp.bfloat16
MIB = 1 << 20
LATE_ROUND = 2
BOOK_ROUND = 4

VM = pl.BlockSpec(memory_space=pltpu.VMEM)
SM = pl.BlockSpec(memory_space=pltpu.SMEM)
HB = pl.BlockSpec(memory_space=pl.ANY)


def call(body, ins, outs, scratch, operands, flops, vmem=58, aliases={}, light=False):
    bytes_all = sum(math.prod(a.shape) * a.dtype.itemsize for a in (*operands, *[o[0] for o in outs]))
    if light:
        flops = bytes_all = 0
    return pl.pallas_call(
        body,
        out_shape=[o[0] for o in outs],
        in_specs=ins,
        out_specs=[o[1] for o in outs],
        scratch_shapes=scratch,
        input_output_aliases=aliases,
        compiler_params=pltpu.CompilerParams(vmem_limit_bytes=vmem * MIB),
        cost_estimate=pl.CostEstimate(flops=flops, bytes_accessed=bytes_all, transcendentals=0),
    )(*operands)


def sds(shape, dtype):
    return jax.ShapeDtypeStruct(shape, dtype)


def dot_nn(a, b):
    return lax.dot_general(a, b, (((1,), (0,)), ((), ())), preferred_element_type=f32)


def dot_nt(a, b):
    return lax.dot_general(a, b, (((1,), (1,)), ((), ())), preferred_element_type=f32)


def dot_tn(a, b):
    return lax.dot_general(a, b, (((0,), (0,)), ((), ())), preferred_element_type=f32)


def group_total(x):
    per = x.shape[1] // GN_GROUPS
    lane = lax.broadcasted_iota(jnp.int32, x.shape, 1)
    step = 1
    while step < per:
        up = pltpu.roll(x, step, 1)
        down = pltpu.roll(x, x.shape[1] - step, 1)
        x = x + jnp.where((lane & step) != 0, up, down)
        step *= 2
    return x


def image_total(e_ref, row, nb, amat):
    total = amat[:, 0:1] * e_ref[row : row + 1, :]
    for j in range(1, nb):
        total = total + amat[:, j : j + 1] * e_ref[row + j : row + j + 1, :]
    return total


def split3(v):
    high = v.astype(bf16)
    rest = v - high.astype(f32)
    mid = rest.astype(bf16)
    low = (rest - mid.astype(f32)).astype(bf16)
    return high, mid, low


def pack_stats(a, b):
    rows = [p.astype(f32) for p in (*split3(a), *split3(b))]
    rows.append(jnp.zeros((STAT - 6, a.shape[1]), f32))
    return jnp.concatenate(rows, axis=0).astype(bf16)


def unpack_stats(block):
    v = block.astype(f32)
    return v[0:1] + v[1:2] + v[2:3], v[3:4] + v[4:5] + v[5:6]


def stat_rows(a, b):
    return jnp.concatenate([a, b, jnp.zeros((6, a.shape[1]), f32)], axis=0)


def totals(t_ref, nb, amat, prev_rows, next_rows):
    first, last = amat[:, nb : nb + 1], amat[:, nb + 1 : nb + 2]
    one = t_ref[0:nb, :] + first * prev_rows[0] + last * next_rows[0]
    two = t_ref[nb : 2 * nb, :] + first * prev_rows[1] + last * next_rows[1]
    inv_count = amat[:, nb + 2 : nb + 3]
    return one * inv_count, two * inv_count


def norm_stats(t_ref, nb, amat, prev_rows, next_rows, stat_ref):
    mean, square = totals(t_ref, nb, amat, prev_rows, next_rows)
    stat_ref[0:nb, :] = mean
    stat_ref[nb : 2 * nb, :] = lax.rsqrt(square - mean * mean + epsilon)


def block_stats(stat_ref, nb, k):
    return stat_ref[k : k + 1, :], stat_ref[nb + k : nb + k + 1, :]


def own_totals(e_ref, nb, amat, t_ref):
    t_ref[0:nb, :] = group_total(image_total(e_ref, 0, nb, amat))
    t_ref[nb : 2 * nb, :] = group_total(image_total(e_ref, nb, nb, amat))


def set_sums(e_ref, nb, k, x, y):
    e_ref[k : k + 1, :] = jnp.sum(x, axis=0, keepdims=True)
    e_ref[nb + k : nb + k + 1, :] = jnp.sum(y, axis=0, keepdims=True)


def silu(pre):
    return pre * jax.nn.sigmoid(pre)


def silu_slope(pre):
    s = jax.nn.sigmoid(pre)
    return s * (1.0 + pre * (1.0 - s))


def shift_columns(mid_ref, left_ref, right_ref, rows):
    left_ref[8 : 8 + rows, :] = mid_ref[7 : 7 + rows, :]
    right_ref[8 : 8 + rows, :] = mid_ref[9 : 9 + rows, :]


def make_patch(refs, patch_ref, mask_ref, ints_ref, k, chans):
    side = ints_ref[0, k]
    for dr in (-1, 0, 1):
        at = 8 + HALO + k * BLK
        if dr != 0:
            at = pl.multiple_of(at + dr * side, 8)
        for dc in (-1, 0, 1):
            tap = (dr + 1) * 3 + dc + 1
            rows = refs[dc + 1][pl.ds(at, BLK), :]
            if tap != 4:
                rows = rows * mask_ref[k * BLK : (k + 1) * BLK, tap : tap + 1]
            patch_ref[k * BLK : (k + 1) * BLK, tap * chans : (tap + 1) * chans] = rows.astype(bf16)


def lookup_kernel(tokens, *refs):
    index_ref, book_ref, out_ref = refs[tokens:]
    codes = book_ref.shape[0]
    total = jnp.zeros(out_ref.shape, f32)
    for c in range(0, codes, 512):
        lane = lax.broadcasted_iota(jnp.int32, (index_ref.shape[0], 512), 1) + c
        hot = jnp.where(index_ref[...] == lane, 1.0, 0.0).astype(bf16)
        total = total + dot_nn(hot, book_ref[c : c + 512, :])
    out_ref[...] = total.astype(bf16)


def lookup(index, book, tokens=()):
    pixels, emb = index.shape[0], book.shape[1]
    step = 256
    return pl.pallas_call(
        functools.partial(lookup_kernel, len(tokens)),
        grid=(pixels // step,),
        out_shape=sds((pixels, emb), bf16),
        in_specs=[HB] * len(tokens) + [pl.BlockSpec((step, 1), lambda i: (i, 0)), pl.BlockSpec(book.shape, lambda i: (0, 0))],
        out_specs=pl.BlockSpec((step, emb), lambda i: (i, 0)),
        compiler_params=pltpu.CompilerParams(vmem_limit_bytes=40 * MIB),
        cost_estimate=pl.CostEstimate(
            flops=2 * pixels * book.shape[0] * emb, bytes_accessed=book.size * 2, transcendentals=0
        ),
    )(*tokens, index, book)


def scatter_kernel(step, tokens, parts, *refs):
    index_refs, grad_refs = refs[tokens : tokens + parts], refs[tokens + parts : tokens + 3 * parts]
    begun_ref, out_ref = refs[-2:]
    half, emb = step * pl.num_programs(0), grad_refs[0].shape[1]
    for side in range(2):
        lanes = slice(side * emb, (side + 1) * emb)
        code = lax.broadcasted_iota(jnp.int32, (step, 512), 0) + (pl.program_id(0) * step + side * half)
        total = begun_ref[:, lanes]
        for index_ref, one_ref, two_ref in zip(index_refs, grad_refs[::2], grad_refs[1::2]):
            for p in range(0, one_ref.shape[0], 512):
                hot = jnp.where(index_ref[0:1, p : p + 512] == code, 1.0, 0.0).astype(bf16)
                grad = one_ref[p : p + 512, :].astype(f32) + two_ref[p : p + 512, :].astype(f32)
                total = total + dot_nn(hot, grad.astype(bf16))
        out_ref[:, lanes] = total.astype(out_ref.dtype)


def scatter(indices, pairs, codes, dtype, begun, tokens):
    grads = [x for pair in pairs for x in pair]
    emb, step, parts = grads[0].shape[1], 256, len(pairs)
    whole = [pl.BlockSpec(a.shape, lambda i: (0, 0)) for a in (*indices, *grads)]
    tile = pl.BlockSpec((step, 2 * emb), lambda i: (i, 0))
    return pl.pallas_call(
        functools.partial(scatter_kernel, step, len(tokens), parts),
        grid=(codes // 2 // step,),
        out_shape=sds((codes // 2, 2 * emb), dtype),
        in_specs=[HB for _ in tokens] + whole + [tile],
        out_specs=tile,
        compiler_params=pltpu.CompilerParams(vmem_limit_bytes=40 * MIB),
        cost_estimate=pl.CostEstimate(
            flops=2 * parts * grads[0].shape[0] * codes * emb, bytes_accessed=codes * emb * 8, transcendentals=0
        ),
    )(*tokens, *indices, *grads, begun)


def own_kernel(step, pass_ref, token_ref, index_ref, grad_ref, quant_ref, err_ref, in_ref, one_ref, two_ref, three_ref,
               query_ref, value_ref, proj_ref, passed_ref, out_ref, small_ref):
    emb = grad_ref.shape[1]
    half = out_ref.shape[0]
    for r in range(0, half, step):
        for side in range(2):
            code = lax.broadcasted_iota(jnp.int32, (step, 512), 0) + (r + side * half)
            total = jnp.zeros((step, emb), f32)
            for p in range(0, grad_ref.shape[0], 512):
                hot = jnp.where(index_ref[0:1, p : p + 512] == code, 1.0, 0.0).astype(bf16)
                total = total + dot_nn(hot, grad_ref[p : p + 512, :])
            out_ref[r : r + step, side * emb : (side + 1) * emb] = total
    small_ref[0:emb, :] = dot_tn(quant_ref[...], err_ref[...]).astype(bf16)
    rows = [in_ref[0:1, :], one_ref[0:3, :], two_ref[0:3, :], three_ref[0:2, :], query_ref[...], value_ref[...], proj_ref[...]]
    filler = jnp.zeros((small_ref.shape[0] - emb - 12, small_ref.shape[1]), f32)
    small_ref[emb:, :] = jnp.concatenate([*rows, filler], axis=0).astype(bf16)


def own_part(passed, token, index, grad, quant, err, vectors, codes):
    emb, chans = grad.shape[1], err.shape[1]
    outs = [(sds(passed.shape, bf16), HB), (sds((codes // 2, 2 * emb), f32), VM), (sds((chans, chans), bf16), VM)]
    operands = (passed, token, index, grad, quant, err, *vectors)
    flops = 2 * grad.shape[0] * emb * (codes + chans)
    return call(functools.partial(own_kernel, 256), [HB] * 2 + [VM] * (len(operands) - 2), outs, [], operands, flops, aliases={0: 0})


def lift_kernel(n_codes, nb, *refs):
    feat_ref, code_refs = refs[0], refs[1 : 1 + n_codes]
    w_ref, b_ref, amat_ref, quant_ref, resid_ref, t_ref, msgp_ref, msgn_ref, e_ref = refs[1 + n_codes :]
    pixels = feat_ref.shape[0]
    for c in range(0, pixels, CHUNK):
        at = slice(c, c + CHUNK)
        code = code_refs[0][at, :].astype(f32)
        for other in code_refs[1:]:
            code = code + other[at, :].astype(f32)
        quant = (feat_ref[at, :].astype(f32) + code).astype(bf16)
        quant_ref[at, :] = quant
        resid_ref[at, :] = dot_nn(quant, w_ref[...]) + b_ref[...]
    for k in range(nb):
        x = resid_ref[k * BLK : (k + 1) * BLK, :]
        set_sums(e_ref, nb, k, x, x * x)
    own_totals(e_ref, nb, amat_ref[...], t_ref)
    send_rows(resid_ref, t_ref, nb, msgp_ref, msgn_ref)


def send_rows(x_ref, t_ref, nb, msgp_ref, msgn_ref):
    pixels = x_ref.shape[0]
    msgp_ref[0:HALO, :] = x_ref[0:HALO, :]
    msgn_ref[0:HALO, :] = x_ref[pixels - HALO : pixels, :]
    send_stats(t_ref, nb, msgp_ref, msgn_ref, HALO)


def send_stats(t_ref, nb, msgp_ref, msgn_ref, at):
    msgp_ref[at : at + 8, :] = stat_rows(t_ref[0:1, :], t_ref[nb : nb + 1, :])
    msgn_ref[at : at + 8, :] = stat_rows(t_ref[nb - 1 : nb, :], t_ref[2 * nb - 1 : 2 * nb, :])


def get_stats(ref, at):
    return ref[at : at + 1, :], ref[at + 1 : at + 2, :]


def conv_forward_kernel(nb, last, *refs):
    x_ref, rp_ref, rn_ref, t_ref, amat_ref, gain_ref, bias_ref, mask_ref, ints_ref, w_hbm, cb_ref = refs[:11]
    refs = refs[11:]
    if last:
        resid_ref, cot_ref = refs[:2]
        refs = refs[2:]
    out_ref, stat_ref, to_ref, msgp_ref, msgn_ref, patch_hbm = refs[:6]
    mid_ref, left_ref, right_ref, patch_ref, w_ref, e_ref, w_sem, p_sem = refs[6:]
    pixels, chans = x_ref.shape
    load = pltpu.make_async_copy(w_hbm, w_ref, w_sem)
    load.start()
    amat = amat_ref[...]
    norm_stats(t_ref, nb, amat, get_stats(rp_ref, HALO), get_stats(rn_ref, HALO), stat_ref)
    gain, bias = gain_ref[...], bias_ref[...]

    def act(x, k):
        mean, inv = block_stats(stat_ref, nb, k)
        return silu((x - mean) * (inv * gain) + bias).astype(bf16).astype(f32)

    mid_ref[8 : 8 + HALO, :] = act(rp_ref[0:HALO, :], 0)
    mid_ref[8 + HALO + pixels : 8 + 2 * HALO + pixels, :] = act(rn_ref[0:HALO, :], nb - 1)
    for k in range(nb):
        mid_ref[8 + HALO + k * BLK : 8 + HALO + (k + 1) * BLK, :] = act(x_ref[k * BLK : (k + 1) * BLK, :], k)
    shift_columns(mid_ref, left_ref, right_ref, pixels + 2 * HALO)
    saves = []
    for c in range(0, pixels, CHUNK):
        for k in range(c // BLK, (c + CHUNK) // BLK):
            make_patch((left_ref, mid_ref, right_ref), patch_ref, mask_ref, ints_ref, k, chans)
        save = pltpu.make_async_copy(
            patch_ref.at[pl.ds(c, CHUNK), :], patch_hbm.at[pl.ds(c, CHUNK), :], p_sem.at[c // CHUNK]
        )
        save.start()
        saves.append(save)
        if c == 0:
            load.wait()
        out = dot_nn(patch_ref[c : c + CHUNK, :], w_ref[...]) + cb_ref[...]
        if last:
            out = out + resid_ref[c : c + CHUNK, :]
        out_ref[c : c + CHUNK, :] = out
        for k in range(c // BLK, (c + CHUNK) // BLK):
            x = out_ref[k * BLK : (k + 1) * BLK, :]
            set_sums(e_ref, nb, k, x, x * x)
    own_totals(e_ref, nb, amat, to_ref)
    if last:
        msgp_ref[0:pixels, :] = out_ref[...].astype(bf16)
        msgn_ref[0:pixels, :] = out_ref[...].astype(bf16)
        msgp_ref[pixels : pixels + HALO, :] = cot_ref[0:HALO, :]
        msgn_ref[pixels : pixels + HALO, :] = cot_ref[pixels - HALO : pixels, :]
        at = pixels + HALO
        msgp_ref[at : at + STAT, :] = pack_stats(to_ref[0:1, :], to_ref[nb : nb + 1, :])
        msgn_ref[at : at + STAT, :] = pack_stats(to_ref[nb - 1 : nb, :], to_ref[2 * nb - 1 : 2 * nb, :])
    else:
        send_rows(out_ref, to_ref, nb, msgp_ref, msgn_ref)
    for save in saves:
        save.wait()


def conv_scratch(pixels, chans, nb, w_shape):
    rows = pixels + 2 * HALO + 16
    return [
        pltpu.VMEM((rows, chans), f32),
        pltpu.VMEM((rows, chans), f32),
        pltpu.VMEM((rows, chans), f32),
        pltpu.VMEM((pixels, 9 * chans), bf16),
        pltpu.VMEM(w_shape, bf16),
        pltpu.VMEM((2 * nb, chans), f32),
    ]


def conv_forward(x, recv_p, recv_n, t, amat, gain, bias, mask, ints, weight, cb, resid=None, cot=None):
    pixels, chans = x.shape
    nb = pixels // BLK
    last = resid is not None
    msg = sds((pixels + HALO + STAT, chans), bf16) if last else sds((HALO + 8, chans), f32)
    operands = [x, recv_p, recv_n, t, amat, gain, bias, mask, ints, weight.reshape(9 * chans, chans), cb]
    ins = [VM, VM, VM, VM, VM, VM, VM, VM, SM, HB, VM]
    if last:
        operands += [resid, cot]
        ins += [VM, VM]
    stats = sds((2 * nb, chans), f32)
    outs = [(sds((pixels, chans), f32), VM), (stats, VM), (stats, VM), (msg, VM), (msg, VM)]
    outs.append((sds((pixels, 9 * chans), bf16), HB))
    scratch = conv_scratch(pixels, chans, nb, (9 * chans, chans))
    scratch += [pltpu.SemaphoreType.DMA, pltpu.SemaphoreType.DMA((pixels // CHUNK,))]
    flops = 18 * pixels * chans * chans
    return call(functools.partial(conv_forward_kernel, nb, last), ins, outs, scratch, operands, flops)


def attention_kernel(nb, *refs):
    (
        x_ref, rp_ref, rn_ref, t_ref, amat_ref, gain_ref, bias_ref, ints_ref, img_ref,
        wq_ref, wk_ref, wv_ref, wp_ref, bq_ref, bv_ref, bp_ref, cot_ref,
    ) = refs[:17]
    (
        norm_hbm, dk_hbm, dv_hbm, out_ref, attn_ref, dq_ref, u_ref, stat_ref, to_ref, vec_ref, msgp_ref, msgn_ref,
    ) = refs[17:29]
    norm_ref, dk_ref, dv_ref, q_ref, k_ref, v_ref, da_ref, at_ref, dqf_ref, dkf_ref, dvf_ref, e_ref, h_ref, sems = refs[29:]
    pixels, chans = x_ref.shape
    own = pixels // CHUNK
    scale = 1.0 / math.sqrt(chans)
    amat = amat_ref[...]
    at = pixels + HALO
    prev_stats = unpack_stats(rp_ref[at : at + STAT, :])
    next_stats = unpack_stats(rn_ref[at : at + STAT, :])
    norm_stats(t_ref, nb, amat, prev_stats, next_stats, stat_ref)
    gain, bias = gain_ref[...], bias_ref[...]
    chunk_lo = ints_ref[1, 0] // CHUNK
    chunk_hi = (ints_ref[2, nb - 1] + CHUNK - 1) // CHUNK
    copies = []

    def send(scratch, hbm, which, c):
        r = pl.ds(c * CHUNK, CHUNK)
        copy = pltpu.make_async_copy(scratch.at[r, :], hbm.at[r, :], sems.at[which, c])
        copy.start()
        copies.append(copy)

    def xhat(c, b):
        r = (c % own) * CHUNK + b * BLK
        if c < own:
            x, k = rp_ref[r : r + BLK, :].astype(f32), 0
        elif c < 2 * own:
            x, k = x_ref[r : r + BLK, :], r // BLK
        else:
            x, k = rn_ref[r : r + BLK, :].astype(f32), nb - 1
        mean, inv = block_stats(stat_ref, nb, k)
        return (x - mean) * inv

    def reached(c, work, otherwise):
        if own <= c < 2 * own:
            work()
        else:
            inside = (c >= chunk_lo) & (c < chunk_hi)
            pl.when(inside)(work)
            pl.when(jnp.logical_not(inside))(otherwise)

    for c in range(3 * own):
        r = slice(c * CHUNK, (c + 1) * CHUNK)

        def keys(c=c, r=r):
            for b in range(CHUNK // BLK):
                norm_ref[c * CHUNK + b * BLK : c * CHUNK + (b + 1) * BLK, :] = (xhat(c, b) * gain + bias).astype(bf16)
            normed = norm_ref[r, :]
            k_ref[r, :] = dot_nn(normed, wk_ref[...]).astype(bf16)
            v_ref[r, :] = (dot_nn(normed, wv_ref[...]) + bv_ref[...]).astype(bf16)
            dkf_ref[r, :] = jnp.zeros((CHUNK, chans), f32)
            dvf_ref[r, :] = jnp.zeros((CHUNK, chans), f32)
            if own <= c < 2 * own:
                o = slice((c - own) * CHUNK, (c - own + 1) * CHUNK)
                q_ref[o, :] = (dot_nn(normed, wq_ref[...]) + bq_ref[...]).astype(bf16)
                da_ref[o, :] = dot_nt(cot_ref[o, :], wp_ref[...]).astype(bf16)

        def nothing(r=r):
            norm_ref[r, :] = jnp.zeros((CHUNK, chans), bf16)

        reached(c, keys, nothing)
        send(norm_ref, norm_hbm, 0, c)
    q_ref[pixels : pixels + CHUNK, :] = jnp.zeros((CHUNK, chans), bf16)
    da_ref[pixels : pixels + CHUNK, :] = jnp.zeros((CHUNK, chans), bf16)

    def attend(count, key_at, row_at, row_end):
        rows = pl.ds(pl.multiple_of(row_at, BLK), CHUNK)
        cols = pl.ds(pl.multiple_of(key_at, BLK), count)
        s = dot_nt(q_ref[rows, :], k_ref[cols, :]) * scale
        p = jnp.exp(s - jnp.max(s, axis=1, keepdims=True))
        at_row = lax.broadcasted_iota(jnp.int32, (CHUNK, 1), 0) + row_at
        p = p * jnp.where(at_row < row_end, 1.0 / jnp.sum(p, axis=1, keepdims=True), 0.0)
        low = p.astype(bf16)
        d_attn = da_ref[rows, :]
        dp = dot_nt(d_attn, v_ref[cols, :])
        at_ref[rows, :] = dot_nn(low, v_ref[cols, :]).astype(bf16)
        dvf_ref[cols, :] += dot_tn(low, d_attn)
        ds = (p * (dp - jnp.sum(p * dp, axis=1, keepdims=True))).astype(bf16)
        dqf_ref[rows, :] = (dot_nn(ds, k_ref[cols, :]) * scale).astype(bf16)
        dkf_ref[cols, :] += dot_tn(ds, q_ref[rows, :])

    def image(m, carry):
        key_at, side, begin, end = (img_ref[t, m] for t in range(4))
        for kind in (GRID // 2, 3 * GRID // 4, GRID):

            @pl.when(side == kind)
            def _():
                def block(i, inner):
                    attend(kind * kind, key_at, begin + i * CHUNK, end)
                    return inner

                lax.fori_loop(0, (end - begin + CHUNK - 1) // CHUNK, block, 0)

        return carry

    lax.fori_loop(0, img_ref[4, 0], image, 0)
    h_ref[...] = jnp.zeros(h_ref.shape, f32)
    for c in range(3 * own):
        r = slice(c * CHUNK, (c + 1) * CHUNK)
        o = slice((c % own) * CHUNK, (c % own + 1) * CHUNK)

        def fold(c=c, r=r, o=o):
            d_key = (dkf_ref[r, :] * scale).astype(bf16)
            d_value = dvf_ref[r, :].astype(bf16)
            dk_ref[r, :] = d_key
            dv_ref[r, :] = d_value
            u = dot_nt(d_key, wk_ref[...]) + dot_nt(d_value, wv_ref[...])
            if own <= c < 2 * own:
                d_query = dqf_ref[o, :]
                dq_ref[o, :] = d_query
                attn = at_ref[o, :]
                attn_ref[o, :] = attn
                out_ref[o, :] = (x_ref[o, :] + dot_nn(attn, wp_ref[...]) + bp_ref[...]).astype(bf16)
                u_ref[o, :] = u + dot_nt(d_query, wq_ref[...])
                for b in range(CHUNK // BLK):
                    k = (c - own) * (CHUNK // BLK) + b
                    u = u_ref[k * BLK : (k + 1) * BLK, :]
                    set_sums(e_ref, nb, k, u, u * xhat(c, b))
            else:
                msg_ref, row = (msgp_ref, 0) if c < own else (msgn_ref, 2)
                msg_ref[o, :] = u.astype(bf16)
                for b in range(CHUNK // BLK):
                    part = u[b * BLK : (b + 1) * BLK, :]
                    h_ref[row : row + 1, :] += jnp.sum(part, axis=0, keepdims=True)
                    h_ref[row + 1 : row + 2, :] += jnp.sum(part * xhat(c, b), axis=0, keepdims=True)

        def nothing(c=c, r=r, o=o):
            zero = jnp.zeros((CHUNK, chans), bf16)
            dk_ref[r, :] = zero
            dv_ref[r, :] = zero
            (msgp_ref if c < own else msgn_ref)[o, :] = zero

        reached(c, fold, nothing)
        send(dk_ref, dk_hbm, 1, c)
        send(dv_ref, dv_hbm, 2, c)
    before, before_x, after, after_x = (h_ref[i : i + 1, :] for i in range(4))
    d_bias = jnp.sum(e_ref[0:nb, :], axis=0, keepdims=True) + before + after
    d_gain = jnp.sum(e_ref[nb : 2 * nb, :], axis=0, keepdims=True) + before_x + after_x
    vec_ref[...] = stat_rows(d_gain, d_bias)
    e_ref[0:1, :] += before
    e_ref[nb : nb + 1, :] += before_x
    e_ref[nb - 1 : nb, :] += after
    e_ref[2 * nb - 1 : 2 * nb, :] += after_x
    e_ref[...] = e_ref[...] * gain
    own_totals(e_ref, nb, amat, to_ref)
    msgp_ref[pixels : pixels + HALO, :] = u_ref[0:HALO, :].astype(bf16)
    msgn_ref[pixels : pixels + HALO, :] = u_ref[pixels - HALO : pixels, :].astype(bf16)
    msgp_ref[at : at + STAT, :] = pack_stats(to_ref[0:1, :], to_ref[nb : nb + 1, :])
    msgn_ref[at : at + STAT, :] = pack_stats(to_ref[nb - 1 : nb, :], to_ref[2 * nb - 1 : 2 * nb, :])
    for copy in copies:
        copy.wait()


def attention(x, recv_p, recv_n, t, amat, gain, bias, ints, images, wq, wk, wv, wp, bq, bv, bp, cot):
    pixels, chans = x.shape
    nb, ext = pixels // BLK, 3 * pixels
    rows16, rows32 = sds((pixels, chans), bf16), sds((pixels, chans), f32)
    ext16 = sds((ext, chans), bf16)
    stats = sds((2 * nb, chans), f32)
    msg = sds((pixels + HALO + STAT, chans), bf16)
    outs = [(ext16, HB)] * 3
    outs += [(o, VM) for o in (rows16, rows16, rows16, rows32, stats, stats, sds((8, chans), f32), msg, msg)]
    padded = pltpu.VMEM((pixels + CHUNK, chans), bf16)
    window = pltpu.VMEM((ext, chans), bf16)
    wide = pltpu.VMEM((ext, chans), f32)
    scratch = [window, window, window, padded, window, window, padded, padded, padded, wide, wide]
    scratch += [pltpu.VMEM((2 * nb, chans), f32), pltpu.VMEM((8, chans), f32)]
    scratch.append(pltpu.SemaphoreType.DMA((3, ext // CHUNK)))
    ins = [VM] * 7 + [SM, SM] + [VM] * 8
    operands = (x, recv_p, recv_n, t, amat, gain, bias, ints, images, wq, wk, wv, wp, bq, bv, bp, cot)
    flops = 2 * pixels * chans * (chans * 9 + 6 * 1280)
    return call(functools.partial(attention_kernel, nb), ins, outs, scratch, operands, flops)


def conv_backward_kernel(nb, first, *refs):
    refs = refs[1:]
    if first:
        u_ref, mine_p_ref, mine_n_ref, rp_ref, rn_ref, xp_ref, xn_ref, cot_ref = refs[:8]
        refs = refs[8:]
    else:
        u_ref, rp_ref, rn_ref, xp_ref, xn_ref = refs[:5]
        refs = refs[5:]
    x_ref, stat_ref, s_ref, gain_ref, amat_ref, mask_ref, ints_ref, w_hbm = refs[:8]
    y_ref, ystat_ref, ygain_ref, ybias_ref = refs[8:12]
    refs = refs[12:]
    refs = refs[1:]
    if first:
        mid_out_ref, refs = refs[0], refs[1:]
    err_ref, v_ref, so_ref, vec_ref, msgp_ref, msgn_ref = refs[:6]
    mid_ref, left_ref, right_ref, patch_ref, w_ref, e_ref, w_sem = refs[6:]
    pixels, chans = x_ref.shape
    loads = []
    for tap in range(9):
        load = pltpu.make_async_copy(
            w_hbm.at[8 - tap], w_ref.at[:, pl.ds(tap * chans, chans)], w_sem.at[tap]
        )
        load.start()
        loads.append(load)
    amat = amat_ref[...]
    if first:
        at = pixels + HALO
        prev_stats = unpack_stats(rp_ref[at : at + STAT, :])
        next_stats = unpack_stats(rn_ref[at : at + STAT, :])
    else:
        prev_stats, next_stats = get_stats(rp_ref, HALO), get_stats(rn_ref, HALO)
    one, two = totals(s_ref, nb, amat, prev_stats, next_stats)
    e_ref[0:nb, :] = one
    e_ref[nb : 2 * nb, :] = two
    gain = gain_ref[...]

    def grad(u, x, k):
        mean, inv = block_stats(stat_ref, nb, k)
        m_one, m_two = block_stats(e_ref, nb, k)
        return inv * (u * gain - m_one - (x - mean) * inv * m_two)

    if first:
        low, high = slice(pixels - HALO, pixels), slice(0, HALO)
        side = slice(pixels, pixels + HALO)
        u = mine_p_ref[low, :].astype(f32) + rp_ref[side, :].astype(f32)
        before = xp_ref[side, :].astype(f32) + grad(u, xp_ref[low, :].astype(f32), 0)
        u = mine_n_ref[high, :].astype(f32) + rn_ref[side, :].astype(f32)
        after = xn_ref[side, :].astype(f32) + grad(u, xn_ref[high, :].astype(f32), nb - 1)
    else:
        before = grad(rp_ref[0:HALO, :], xp_ref[0:HALO, :], 0)
        after = grad(rn_ref[0:HALO, :], xn_ref[0:HALO, :], nb - 1)
    mid_ref[8 : 8 + HALO, :] = before.astype(bf16).astype(f32)
    mid_ref[8 + HALO + pixels : 8 + 2 * HALO + pixels, :] = after.astype(bf16).astype(f32)
    column = jnp.zeros((1, chans), f32)
    for k in range(nb):
        r = slice(k * BLK, (k + 1) * BLK)
        u = u_ref[r, :]
        if first:
            u = u + rp_ref[r, :].astype(f32) + rn_ref[r, :].astype(f32)
        g = grad(u, x_ref[r, :], k)
        if first:
            g = g + cot_ref[r, :].astype(f32)
            mid_out_ref[r, :] = g
        low = g.astype(bf16)
        err_ref[r, :] = low
        g = low.astype(f32)
        column = column + jnp.sum(g, axis=0, keepdims=True)
        mid_ref[8 + HALO + k * BLK : 8 + HALO + (k + 1) * BLK, :] = g
    shift_columns(mid_ref, left_ref, right_ref, pixels + 2 * HALO)
    y_gain, y_bias = ygain_ref[...], ybias_ref[...]
    for c in range(0, pixels, CHUNK):
        for k in range(c // BLK, (c + CHUNK) // BLK):
            make_patch((left_ref, mid_ref, right_ref), patch_ref, mask_ref, ints_ref, k, chans)
        if c == 0:
            for load in loads:
                load.wait()
        v_ref[c : c + CHUNK, :] = dot_nt(patch_ref[c : c + CHUNK, :], w_ref[...])
        for k in range(c // BLK, (c + CHUNK) // BLK):
            r = slice(k * BLK, (k + 1) * BLK)
            mean, inv = block_stats(ystat_ref, nb, k)
            xh = (y_ref[r, :] - mean) * inv
            v = v_ref[r, :] * silu_slope(xh * y_gain + y_bias)
            v_ref[r, :] = v
            set_sums(e_ref, nb, k, v, v * xh)
    d_bias = jnp.sum(e_ref[0:nb, :], axis=0, keepdims=True)
    d_gain = jnp.sum(e_ref[nb : 2 * nb, :], axis=0, keepdims=True)
    vec_ref[...] = jnp.concatenate([d_gain, d_bias, column, jnp.zeros((5, chans), f32)], axis=0)
    e_ref[...] = e_ref[...] * y_gain
    own_totals(e_ref, nb, amat, so_ref)
    if first:
        send_rows(v_ref, so_ref, nb, msgp_ref, msgn_ref)
    else:
        send_stats(so_ref, nb, msgp_ref, msgn_ref, 0)


def conv_backward(first, token, heads, x, stat, s, gain, amat, mask, ints, weight, y, ystat, ygain, ybias):
    pixels, chans = x.shape
    nb = pixels // BLK
    operands = [token, *heads, x, stat, s, gain, amat, mask, ints, weight.reshape(9, chans, chans), y, ystat, ygain, ybias]
    ins = [HB] + [VM] * len(heads) + [VM] * 6 + [SM, HB] + [VM] * 4
    msg = sds((HALO + 8 if first else 8, chans), f32)
    rows = sds((pixels, chans), f32)
    outs = [sds(token.shape, token.dtype)] + ([rows] if first else [])
    outs += [sds((pixels, chans), bf16), rows, sds((2 * nb, chans), f32), sds((8, chans), f32), msg, msg]
    scratch = conv_scratch(pixels, chans, nb, (chans, 9 * chans)) + [pltpu.SemaphoreType.DMA((9,))]
    flops = 18 * pixels * chans * chans
    return call(
        functools.partial(conv_backward_kernel, nb, first), ins, [(outs[0], HB)] + [(o, VM) for o in outs[1:]], scratch,
        operands, flops, aliases={0: 0},
    )


def tail_kernel(nb, passes, *refs):
    v_ref, rp_ref, rn_ref, s_ref, x_ref, stat_ref, gain_ref, amat_ref, mid_ref, w_ref = refs[passes : passes + 10]
    err_ref, fg_ref, vec_ref, e_ref = refs[2 * passes + 10 :]
    pixels, chans = x_ref.shape
    one, two = totals(s_ref, nb, amat_ref[...], get_stats(rp_ref, 0), get_stats(rn_ref, 0))
    e_ref[0:nb, :] = one
    e_ref[nb : 2 * nb, :] = two
    gain = gain_ref[...]
    column = jnp.zeros((1, chans), f32)
    for c in range(0, pixels, CHUNK):
        for k in range(c // BLK, (c + CHUNK) // BLK):
            r = slice(k * BLK, (k + 1) * BLK)
            mean, inv = block_stats(stat_ref, nb, k)
            m_one, m_two = block_stats(e_ref, nb, k)
            g = mid_ref[r, :] + inv * (v_ref[r, :] * gain - m_one - (x_ref[r, :] - mean) * inv * m_two)
            low = g.astype(bf16)
            err_ref[r, :] = low
            column = column + jnp.sum(low.astype(f32), axis=0, keepdims=True)
        fg_ref[c : c + CHUNK, :] = dot_nt(err_ref[c : c + CHUNK, :], w_ref[...]).astype(bf16)
    vec_ref[...] = jnp.concatenate([column, jnp.zeros((7, chans), f32)], axis=0)


def tail(passed, v, recv_p, recv_n, s, x, stat, gain, amat, mid, w_in):
    pixels, chans = x.shape
    nb = pixels // BLK
    count = len(passed)
    outs = [(sds(a.shape, a.dtype), HB) for a in passed]
    outs += [(sds((pixels, chans), bf16), VM), (sds((pixels, w_in.shape[0]), bf16), VM), (sds((8, chans), f32), VM)]
    operands = (*passed, v, recv_p, recv_n, s, x, stat, gain, amat, mid, w_in)
    scratch = [pltpu.VMEM((2 * nb, chans), f32)]
    flops = 2 * pixels * chans * w_in.shape[0]
    body = functools.partial(tail_kernel, nb, count)
    aliases = {i: i for i in range(count)}
    return call(body, [HB] * count + [VM] * 10, outs, scratch, operands, flops, aliases=aliases)


def finish_kernel(places, tokens, *refs):
    up_ref, mine_hbm, other_hbm, *out_refs, read_ref, stage_ref, read_sems, sems = refs[tokens:]
    slots = stage_ref.shape[0]

    def write(own):
        work = []
        for source, half in ((mine_hbm, own), (other_hbm, 1 - own)):
            for row, moves in places(half, out_refs):
                work.append((source.at[pl.ds(row, CHUNK), :], moves))
        reads = [
            pltpu.make_async_copy(source, read_ref.at[i % slots], read_sems.at[i % slots])
            for i, (source, _) in enumerate(work)
        ]
        for read in reads[:slots]:
            read.start()
        pending = [[] for _ in range(slots)]
        for i, (_, moves) in enumerate(work):
            slot = i % slots
            reads[i].wait()
            for copy in pending[slot]:
                copy.wait()
            stage_ref[slot] = read_ref[slot].astype(f32)
            if i + slots < len(work):
                reads[i + slots].start()
            pending[slot] = []
            for k, (lanes, target) in enumerate(moves):
                copy = pltpu.make_async_copy(stage_ref.at[slot, :, lanes], target, sems.at[slot, k])
                copy.start()
                pending[slot].append(copy)
        for copies in pending:
            for copy in copies:
                copy.wait()

    for own in range(2):
        pl.when(up_ref[0] == own)(functools.partial(write, own))


def finish(places, up, mine, outs, tokens=()):
    chans = mine.shape[1]
    slots = 16
    scratch = [pltpu.VMEM((slots, CHUNK, chans), bf16), pltpu.VMEM((slots, CHUNK, chans), f32)]
    scratch += [pltpu.SemaphoreType.DMA((slots,)), pltpu.SemaphoreType.DMA((slots, 2))]
    body = functools.partial(finish_kernel, places, len(tokens))
    operands = (*tokens, up.reshape(1), mine, partner(mine, "rows", 1))
    return call(body, [HB] * len(tokens) + [SM, HB, HB], [(o, HB) for o in outs], scratch, operands, 0)


def conv_places(half, out_ref):
    rows = out_ref.shape[0] // 2
    return [(r, [(slice(None), out_ref.at[pl.ds(half * rows + r, CHUNK), :])]) for r in range(0, rows, CHUNK)]


def early_places(half, out_refs):
    conv_ref, *squares = out_refs
    out = conv_places(half, conv_ref)
    row = conv_ref.shape[0] // 2
    for ref in squares[2 * half : 2 * half + 2]:
        for r in range(0, ref.shape[0], CHUNK):
            out.append((row, [(slice(None), ref.at[pl.ds(r, CHUNK), :])]))
            row += CHUNK
    return out


def late_places(half, out_refs):
    conv_ref, in_ref, vec_ref = out_refs
    return conv_places(half, conv_ref) + [(conv_ref.shape[0] // 2, [(slice(None), (in_ref, vec_ref)[half])])]


def book_places(half, out_refs):
    (book_ref,) = out_refs
    quarter, emb = book_ref.shape[0] // 4, book_ref.shape[1]
    out = []
    for r in range(0, quarter, CHUNK):
        to = half * quarter + r
        left = (pl.ds(0, emb), book_ref.at[pl.ds(to, CHUNK), :])
        right = (pl.ds(emb, emb), book_ref.at[pl.ds(2 * quarter + to, CHUNK), :])
        out.append((r, [left, right]))
    return out


def along(array, axis, by):
    count = lax.axis_size(axis)
    return lax.ppermute(array, axis, [(i, i + by) for i in range(count) if 0 <= i + by < count])


def around(array, axis, by):
    count = lax.axis_size(axis)
    return lax.ppermute(array, axis, [(i, (i + by) % count) for i in range(count)])


def swap(to_prev, to_next):
    return along(to_next, "rows", 1), along(to_prev, "rows", -1)


def partner(array, axis, bit):
    return lax.ppermute(array, axis, [(i, i ^ bit) for i in range(lax.axis_size(axis))])


def bits(axis):
    return [(axis, 1 << b) for b in range(lax.axis_size(axis).bit_length() - 1)]


def half_of(x, which):
    return lax.dynamic_slice_in_dim(x, which * (x.shape[0] // 2), x.shape[0] // 2)


def core_send(arrays):
    up = lax.axis_index("rows") % 2
    send = [half_of(x, 1 - up) for x in arrays]
    return partner(jnp.concatenate(send) if len(send) > 1 else send[0], "rows", 1)


def add(one, two):
    return (one.astype(f32) + two.astype(f32)).astype(bf16)


def join(parts):
    return jnp.concatenate(parts) if len(parts) > 1 else parts[0]


def exchange(axis, bit, jobs):
    up = (lax.axis_index(axis) // bit) % 2
    keep = [half_of(x, up) if reduce else x for reduce, x in jobs]
    got = partner(join([half_of(x, 1 - up) if reduce else x for reduce, x in jobs]), axis, bit)
    at, out = 0, []
    for (reduce, _), x in zip(jobs, keep):
        other = got[at : at + x.shape[0]]
        at += x.shape[0]
        if reduce:
            out.append(add(x, other))
        else:
            out.append(jnp.where(up == 0, jnp.concatenate([x, other]), jnp.concatenate([other, x])))
    return out


def plan(flip, *axes):
    middle = bits(axes[0])[1:]
    steps = (middle[::-1] if flip else middle) + [step for axis in axes[1:] for step in bits(axis)]
    return [(step, True) for step in steps] + [(step, False) for step in steps[::-1]]


def rounds(arrays, plans, begins, turns=None):
    arrays = list(arrays)
    for turn in turns or range(max(begin + len(p) for p, begin in zip(plans, begins))):
        by_partner = {}
        for i, (p, begin) in enumerate(zip(plans, begins)):
            if 0 <= turn - begin < len(p):
                step, reduce = p[turn - begin]
                by_partner.setdefault((begin, *step), []).append((i, reduce))
        for (_, *step), jobs in by_partner.items():
            out = exchange(*step, [(reduce, arrays[i]) for i, reduce in jobs])
            for (i, _), x in zip(jobs, out):
                arrays[i] = x
    return arrays


def streams(x, *axes):
    world = math.prod(lax.axis_size(axis) for axis in axes) // 2
    unit = 16 * world
    cut = -(-x.shape[0] // (2 * unit)) * unit
    return [x[:cut], x[cut:]]


def half_of(x, which):
    return lax.dynamic_slice_in_dim(x, which * (x.shape[0] // 2), x.shape[0] // 2)


def core_swap(x):
    up = lax.axis_index("rows") % 2
    return half_of(x, up), partner(half_of(x, 1 - up), "rows", 1)


def per_device(
    features, indices, img_width, img_start, codebook, w_in, b_in, gn1_gain, gn1_bias, conv1_w, conv1_b,
    gn2_gain, gn2_bias, conv2_w, conv2_b, gn3_gain, gn3_bias, w_query, b_query, w_key, w_value, b_value,
    w_proj, b_proj, cotangent,
):
    pixels, emb = features.shape[1], features.shape[2]
    chans = w_in.shape[1]
    nb = pixels // BLK
    widths, starts = img_width[0], img_start[0]
    first_pos = lax.axis_index("rows") * pixels
    row = lambda v: v.reshape(1, -1)

    positions = first_pos + jnp.arange(pixels, dtype=jnp.int32)
    image_id = jnp.sum((starts[None, :] <= positions[:, None]).astype(jnp.int32), axis=1) - 1
    choose = image_id[:, None] == jnp.arange(widths.shape[0], dtype=jnp.int32)[None, :]
    side = jnp.sum(jnp.where(choose, widths[None, :], 0), axis=1)
    begin = jnp.sum(jnp.where(choose, starts[None, :], 0), axis=1)
    offset = positions - begin
    safe = jnp.maximum(side, 1)
    row_at, col_at = offset // safe, offset % safe
    valid = []
    for dr in (-1, 0, 1):
        for dc in (-1, 0, 1):
            r, c = row_at + dr, col_at + dc
            valid.append((r >= 0) & (r < side) & (c >= 0) & (c < side))
    mask = jnp.stack(valid, axis=1).astype(f32)
    low_key = begin - first_pos + pixels
    spans = jnp.stack([low_key, low_key + side * side], axis=1)
    block_id = image_id[::BLK]
    ints = jnp.stack([side[::BLK], spans[::BLK, 0], spans[::BLK, 1]])
    count = (jnp.maximum(side * side, 1)[::BLK] * (chans // GN_GROUPS)).astype(f32)
    amat = jnp.concatenate(
        [
            (block_id[:, None] == block_id[None, :]).astype(f32),
            (block_id == block_id[0]).astype(f32)[:, None],
            (block_id == block_id[-1]).astype(f32)[:, None],
            (1.0 / count)[:, None],
        ],
        axis=1,
    )

    at_image = jnp.minimum(block_id[0] + jnp.arange(8, dtype=jnp.int32), widths.shape[0] - 1)
    pick = at_image[:, None] == jnp.arange(widths.shape[0], dtype=jnp.int32)[None, :]
    img_side = jnp.sum(jnp.where(pick, widths[None, :], 0), axis=1)
    img_at = jnp.sum(jnp.where(pick, starts[None, :], 0), axis=1) - first_pos
    images = jnp.stack(
        [
            img_at + pixels,
            img_side,
            jnp.maximum(img_at, 0),
            jnp.minimum(img_at + img_side * img_side, pixels),
            jnp.broadcast_to(block_id[-1] - block_id[0] + 1, (8,)),
        ]
    )

    groups = lax.axis_size("chan")
    codes = codebook.shape[0]
    ring = [indices[0]] + [around(indices, "chan", -d)[0] for d in range(1, groups)]
    local = [index - lax.axis_index("chan") * codes for index in ring]
    found = [lookup(index[:, None], codebook) for index in local[1:]]
    found.insert(0, lookup(local[0][:, None], codebook, found))
    rows_in = [found[0]] + [around(found[d], "chan", d) for d in range(1, groups)]

    stats2 = sds((2 * nb, chans), f32)
    rows32 = sds((pixels, chans), f32)
    msg32 = sds((HALO + 8, chans), f32)
    quant, resid_in, t_one, to_p, to_n = call(
        functools.partial(lift_kernel, groups, nb),
        [VM] * (4 + groups),
        [(o, VM) for o in (sds((pixels, emb), bf16), rows32, stats2, msg32, msg32)],
        [pltpu.VMEM((2 * nb, chans), f32)],
        (features[0], *rows_in, w_in, row(b_in), amat),
        2 * pixels * emb * chans,
    )
    p_one, n_one = swap(to_p, to_n)
    hid_one, stat_one, t_two, to_p, to_n, patch_one = conv_forward(
        resid_in, p_one, n_one, t_one, amat, row(gn1_gain), row(gn1_bias), mask, ints, conv1_w, row(conv1_b)
    )
    p_two, n_two = swap(to_p, to_n)
    cot = cotangent[0]
    resid_mid, stat_two, t_three, to_p, to_n, patch_two = conv_forward(
        hid_one, p_two, n_two, t_two, amat, row(gn2_gain), row(gn2_bias), mask, ints, conv2_w, row(conv2_b),
        resid_in, cot,
    )
    p_three, n_three = swap(to_p, to_n)
    normed, d_key, d_value, output, attn, d_query, u_own, stat_three, s_three, vec_three, to_p, to_n = attention(
        resid_mid, p_three, n_three, t_three, amat, row(gn3_gain), row(gn3_bias), ints, images,
        w_query, w_key, w_value, w_proj, row(b_query), row(b_value), row(b_proj), cot,
    )
    p_back, n_back = swap(to_p, to_n)
    tn = lambda a, b: jnp.einsum("nk,nc->kc", a, b, preferred_element_type=f32).astype(bf16)
    own_normed = normed[pixels : 2 * pixels]
    g_proj = tn(attn, cot)
    g_query = tn(own_normed, d_query)
    g_key = tn(normed, d_key)
    g_value = tn(normed, d_value)
    g_attn = jnp.concatenate([g_proj, g_query, g_key, g_value])
    g_b_proj = jnp.sum(cot.astype(f32), axis=0, keepdims=True)
    g_b_query = jnp.sum(d_query.astype(f32), axis=0, keepdims=True)
    g_b_value = jnp.sum(d_value.astype(f32), axis=0, keepdims=True)
    g_attn, d_mid, err_two, v_two, s_two, vec_two, msg_p, msg_n = conv_backward(
        True, g_attn, (u_own, to_p, to_n, p_back, n_back, p_three, n_three, cot),
        resid_mid, stat_three, s_three, row(gn3_gain), amat, mask, ints, conv2_w,
        hid_one, stat_two, row(gn2_gain), row(gn2_bias),
    )
    p_four, n_four = swap(msg_p, msg_n)
    g_conv2 = tn(patch_two, err_two)
    g_conv2, err_one, v_one, s_one, vec_one, msg_p, msg_n = conv_backward(
        False, g_conv2, (v_two, p_four, n_four, p_two, n_two),
        hid_one, stat_two, s_two, row(gn2_gain), amat, mask, ints, conv1_w,
        resid_in, stat_one, row(gn1_gain), row(gn1_bias),
    )
    p_five, n_five = swap(msg_p, msg_n)
    err_one, g_conv2, g_attn, err_in, feature_grad, vec_in = tail(
        (err_one, g_conv2, g_attn), v_one, p_five, n_five, s_one, resid_in, stat_one, row(gn1_gain), amat, d_mid, w_in
    )
    below, above = [feature_grad], [feature_grad]
    for _ in range(1, groups):
        below.append(along(below[-1], "chan", 1))
        above.append(along(above[-1], "chan", -1))
    two = jnp.concatenate([add(*core_swap(g_conv2)), add(*core_swap(g_attn))])
    g_conv1 = tn(patch_one, err_one)
    vectors = (vec_in, vec_one, vec_two, vec_three, g_b_query, g_b_value, g_b_proj)
    g_conv1, begun, small = own_part(g_conv1, two, row(local[0]), feature_grad, quant, err_in, vectors, codes)
    one = add(*core_swap(g_conv1))
    small = add(*core_swap(small))
    both = [plan(flip, "rows", "chan") for flip in (False, True)]
    plans = both + both + both[1:] + [plan(flip, "rows") for flip in (False, True)]
    begins = [0, 0, LATE_ROUND, LATE_ROUND, LATE_ROUND, BOOK_ROUND, BOOK_ROUND]
    pair = lambda d: (row(local[groups - d]), (below[d], above[groups - d]))
    middle = [pair(d) for d in range(1, groups) if 2 * d == groups]
    outer = [pair(d) for d in range(1, groups) if 2 * d != groups]
    work = rounds(streams(two, "rows", "chan"), plans[:2], begins, range(1))
    book = scatter(*zip(*middle), codes, f32, begun, work)
    work = rounds(work, plans[:2], begins, range(1, 2))
    book = scatter(*zip(*outer), codes, bf16, book, work)
    book = add(*core_swap(book))
    work += streams(one, "rows", "chan") + [small] + streams(book, "rows")
    turns = max(begin + len(p) for p, begin in zip(plans, begins))
    work = rounds(work, plans, begins, range(2, turns))
    up = lax.axis_index("rows") % 2
    square, conv = sds((chans, chans), f32), sds((9 * chans, chans), f32)
    early = finish(early_places, up, jnp.concatenate(work[:2]), [conv] + [square] * 4)
    book = finish(book_places, up, jnp.concatenate(work[5:]), [sds((codes, emb), f32)])
    narrow = [sds((emb, chans), f32), sds((chans - emb, chans), f32)]
    sum_one, s_in, vec = finish(
        late_places, up, jnp.concatenate(work[2:5]), [conv] + narrow, (early[0], book[0])
    )
    sum_two, s_proj, s_query, s_key, s_value = early
    (book_grad,) = book
    return (
        output[None],
        feature_grad[None],
        book_grad,
        s_in,
        vec[0],
        vec[1],
        vec[2],
        sum_one.reshape(conv1_w.shape),
        vec[3],
        vec[4],
        vec[5],
        sum_two.reshape(conv2_w.shape),
        vec[6],
        vec[7],
        vec[8],
        s_query,
        vec[9],
        s_key,
        s_value,
        vec[10],
        s_proj,
        vec[11],
    )


def solution(mesh):
    group, copied = P("chan", "rows", None), P()
    placed = (group, P("chan", "rows"), P("chan", None), P("chan", None), P("chan", None))
    return jax.shard_map(
        per_device,
        mesh=mesh,
        in_specs=placed + (copied,) * 19 + (group,),
        out_specs=(group, group, P("chan", None)) + (copied,) * 19,
        check_vma=False,
    )
```

time: 1630 us -> 528 us (0.32)
  local copies, waits for them, and re-layouts: 470 us -> 25.2 us
  waiting for transfers between devices: 583 us -> 164 us
  matrix products: 188 us -> 28 us
  Pallas kernels: 0 us -> 141 us
  other arithmetic: 148 us -> 24.9 us
  blocking collectives: 52.6 us -> 0 us
    psum x2 -> x0, waiting for transfers between devices: 382 us -> none  [the longest x1 380 us: per_device(): lax.psum((g_w_in, g_b_in, g_gain_one, g_bias_one, g_conv1_w, g_conv1_b, g...]
    gather x9 -> x0, local copies, waits for them, and re-layouts: 230 us -> none  [the longest x8 221 us: gather_taps(): picked = jnp.take(extended, tap_index, axis=0)]
    all_gather x2 -> x0, waiting for transfers between devices: 185 us -> none  [the longest x1 152 us: per_device(): lax.all_gather(codebook, 'chan', axis=0, tiled=True)]
    dot_general x56 -> x6, matrix products: 188 us -> 28 us  [per_device(): jnp.einsum('nk,nc->kc', a, b, preferred_element_type=f32).astype(bf16)]
    ppermute x24 -> x64, waiting for transfers between devices: 16 us -> 164 us  [the longest x40 122 us: partner(): lax.ppermute(array, axis, [(i, i ^ bit) for i in range(lax.axis_size(axis...]
    pallas_call x0 -> x17, Pallas kernels: none -> 141 us  [the longest x11 119 us: call(): pl.pallas_call(body, out_shape=[o[0] for o in outs], in_specs=ins, out_sp...]
    dynamic_update_slice x4 -> x0, local copies, waits for them, and re-layouts: 82 us -> none  [the longest x2 81.9 us: block_backward(): lax.dynamic_update_slice_in_dim(grad_ext, current + jnp.concatenate([d_ke...]
    select_n x3 -> x0, local copies, waits for them, and re-layouts: 43.9 us -> none  [the longest x2 43.7 us: gather_taps(): jnp.where(tap_valid[:, :, None], picked, jnp.zeros((), extended.dtype))]
  transfers between devices with their start and end apart: 28 -> 64, of which waited for: 13 -> 31; matrix products, arithmetic and copies ran while one was open for 4% -> 12% of each run, Pallas kernels for 0% -> 7%
where the time goes in v1:
time: 528 us; the launch traced here: 520 us
  waiting for transfers between devices  164 us (31%)
  Pallas kernels  141 us (27%)
  starting transfers between devices  133 us (25%)
  matrix products  28 us (5%)
  local copies, waits for them, and re-layouts  25.2 us (5%)
  other arithmetic  24.9 us (5%)
    ppermute x40, waiting for transfers between devices, partner(): lax.ppermute(array, axis, [(i, i ^ bit) for i in range(lax.axis_size(axis...  122 us
    pallas_call x11, Pallas kernels, call(): pl.pallas_call(body, out_shape=[o[0] for o in outs], in_specs=ins, out_sp...  119 us
    ppermute x18, starting transfers between devices, along(): lax.ppermute(array, axis, [(i, i + by) for i in range(count) if 0 <= i +...  87.9 us
    ppermute x40, starting transfers between devices, partner(): lax.ppermute(array, axis, [(i, i ^ bit) for i in range(lax.axis_size(axis...  33.8 us
    dot_general x6, matrix products, per_device(): jnp.einsum('nk,nc->kc', a, b, preferred_element_type=f32).astype(bf16)  28 us
    ppermute x6, waiting for transfers between devices, around(): lax.ppermute(array, axis, [(i, (i + by) % count) for i in range(count)])  28 us
    unnamed x82, local copies, waits for them, and re-layouts  15.2 us
    ppermute x18, waiting for transfers between devices, along(): lax.ppermute(array, axis, [(i, i + by) for i in range(count) if 0 <= i +...  13.9 us
  transfers between devices with their start and end apart: 64, of which 31 were waited for; matrix products, arithmetic and copies ran while one was open for 12% of the time, Pallas kernels for 7%

profile of v1, /device:TPU:0, one launch (start us, length us, event | category | flops | bytes accessed | tf_op | source)
XLA Modules:
  0.0 520.0 jit_solution(2587353765865927826)
XLA Ops:
  0.7 4.1 collective-permute-start.1
  14.5 3.0 shard_map.410.refs_2_
  17.5 3.0 shard_map.408.refs_0_
  22.4 3.0 shard_map.409.refs_1_
  26.6 2.7 collective-permute-start.3
  31.1 3.0 shard_map.411.refs_1_
  35.0 28.0 %collective-permute-done.4.refs_3_ = bf16[1024,256]{1,0:T(8,128)(2,1)S(1)} collective-permute-done((bf16[1024,256]{1,0:T(8,128)(2,1)S(1)}, bf16[1024,256]{1,0:T(8,128)(2,1)S(1)}, u32[]{:S(2)}, u32[]{:S(2)}) %collective-permute-start.4) | collective-permute-done | bytes 524320 | tf_op jit(solution)/shard_map/ppermute | solution.py:785
  64.1 4.1 shard_map.412
  69.5 1.8 collective-permute-start.7
  75.3 14.4 %shard_map.413 = (f32[1024,512]{1,0:T(8,128)}, f32[32,512]{1,0:T(8,128)}, f32[32,512]{1,0:T(8,128)}, f32[72,512]{1,0:T(8,128)}, f32[72,512]{1,0:T(8,128)}, /*index=5*/bf16[1024,4608]{1,0:T(8,128)(2,1)}) custom-call(f32[1024,512]{1,0:T(8,128)} %get-tuple-element.83.refs_0_.refs_11_.refs_14_.refs_7_, f32[72,512]{1,0:T(8,128)} %copy-done.30, ...), custom_call_target="tpu_custom_call" | custom-call | flops 4831838208 | bytes 19180928 | tf_op jit(solution)/shard_map/pallas_call | solution.py:34
  89.7 5.6 %collective-permute-start.8 = (f32[72,512]{1,0:T(8,128)}, f32[72,512]{1,0:T(8,128)S(1)}, u32[]{:S(2)}, u32[]{:S(2)}) collective-permute-start(f32[72,512]{1,0:T(8,128)} %get-tuple-element.88), channel_id=1, source_target_pairs={{0,4},{4,8},{8,12},{12,16},{16,20},{20,24},{24,28},{1,5},{5,9},{9,... | collective-permute-start | bytes 442376 | tf_op jit(solution)/shard_map/ppermute | solution.py:780
  100.0 16.1 %shard_map.414 = (f32[1024,512]{1,0:T(8,128)}, f32[32,512]{1,0:T(8,128)}, f32[32,512]{1,0:T(8,128)}, bf16[1104,512]{1,0:T(8,128)(2,1)}, bf16[1104,512]{1,0:T(8,128)(2,1)}, /*index=5*/bf16[1024,4608]{1,0:T(8,128)(2,1)}) custom-call(f32[1024,512]{1,0:T(8,128)} %get-tuple-element.87.refs_0_.refs_17_.refs_6_, f32[72,512]{1,0:T(8,128)} %copy-done.28, ...), custom_call_target="tpu_custom_call" | custom-call | flops 4831838208 | bytes 24292736 | tf_op jit(solution)/shard_map/pallas_call | solution.py:34
  116.0 5.4 %collective-permute-start.10 = (bf16[1104,512]{1,0:T(8,128)(2,1)}, bf16[1104,512]{1,0:T(8,128)(2,1)S(1)}, u32[]{:S(2)}, u32[]{:S(2)}) collective-permute-start(bf16[1104,512]{1,0:T(8,128)(2,1)} %get-tuple-element.92), channel_id=1, source_target_pairs={{0,4},{4,8},{8,12},{12,16},{16,20},{20,24},{24,28},{1,5},{5,9},{9,... | collective-permute-start | bytes 3391496 | tf_op jit(solution)/shard_map/ppermute | solution.py:780
  127.3 25.6 %shard_map.415 = (bf16[3072,512]{1,0:T(8,128)(2,1)}, bf16[3072,512]{1,0:T(8,128)(2,1)}, bf16[3072,512]{1,0:T(8,128)(2,1)}, bf16[1024,512]{1,0:T(8,128)(2,1)}, bf...) custom-call(f32[1024,512]{1,0:T(8,128)} %get-tuple-element.91.refs_0, ...), custom_call_target="tpu_custom_call" | custom-call | flops 12884901888 | bytes 24669728 | tf_op jit(solution)/shard_map/pallas_call | solution.py:34
  154.2 26.5 %collective-permute-start.12 = (bf16[1104,512]{1,0:T(8,128)(2,1)}, bf16[1104,512]{1,0:T(8,128)(2,1)S(1)}, u32[]{:S(2)}, u32[]{:S(2)}) collective-permute-start(bf16[1104,512]{1,0:T(8,128)(2,1)} %get-tuple-element.104.refs_3_), channel_id=1, source_target_pairs={{0,4},{4,8},{8,12},{12,16},{16,20},{20,24},{24,28},{1,5},{5,9},{9,... | collective-permute-start | bytes 3391496 | tf_op jit(solution)/shard_map/ppermute | solution.py:780
  180.7 4.8 convolution_convert_fusion.2
  189.0 1.8 convolution_convert_fusion.3
  193.6 17.1 %shard_map.416 = (bf16[2048,512]{1,0:T(8,128)(2,1)}, f32[1024,512]{1,0:T(8,128)}, bf16[1024,512]{1,0:T(8,128)(2,1)}, f32[1024,512]{1,0:T(8,128)}, f32[32,512]{1,...) custom-call(bf16[2048,512]{1,0:T(8,128)(2,1)} %pad_maximum_fusion.3.re, ...), custom_call_target="tpu_custom_call", output_to_operand_aliasing={{0}: (0, {})} | custom-call | flops 4831838208 | bytes 28896640 | tf_op jit(solution)/shard_map/pallas_call | solution.py:34
  210.7 10.0 %collective-permute-start.14 = (f32[72,512]{1,0:T(8,128)}, f32[72,512]{1,0:T(8,128)S(1)}, u32[]{:S(2)}, u32[]{:S(2)}) collective-permute-start(f32[72,512]{1,0:T(8,128)} %get-tuple-element.110), channel_id=1, source_target_pairs={{0,4},{4,8},{8,12},{12,16},{16,20},{20,24},{24,28},{1,5},{5,9},{9,... | collective-permute-start | bytes 442376 | tf_op jit(solution)/shard_map/ppermute | solution.py:780
  222.2 9.4 %convolution_convert_fusion.1.refs_0_ = bf16[4608,512]{1,0:T(8,128)(2,1)} fusion(bf16[1024,4608]{1,0:T(8,128)(2,1)} %get-tuple-element.96, bf16[1024,512]{1,0:T(8,128)(2,1)} %get-tuple-element.108), kind=kOutput, calls=%fused_computation.1 | convolution fusion | flops 4834197504 | bytes 15204352 | tf_op jit(solution)/shard_map/nk,nc->kc/dot_general | solution.py:960
  232.2 14.7 %shard_map.417 = (bf16[4608,512]{1,0:T(8,128)(2,1)}, bf16[1024,512]{1,0:T(8,128)(2,1)}, f32[1024,512]{1,0:T(8,128)}, f32[32,512]{1,0:T(8,128)}, f32[8,512]{1,0:T...) custom-call(bf16[4608,512]{1,0:T(8,128)(2,1)} %convolution_convert_fusion.1.refs_0_, ...), custom_call_target="tpu_custom_call", output_to_operand_aliasing={{0}: (0, {})} | custom-call | flops 4831838208 | bytes 24538496 | tf_op jit(solution)/shard_map/pallas_call | solution.py:34
  247.0 3.6 collective-permute-start.16
  252.0 8.0 %collective-permute-done.17.refs_5_ = f32[8,512]{1,0:T(8,128)S(1)} collective-permute-done((f32[8,512]{1,0:T(8,128)}, f32[8,512]{1,0:T(8,128)S(1)}, u32[]{:S(2)}, u32[]{:S(2)}) %collective-permute-start.17) | collective-permute-done | bytes 16416 | tf_op jit(solution)/shard_map/ppermute | solution.py:780
  260.6 4.9 shard_map.418
  266.8 13.9 %collective-permute-start.24 = (bf16[1024,256]{1,0:T(8,128)(2,1)}, bf16[1024,256]{1,0:T(8,128)(2,1)S(1)}, u32[]{:S(2)}, u32[]{:S(2)}) collective-permute-start(bf16[1024,256]{1,0:T(8,128)(2,1)} %get-tuple-element.122.grad_ref), channel_id=1, source_target_pairs={{0,1},{1,2},{2,3},{4,5},{5,6},{6,7},{8,9},{9,10},{10,11},{12,13},{... | collective-permute-start | bytes 1572872 | tf_op jit(solution)/shard_map/ppermute | solution.py:780
  280.7 2.0 constant_dynamic-slice_fusion.28
  282.7 2.3 collective-permute-start.18
  287.0 2.7 collective-permute-done.25.refs_7_
  291.5 4.3 collective-permute-start.28
  295.8 10.6 %convolution_convert_fusion.pass_ref = bf16[4608,512]{1,0:T(8,128)(2,1)} fusion(bf16[1024,4608]{1,0:T(8,128)(2,1)} %get-tuple-element.125, bf16[1024,512]{1,0:T(8,128)(2,1)S(1)} %copy-done.16), kind=kOutput, calls=%fused_computation | convolution fusion | flops 4834197504 | bytes 15204352 | tf_op jit(solution)/shard_map/nk,nc->kc/dot_general | solution.py:960
  307.8 4.9 collective-permute-start.29
  316.1 5.5 %collective-permute-start.22 = (bf16[768,512]{1,0:T(8,128)(2,1)}, bf16[768,512]{1,0:T(8,128)(2,1)}, u32[]{:S(2)}, u32[]{:S(2)}) collective-permute-start(bf16[768,512]{1,0:T(8,128)(2,1)} %constant_dynamic-slice_fusion.24), channel_id=1, source_target_pairs={{0,16},{4,20},{8,24},{12,28},{16,0},{20,4},{24,8},{28,12},{1,17},{... | collective-permute-start | bytes 2359304 | tf_op jit(solution)/shard_map/ppermute | solution.py:793
  322.6 2.0 pad_maximum_fusion.token_ref
  324.6 6.1 %shard_map.419 = (bf16[4608,512]{1,0:T(8,128)(2,1)}, f32[2048,512]{1,0:T(8,128)}, bf16[512,512]{1,0:T(8,128)(2,1)}) custom-call(bf16[4608,512]{1,0:T(8,128)(2,1)} %convolution_convert_fusion.pass_ref, bf16[3328,512]{1,0:T(8,128)(2,1)} %pad_maximum_fusion.token_ref, s32[1,1024]{1,0:T(1,128)} %broadcast_subtract_fusion.index_ref, ...), custom_call_target="tpu_custom_call", output_to_operand_aliasing={{0}: (0, {})} | custom-call | flops 2415919104 | bytes 19736576 | tf_op jit(solution)/shard_map/pallas_call | solution.py:34
  330.7 7.8 %collective-permute-done.22 = bf16[768,512]{1,0:T(8,128)(2,1)} collective-permute-done((bf16[768,512]{1,0:T(8,128)(2,1)}, bf16[768,512]{1,0:T(8,128)(2,1)}, u32[]{:S(2)}, u32[]{:S(2)}) %collective-permute-start.22) | collective-permute-done | bytes 786464 | tf_op jit(solution)/shard_map/ppermute | solution.py:793
  338.5 1.7 add_convert_fusion.5.refs_1_
  340.4 5.7 %collective-permute-done.19 = bf16[896,512]{1,0:T(8,128)(2,1)S(1)} collective-permute-done((bf16[896,512]{1,0:T(8,128)(2,1)}, bf16[896,512]{1,0:T(8,128)(2,1)S(1)}, u32[]{:S(2)}, u32[]{:S(2)}) %collective-permute-start.19) | collective-permute-done | bytes 917536 | tf_op jit(solution)/shard_map/ppermute | solution.py:793
  346.5 5.5 %collective-permute-done.23 = bf16[384,512]{1,0:T(8,128)(2,1)S(1)} collective-permute-done((bf16[384,512]{1,0:T(8,128)(2,1)S(1)}, bf16[384,512]{1,0:T(8,128)(2,1)S(1)}, u32[]{:S(2)}, u32[]{:S(2)}) %collective-permute-start.23) | collective-permute-done | bytes 393248 | tf_op jit(solution)/shard_map/ppermute | solution.py:793
  352.2 2.7 collective-permute-done.20
  356.5 9.1 %collective-permute-done.40 = bf16[416,512]{1,0:T(8,128)(2,1)S(1)} collective-permute-done((bf16[416,512]{1,0:T(8,128)(2,1)S(1)}, bf16[416,512]{1,0:T(8,128)(2,1)S(1)}, u32[]{:S(2)}, u32[]{:S(2)}) %collective-permute-start.40) | collective-permute-done | bytes 426016 | tf_op jit(solution)/shard_map/ppermute | solution.py:793
  365.9 4.1 shard_map.420.refs_8_
  370.0 7.2 %collective-permute-done.41 = bf16[208,512]{1,0:T(8,128)(2,1)S(1)} collective-permute-done((bf16[208,512]{1,0:T(8,128)(2,1)S(1)}, bf16[208,512]{1,0:T(8,128)(2,1)S(1)}, u32[]{:S(2)}, u32[]{:S(2)}) %collective-permute-start.41) | collective-permute-done | bytes 213024 | tf_op jit(solution)/shard_map/ppermute | solution.py:793
  377.4 5.9 %shard_map.421 = bf16[2048,512]{1,0:T(8,128)(2,1)S(1)} custom-call(bf16[448,512]{1,0:T(8,128)(2,1)S(1)} %add_convert_fusion.8.refs_0_, bf16[384,512]{1,0:T(8,128)(2,1)S(1)} %add_convert_fusion.9.refs_1_, s32[1,1024]{1,0:T(1,128)S(1)} %broadcast_subtract_fusion.1.refs_2_, s32[1,1024]{1,0:T(1,128)S(1)} %broadcast_subtract_fusion.3.refs_3_, ...), custom_call_target="tpu_custom_call" | custom-call | flops 4294967296 | bytes 8388608 | tf_op jit(solution)/shard_map/pallas_call | solution.py:208
  383.5 1.9 collective-permute-done.42
  388.2 15.8 %collective-permute-done.50 = bf16[640,512]{1,0:T(8,128)(2,1)S(1)} collective-permute-done((bf16[640,512]{1,0:T(8,128)(2,1)S(1)}, bf16[640,512]{1,0:T(8,128)(2,1)S(1)}, u32[]{:S(2)}, u32[]{:S(2)}) %collective-permute-start.50) | collective-permute-done | bytes 655392 | tf_op jit(solution)/shard_map/ppermute | solution.py:793
  406.2 7.1 %collective-permute-done.51 = bf16[320,512]{1,0:T(8,128)(2,1)S(1)} collective-permute-done((bf16[320,512]{1,0:T(8,128)(2,1)S(1)}, bf16[320,512]{1,0:T(8,128)(2,1)S(1)}, u32[]{:S(2)}, u32[]{:S(2)}) %collective-permute-start.51) | collective-permute-done | bytes 327712 | tf_op jit(solution)/shard_map/ppermute | solution.py:793
  418.1 3.8 collective-permute-done.55
  422.0 1.8 collective-permute-start.56
  424.7 4.3 collective-permute-done.46
  431.0 2.2 collective-permute-start.57
  433.4 4.2 collective-permute-done.44
  441.4 11.3 %collective-permute-done.47 = bf16[768,512]{1,0:T(8,128)(2,1)S(1)} collective-permute-done((bf16[768,512]{1,0:T(8,128)(2,1)S(1)}, bf16[768,512]{1,0:T(8,128)(2,1)S(1)}, u32[]{:S(2)}, u32[]{:S(2)}) %collective-permute-start.47) | collective-permute-done | bytes 786464 | tf_op jit(solution)/shard_map/ppermute | solution.py:793
  457.3 3.3 collective-permute-done.61
  461.4 5.1 collective-permute-done.59
  467.7 9.0 %collective-permute-done.62 = bf16[640,512]{1,0:T(8,128)(2,1)S(1)} collective-permute-done((bf16[640,512]{1,0:T(8,128)(2,1)S(1)}, bf16[640,512]{1,0:T(8,128)(2,1)S(1)}, u32[]{:S(2)}, u32[]{:S(2)}) %collective-permute-start.62) | collective-permute-done | bytes 655392 | tf_op jit(solution)/shard_map/ppermute | solution.py:793
  480.1 4.2 collective-permute-done.36
  486.5 4.2 collective-permute-done.37
  492.4 2.7 collective-permute-done.34
  495.3 2.0 collective-permute-done.38
  498.6 2.7 collective-permute-done.39.refs_2_
  502.2 3.5 shard_map.422.refs_1_
  505.8 6.9 %shard_map.423 = (f32[4608,512]{1,0:T(8,128)}, f32[512,512]{1,0:T(8,128)}, f32[512,512]{1,0:T(8,128)}, f32[512,512]{1,0:T(8,128)}, f32[512,512]{1,0:T(8,128)}) custom-call(s32[1]{0:T(128)} %bitcast.38.refs_0_.refs_2_, bf16[3328,512]{1,0:T(8,128)(2,1)} %copy-done.5, bf16[3328,512]{1,0:T(8,128)(2,1)} %collective-permute-done.48.refs_2_), custom_call_target="tpu_custom_call" | custom-call | bytes 20447236 | tf_op jit(solution)/shard_map/pallas_call | solution.py:34
  512.7 5.4 %shard_map.424 = (f32[4608,512]{1,0:T(8,128)}, f32[256,512]{1,0:T(8,128)}, f32[256,512]{1,0:T(8,128)}) custom-call(f32[4608,512]{1,0:T(8,128)} %get-tuple-element.134.refs_0_, f32[4096,256]{1,0:T(8,128)} %shard_map.422.refs_1_, s32[1]{0:T(128)} %bitcast.38.refs_0_.refs_2_, bf16[2560,512]{1,0:T(8,128)(2,1)} %copy-done.6, ...), custom_call_target="tpu_custom_call" | custom-call | bytes 29360132 | tf_op jit(solution)/shard_map/pallas_call | solution.py:34
  518.1 1.6 fusion.11
  (335 shorter events, 88.1 us)
Async XLA Ops:
  0.7 19.9 %collective-permute-start.1 = (s32[1,1024]{1,0:T(1,128)}, s32[1,1024]{1,0:T(1,128)S(1)}, u32[]{:S(2)}, u32[]{:S(2)}) collective-permute-start(s32[1,1024]{1,0:T(1,128)} %param.26), channel_id=1, source_target_pairs={{0,2},{1,3},{2,0},{3,1},{4,6},{5,7},{6,4},{7,5},{8,10},{9,11},{10,... | collective-permute-start | bytes 12296 | tf_op jit(solution)/shard_map/ppermute | solution.py:785
  4.8 7.9 %collective-permute-start = (s32[1,1024]{1,0:T(1,128)}, s32[1,1024]{1,0:T(1,128)S(1)}, u32[]{:S(2)}, u32[]{:S(2)}) collective-permute-start(s32[1,1024]{1,0:T(1,128)} %param.26), channel_id=1, source_target_pairs={{0,3},{1,0},{2,1},{3,2},{4,7},{5,4},{6,5},{7,6},{8,11},{9,8},{10,9... | collective-permute-start | bytes 12296 | tf_op jit(solution)/shard_map/ppermute | solution.py:785
  6.1 6.3 %collective-permute-start.2 = (s32[1,1024]{1,0:T(1,128)}, s32[1,1024]{1,0:T(1,128)S(1)}, u32[]{:S(2)}, u32[]{:S(2)}) collective-permute-start(s32[1,1024]{1,0:T(1,128)} %param.26), channel_id=1, source_target_pairs={{0,1},{1,2},{2,3},{3,0},{4,5},{5,6},{6,7},{7,4},{8,9},{9,10},{10,1... | collective-permute-start | bytes 12296 | tf_op jit(solution)/shard_map/ppermute | solution.py:785
  25.5 37.5 %collective-permute-start.4 = (bf16[1024,256]{1,0:T(8,128)(2,1)S(1)}, bf16[1024,256]{1,0:T(8,128)(2,1)S(1)}, u32[]{:S(2)}, u32[]{:S(2)}) collective-permute-start(bf16[1024,256]{1,0:T(8,128)(2,1)S(1)} %shard_map.409.refs_1_), channel_id=1, source_target_pairs={{0,2},{1,3},{2,0},{3,1},{4,6},{5,7},{6,4},{7,5},{8,10},{9,11},{10,... | collective-permute-start | bytes 1572872 | tf_op jit(solution)/shard_map/ppermute | solution.py:785
  26.6 36.4 %collective-permute-start.3 = (bf16[1024,256]{1,0:T(8,128)(2,1)S(1)}, bf16[1024,256]{1,0:T(8,128)(2,1)S(1)}, u32[]{:S(2)}, u32[]{:S(2)}) collective-permute-start(bf16[1024,256]{1,0:T(8,128)(2,1)S(1)} %shard_map.408.refs_0_), channel_id=1, source_target_pairs={{0,1},{1,2},{2,3},{3,0},{4,5},{5,6},{6,7},{7,4},{8,9},{9,10},{10,1... | collective-permute-start | bytes 1572872 | tf_op jit(solution)/shard_map/ppermute | solution.py:785
  29.3 33.7 %collective-permute-start.5 = (bf16[1024,256]{1,0:T(8,128)(2,1)S(1)}, bf16[1024,256]{1,0:T(8,128)(2,1)S(1)}, u32[]{:S(2)}, u32[]{:S(2)}) collective-permute-start(bf16[1024,256]{1,0:T(8,128)(2,1)S(1)} %shard_map.410.refs_2_), channel_id=1, source_target_pairs={{0,3},{1,0},{2,1},{3,2},{4,7},{5,4},{6,5},{7,6},{8,11},{9,8},{10,9... | collective-permute-start | bytes 1572872 | tf_op jit(solution)/shard_map/ppermute | solution.py:785
  68.2 5.3 %collective-permute-start.6 = (f32[72,512]{1,0:T(8,128)}, f32[72,512]{1,0:T(8,128)S(1)}, u32[]{:S(2)}, u32[]{:S(2)}) collective-permute-start(f32[72,512]{1,0:T(8,128)} %get-tuple-element.84), channel_id=1, source_target_pairs={{0,4},{4,8},{8,12},{12,16},{16,20},{20,24},{24,28},{1,5},{5,9},{9,... | collective-permute-start | bytes 442376 | tf_op jit(solution)/shard_map/ppermute | solution.py:780
  69.5 5.2 collective-permute-start.7
  89.7 9.6 %collective-permute-start.8 = (f32[72,512]{1,0:T(8,128)}, f32[72,512]{1,0:T(8,128)S(1)}, u32[]{:S(2)}, u32[]{:S(2)}) collective-permute-start(f32[72,512]{1,0:T(8,128)} %get-tuple-element.88), channel_id=1, source_target_pairs={{0,4},{4,8},{8,12},{12,16},{16,20},{20,24},{24,28},{1,5},{5,9},{9,... | collective-permute-start | bytes 442376 | tf_op jit(solution)/shard_map/ppermute | solution.py:780
  95.3 4.0 collective-permute-start.9
  116.0 9.0 %collective-permute-start.10 = (bf16[1104,512]{1,0:T(8,128)(2,1)}, bf16[1104,512]{1,0:T(8,128)(2,1)S(1)}, u32[]{:S(2)}, u32[]{:S(2)}) collective-permute-start(bf16[1104,512]{1,0:T(8,128)(2,1)} %get-tuple-element.92), channel_id=1, source_target_pairs={{0,4},{4,8},{8,12},{12,16},{16,20},{20,24},{24,28},{1,5},{5,9},{9,... | collective-permute-start | bytes 3391496 | tf_op jit(solution)/shard_map/ppermute | solution.py:780
  121.4 4.9 collective-permute-start.11
  152.9 39.3 %collective-permute-start.13 = (bf16[1104,512]{1,0:T(8,128)(2,1)}, bf16[1104,512]{1,0:T(8,128)(2,1)S(1)}, u32[]{:S(2)}, u32[]{:S(2)}) collective-permute-start(bf16[1104,512]{1,0:T(8,128)(2,1)} %get-tuple-element.103.refs_2_), channel_id=1, source_target_pairs={{4,0},{8,4},{12,8},{16,12},{20,16},{24,20},{28,24},{5,1},{9,5},{13... | collective-permute-start | bytes 3391496 | tf_op jit(solution)/shard_map/ppermute | solution.py:780
  154.2 38.0 %collective-permute-start.12 = (bf16[1104,512]{1,0:T(8,128)(2,1)}, bf16[1104,512]{1,0:T(8,128)(2,1)S(1)}, u32[]{:S(2)}, u32[]{:S(2)}) collective-permute-start(bf16[1104,512]{1,0:T(8,128)(2,1)} %get-tuple-element.104.refs_3_), channel_id=1, source_target_pairs={{0,4},{4,8},{8,12},{12,16},{16,20},{20,24},{24,28},{1,5},{5,9},{9,... | collective-permute-start | bytes 3391496 | tf_op jit(solution)/shard_map/ppermute | solution.py:780
  210.7 20.8 %collective-permute-start.14 = (f32[72,512]{1,0:T(8,128)}, f32[72,512]{1,0:T(8,128)S(1)}, u32[]{:S(2)}, u32[]{:S(2)}) collective-permute-start(f32[72,512]{1,0:T(8,128)} %get-tuple-element.110), channel_id=1, source_target_pairs={{0,4},{4,8},{8,12},{12,16},{16,20},{20,24},{24,28},{1,5},{5,9},{9,... | collective-permute-start | bytes 442376 | tf_op jit(solution)/shard_map/ppermute | solution.py:780
  220.7 10.8 %collective-permute-start.15 = (f32[72,512]{1,0:T(8,128)}, f32[72,512]{1,0:T(8,128)S(1)}, u32[]{:S(2)}, u32[]{:S(2)}) collective-permute-start(f32[72,512]{1,0:T(8,128)} %get-tuple-element.111), channel_id=1, source_target_pairs={{4,0},{8,4},{12,8},{16,12},{20,16},{24,20},{28,24},{5,1},{9,5},{13... | collective-permute-start | bytes 442376 | tf_op jit(solution)/shard_map/ppermute | solution.py:780
  247.0 5.0 collective-permute-start.16
  250.6 9.4 %collective-permute-start.17 = (f32[8,512]{1,0:T(8,128)}, f32[8,512]{1,0:T(8,128)S(1)}, u32[]{:S(2)}, u32[]{:S(2)}) collective-permute-start(f32[8,512]{1,0:T(8,128)} %get-tuple-element.119), channel_id=1, source_target_pairs={{4,0},{8,4},{12,8},{16,12},{20,16},{24,20},{28,24},{5,1},{9,5},{13... | collective-permute-start | bytes 49160 | tf_op jit(solution)/shard_map/ppermute | solution.py:780
  265.5 24.1 %collective-permute-start.25 = (bf16[1024,256]{1,0:T(8,128)(2,1)}, bf16[1024,256]{1,0:T(8,128)(2,1)S(1)}, u32[]{:S(2)}, u32[]{:S(2)}) collective-permute-start(bf16[1024,256]{1,0:T(8,128)(2,1)} %get-tuple-element.122.grad_ref), channel_id=1, source_target_pairs={{1,0},{2,1},{3,2},{5,4},{6,5},{7,6},{9,8},{10,9},{11,10},{13,12},{... | collective-permute-start | bytes 1572872 | tf_op jit(solution)/shard_map/ppermute | solution.py:780
  266.8 24.7 %collective-permute-start.24 = (bf16[1024,256]{1,0:T(8,128)(2,1)}, bf16[1024,256]{1,0:T(8,128)(2,1)S(1)}, u32[]{:S(2)}, u32[]{:S(2)}) collective-permute-start(bf16[1024,256]{1,0:T(8,128)(2,1)} %get-tuple-element.122.grad_ref), channel_id=1, source_target_pairs={{0,1},{1,2},{2,3},{4,5},{5,6},{6,7},{8,9},{9,10},{10,11},{12,13},{... | collective-permute-start | bytes 1572872 | tf_op jit(solution)/shard_map/ppermute | solution.py:780
  282.7 30.3 %collective-permute-start.18 = (bf16[2304,512]{1,0:T(8,128)(2,1)S(1)}, bf16[2304,512]{1,0:T(8,128)(2,1)S(1)}, u32[]{:S(2)}, u32[]{:S(2)}) collective-permute-start(bf16[2304,512]{1,0:T(8,128)(2,1)S(1)} %constant_dynamic-slice_fusion.28), channel_id=1, source_target_pairs={{0,4},{4,0},{8,12},{12,8},{16,20},{20,16},{24,28},{28,24},{1,5},{5... | collective-permute-start | bytes 7077896 | tf_op jit(solution)/shard_map/ppermute | solution.py:793
  286.9 25.7 %collective-permute-start.21 = (bf16[1024,512]{1,0:T(8,128)(2,1)S(1)}, bf16[1024,512]{1,0:T(8,128)(2,1)S(1)}, u32[]{:S(2)}, u32[]{:S(2)}) collective-permute-start(bf16[1024,512]{1,0:T(8,128)(2,1)S(1)} %constant_dynamic-slice_fusion.25), channel_id=1, source_target_pairs={{0,4},{4,0},{8,12},{12,8},{16,20},{20,16},{24,28},{28,24},{1,5},{5... | collective-permute-start | bytes 3145736 | tf_op jit(solution)/shard_map/ppermute | solution.py:793
  289.6 16.8 %collective-permute-start.26 = (bf16[1024,256]{1,0:T(8,128)(2,1)S(1)}, bf16[1024,256]{1,0:T(8,128)(2,1)S(1)}, u32[]{:S(2)}, u32[]{:S(2)}) collective-permute-start(bf16[1024,256]{1,0:T(8,128)(2,1)S(1)} %collective-permute-done.25.refs_7_), channel_id=1, source_target_pairs={{1,0},{2,1},{3,2},{5,4},{6,5},{7,6},{9,8},{10,9},{11,10},{13,12},{... | collective-permute-start | bytes 1572872 | tf_op jit(solution)/shard_map/ppermute | solution.py:780
  291.5 16.3 %collective-permute-start.28 = (bf16[1024,256]{1,0:T(8,128)(2,1)S(1)}, bf16[1024,256]{1,0:T(8,128)(2,1)S(1)}, u32[]{:S(2)}, u32[]{:S(2)}) collective-permute-start(bf16[1024,256]{1,0:T(8,128)(2,1)S(1)} %collective-permute-done.24.refs_4_), channel_id=1, source_target_pairs={{0,1},{1,2},{2,3},{4,5},{5,6},{6,7},{8,9},{9,10},{10,11},{12,13},{... | collective-permute-start | bytes 1572872 | tf_op jit(solution)/shard_map/ppermute | solution.py:780
  306.5 70.9 %collective-permute-start.27 = (bf16[1024,256]{1,0:T(8,128)(2,1)S(1)}, bf16[1024,256]{1,0:T(8,128)(2,1)S(1)}, u32[]{:S(2)}, u32[]{:S(2)}) collective-permute-start(bf16[1024,256]{1,0:T(8,128)(2,1)S(1)} %collective-permute-done.26.refs_4_), channel_id=1, source_target_pairs={{1,0},{2,1},{3,2},{5,4},{6,5},{7,6},{9,8},{10,9},{11,10},{13,12},{... | collective-permute-start | bytes 1572872 | tf_op jit(solution)/shard_map/ppermute | solution.py:780
  307.8 69.6 %collective-permute-start.29 = (bf16[1024,256]{1,0:T(8,128)(2,1)S(1)}, bf16[1024,256]{1,0:T(8,128)(2,1)S(1)}, u32[]{:S(2)}, u32[]{:S(2)}) collective-permute-start(bf16[1024,256]{1,0:T(8,128)(2,1)S(1)} %collective-permute-done.28.refs_3_), channel_id=1, source_target_pairs={{0,1},{1,2},{2,3},{4,5},{5,6},{6,7},{8,9},{9,10},{10,11},{12,13},{... | collective-permute-start | bytes 1572872 | tf_op jit(solution)/shard_map/ppermute | solution.py:780
  316.1 22.4 %collective-permute-start.22 = (bf16[768,512]{1,0:T(8,128)(2,1)}, bf16[768,512]{1,0:T(8,128)(2,1)}, u32[]{:S(2)}, u32[]{:S(2)}) collective-permute-start(bf16[768,512]{1,0:T(8,128)(2,1)} %constant_dynamic-slice_fusion.24), channel_id=1, source_target_pairs={{0,16},{4,20},{8,24},{12,28},{16,0},{20,4},{24,8},{28,12},{1,17},{... | collective-permute-start | bytes 2359304 | tf_op jit(solution)/shard_map/ppermute | solution.py:793
  322.6 23.4 %collective-permute-start.19 = (bf16[896,512]{1,0:T(8,128)(2,1)}, bf16[896,512]{1,0:T(8,128)(2,1)S(1)}, u32[]{:S(2)}, u32[]{:S(2)}) collective-permute-start(bf16[896,512]{1,0:T(8,128)(2,1)} %constant_dynamic-slice_fusion.27), channel_id=1, source_target_pairs={{0,8},{4,12},{8,0},{12,4},{16,24},{20,28},{24,16},{28,20},{1,9},{5... | collective-permute-start | bytes 2752520 | tf_op jit(solution)/shard_map/ppermute | solution.py:793
  340.3 11.8 %collective-permute-start.23 = (bf16[384,512]{1,0:T(8,128)(2,1)S(1)}, bf16[384,512]{1,0:T(8,128)(2,1)S(1)}, u32[]{:S(2)}, u32[]{:S(2)}) collective-permute-start(bf16[384,512]{1,0:T(8,128)(2,1)S(1)} %constant_dynamic-slice_fusion.23), channel_id=1, source_target_pairs={{0,8},{4,12},{8,0},{12,4},{16,24},{20,28},{24,16},{28,20},{1,9},{5... | collective-permute-start | bytes 1179656 | tf_op jit(solution)/shard_map/ppermute | solution.py:793
  346.3 8.5 %collective-permute-start.20 = (bf16[448,512]{1,0:T(8,128)(2,1)S(1)}, bf16[448,512]{1,0:T(8,128)(2,1)S(1)}, u32[]{:S(2)}, u32[]{:S(2)}) collective-permute-start(bf16[448,512]{1,0:T(8,128)(2,1)S(1)} %constant_dynamic-slice_fusion.26), channel_id=1, source_target_pairs={{0,16},{4,20},{8,24},{12,28},{16,0},{20,4},{24,8},{28,12},{1,17},{... | collective-permute-start | bytes 1376264 | tf_op jit(solution)/shard_map/ppermute | solution.py:793
  346.5 9.9 %collective-permute-start.52 = (bf16[256,512]{1,0:T(8,128)(2,1)S(1)}, bf16[256,512]{1,0:T(8,128)(2,1)S(1)}, u32[]{:S(2)}, u32[]{:S(2)}) collective-permute-start(bf16[256,512]{1,0:T(8,128)(2,1)S(1)} %constant_dynamic-slice_fusion.8), channel_id=1, source_target_pairs={{0,4},{4,0},{8,12},{12,8},{16,20},{20,16},{24,28},{28,24},{1,5},{5... | collective-permute-start | bytes 786440 | tf_op jit(solution)/shard_map/ppermute | solution.py:793
  355.1 10.5 %collective-permute-start.40 = (bf16[416,512]{1,0:T(8,128)(2,1)S(1)}, bf16[416,512]{1,0:T(8,128)(2,1)S(1)}, u32[]{:S(2)}, u32[]{:S(2)}) collective-permute-start(bf16[416,512]{1,0:T(8,128)(2,1)S(1)} %pad_maximum_fusion.7), channel_id=1, source_target_pairs={{0,1},{1,0},{2,3},{3,2},{4,5},{5,4},{6,7},{7,6},{8,9},{9,8},{10,11... | collective-permute-start | bytes 1277960 | tf_op jit(solution)/shard_map/ppermute | solution.py:793
  356.3 29.8 %collective-permute-start.49 = (bf16[2304,512]{1,0:T(8,128)(2,1)S(1)}, bf16[2304,512]{1,0:T(8,128)(2,1)S(1)}, u32[]{:S(2)}, u32[]{:S(2)}) collective-permute-start(bf16[2304,512]{1,0:T(8,128)(2,1)S(1)} %constant_dynamic-slice_fusion.13), channel_id=1, source_target_pairs={{0,4},{4,0},{8,12},{12,8},{16,20},{20,16},{24,28},{28,24},{1,5},{5... | collective-permute-start | bytes 7077896 | tf_op jit(solution)/shard_map/ppermute | solution.py:793
  365.8 11.4 %collective-permute-start.41 = (bf16[208,512]{1,0:T(8,128)(2,1)S(1)}, bf16[208,512]{1,0:T(8,128)(2,1)S(1)}, u32[]{:S(2)}, u32[]{:S(2)}) collective-permute-start(bf16[208,512]{1,0:T(8,128)(2,1)S(1)} %pad_maximum_fusion.14), channel_id=1, source_target_pairs={{0,2},{1,3},{2,0},{3,1},{4,6},{5,7},{6,4},{7,5},{8,10},{9,11},{10,... | collective-permute-start | bytes 638984 | tf_op jit(solution)/shard_map/ppermute | solution.py:793
  377.3 8.1 %collective-permute-start.42 = (bf16[208,512]{1,0:T(8,128)(2,1)S(1)}, bf16[208,512]{1,0:T(8,128)(2,1)S(1)}, u32[]{:S(2)}, u32[]{:S(2)}) collective-permute-start(bf16[208,512]{1,0:T(8,128)(2,1)S(1)} %pad_maximum_fusion.15), channel_id=1, source_target_pairs={{0,2},{1,3},{2,0},{3,1},{4,6},{5,7},{6,4},{7,5},{8,10},{9,11},{10,... | collective-permute-start | bytes 638984 | tf_op jit(solution)/shard_map/ppermute | solution.py:793
  383.4 4.4 collective-permute-start.30
  385.5 30.8 %collective-permute-start.43 = (bf16[416,512]{1,0:T(8,128)(2,1)S(1)}, bf16[416,512]{1,0:T(8,128)(2,1)S(1)}, u32[]{:S(2)}, u32[]{:S(2)}) collective-permute-start(bf16[416,512]{1,0:T(8,128)(2,1)S(1)} %pad_maximum_fusion.8), channel_id=1, source_target_pairs={{0,1},{1,0},{2,3},{3,2},{4,5},{5,4},{6,7},{7,6},{8,9},{9,8},{10,11... | collective-permute-start | bytes 1277960 | tf_op jit(solution)/shard_map/ppermute | solution.py:793
  387.0 16.9 %collective-permute-start.50 = (bf16[640,512]{1,0:T(8,128)(2,1)S(1)}, bf16[640,512]{1,0:T(8,128)(2,1)S(1)}, u32[]{:S(2)}, u32[]{:S(2)}) collective-permute-start(bf16[640,512]{1,0:T(8,128)(2,1)S(1)} %constant_dynamic-slice_fusion.12), channel_id=1, source_target_pairs={{0,8},{4,12},{8,0},{12,4},{16,24},{20,28},{24,16},{28,20},{1,9},{5... | collective-permute-start | bytes 1966088 | tf_op jit(solution)/shard_map/ppermute | solution.py:793
  387.7 16.7 %collective-permute-start.53 = (bf16[640,512]{1,0:T(8,128)(2,1)S(1)}, bf16[640,512]{1,0:T(8,128)(2,1)S(1)}, u32[]{:S(2)}, u32[]{:S(2)}) collective-permute-start(bf16[640,512]{1,0:T(8,128)(2,1)S(1)} %pad_maximum_fusion.5), channel_id=1, source_target_pairs={{0,16},{4,20},{8,24},{12,28},{16,0},{20,4},{24,8},{28,12},{1,17},{... | collective-permute-start | bytes 1966088 | tf_op jit(solution)/shard_map/ppermute | solution.py:793
  404.2 9.1 %collective-permute-start.51 = (bf16[320,512]{1,0:T(8,128)(2,1)S(1)}, bf16[320,512]{1,0:T(8,128)(2,1)S(1)}, u32[]{:S(2)}, u32[]{:S(2)}) collective-permute-start(bf16[320,512]{1,0:T(8,128)(2,1)S(1)} %constant_dynamic-slice_fusion.11), channel_id=1, source_target_pairs={{0,16},{4,20},{8,24},{12,28},{16,0},{20,4},{24,8},{28,12},{1,17},{... | collective-permute-start | bytes 983048 | tf_op jit(solution)/shard_map/ppermute | solution.py:793
  404.7 8.9 %collective-permute-start.54 = (bf16[320,512]{1,0:T(8,128)(2,1)S(1)}, bf16[320,512]{1,0:T(8,128)(2,1)S(1)}, u32[]{:S(2)}, u32[]{:S(2)}) collective-permute-start(bf16[320,512]{1,0:T(8,128)(2,1)S(1)} %pad_maximum_fusion.11), channel_id=1, source_target_pairs={{0,8},{4,12},{8,0},{12,4},{16,24},{20,28},{24,16},{28,20},{1,9},{5... | collective-permute-start | bytes 983048 | tf_op jit(solution)/shard_map/ppermute | solution.py:793
  413.8 8.0 %collective-permute-start.55 = (bf16[320,512]{1,0:T(8,128)(2,1)S(1)}, bf16[320,512]{1,0:T(8,128)(2,1)S(1)}, u32[]{:S(2)}, u32[]{:S(2)}) collective-permute-start(bf16[320,512]{1,0:T(8,128)(2,1)S(1)} %pad_maximum_fusion.12), channel_id=1, source_target_pairs={{0,1},{1,0},{2,3},{3,2},{4,5},{5,4},{6,7},{7,6},{8,9},{9,8},{10,11... | collective-permute-start | bytes 983048 | tf_op jit(solution)/shard_map/ppermute | solution.py:793
  414.0 19.3 %collective-permute-start.31 = (bf16[256,512]{1,0:T(8,128)(2,1)S(1)}, bf16[256,512]{1,0:T(8,128)(2,1)S(1)}, u32[]{:S(2)}, u32[]{:S(2)}) collective-permute-start(bf16[256,512]{1,0:T(8,128)(2,1)S(1)} %constant_dynamic-slice_fusion.21), channel_id=1, source_target_pairs={{0,8},{4,12},{8,0},{12,4},{16,24},{20,28},{24,16},{28,20},{1,9},{5... | collective-permute-start | bytes 786440 | tf_op jit(solution)/shard_map/ppermute | solution.py:793
  415.3 62.9 %collective-permute-start.35 = (bf16[256,512]{1,0:T(8,128)(2,1)S(1)}, bf16[256,512]{1,0:T(8,128)(2,1)S(1)}, u32[]{:S(2)}, u32[]{:S(2)}) collective-permute-start(bf16[256,512]{1,0:T(8,128)(2,1)S(1)} %constant_dynamic-slice_fusion.19), channel_id=1, source_target_pairs={{0,16},{4,20},{8,24},{12,28},{16,0},{20,4},{24,8},{28,12},{1,17},{... | collective-permute-start | bytes 786440 | tf_op jit(solution)/shard_map/ppermute | solution.py:793
  416.5 12.5 %collective-permute-start.46 = (bf16[384,512]{1,0:T(8,128)(2,1)S(1)}, bf16[384,512]{1,0:T(8,128)(2,1)S(1)}, u32[]{:S(2)}, u32[]{:S(2)}) collective-permute-start(bf16[384,512]{1,0:T(8,128)(2,1)S(1)} %maximum_select_fusion.11), channel_id=1, source_target_pairs={{0,8},{4,12},{8,0},{12,4},{16,24},{20,28},{24,16},{28,20},{1,9},{5... | collective-permute-start | bytes 1179656 | tf_op jit(solution)/shard_map/ppermute | solution.py:793
  422.0 8.9 %collective-permute-start.56 = (bf16[160,512]{1,0:T(8,128)(2,1)S(1)}, bf16[160,512]{1,0:T(8,128)(2,1)S(1)}, u32[]{:S(2)}, u32[]{:S(2)}) collective-permute-start(bf16[160,512]{1,0:T(8,128)(2,1)S(1)} %pad_maximum_fusion.18), channel_id=1, source_target_pairs={{0,2},{1,3},{2,0},{3,1},{4,6},{5,7},{6,4},{7,5},{8,10},{9,11},{10,... | collective-permute-start | bytes 491528 | tf_op jit(solution)/shard_map/ppermute | solution.py:793
  424.0 13.5 %collective-permute-start.44 = (bf16[448,512]{1,0:T(8,128)(2,1)S(1)}, bf16[448,512]{1,0:T(8,128)(2,1)S(1)}, u32[]{:S(2)}, u32[]{:S(2)}) collective-permute-start(bf16[448,512]{1,0:T(8,128)(2,1)S(1)} %maximum_select_fusion.10), channel_id=1, source_target_pairs={{0,16},{4,20},{8,24},{12,28},{16,0},{20,4},{24,8},{28,12},{1,17},{... | collective-permute-start | bytes 1376264 | tf_op jit(solution)/shard_map/ppermute | solution.py:793
  429.3 23.4 %collective-permute-start.47 = (bf16[768,512]{1,0:T(8,128)(2,1)S(1)}, bf16[768,512]{1,0:T(8,128)(2,1)S(1)}, u32[]{:S(2)}, u32[]{:S(2)}) collective-permute-start(bf16[768,512]{1,0:T(8,128)(2,1)S(1)} %maximum_select_fusion.5), channel_id=1, source_target_pairs={{0,16},{4,20},{8,24},{12,28},{16,0},{20,4},{24,8},{28,12},{1,17},{... | collective-permute-start | bytes 2359304 | tf_op jit(solution)/shard_map/ppermute | solution.py:793
  431.0 8.0 %collective-permute-start.57 = (bf16[160,512]{1,0:T(8,128)(2,1)S(1)}, bf16[160,512]{1,0:T(8,128)(2,1)S(1)}, u32[]{:S(2)}, u32[]{:S(2)}) collective-permute-start(bf16[160,512]{1,0:T(8,128)(2,1)S(1)} %fusion.5), channel_id=1, source_target_pairs={{0,2},{1,3},{2,0},{3,1},{4,6},{5,7},{6,4},{7,5},{8,10},{9,11},{10,... | collective-permute-start | bytes 491528 | tf_op jit(solution)/shard_map/ppermute | solution.py:793
  438.0 17.3 %collective-permute-start.45 = (bf16[896,512]{1,0:T(8,128)(2,1)S(1)}, bf16[896,512]{1,0:T(8,128)(2,1)S(1)}, u32[]{:S(2)}, u32[]{:S(2)}) collective-permute-start(bf16[896,512]{1,0:T(8,128)(2,1)S(1)} %maximum_select_fusion.4), channel_id=1, source_target_pairs={{0,8},{4,12},{8,0},{12,4},{16,24},{20,28},{24,16},{28,20},{1,9},{5... | collective-permute-start | bytes 2752520 | tf_op jit(solution)/shard_map/ppermute | solution.py:793
  439.2 14.2 %collective-permute-start.58 = (bf16[320,512]{1,0:T(8,128)(2,1)S(1)}, bf16[320,512]{1,0:T(8,128)(2,1)S(1)}, u32[]{:S(2)}, u32[]{:S(2)}) collective-permute-start(bf16[320,512]{1,0:T(8,128)(2,1)S(1)} %fusion.3), channel_id=1, source_target_pairs={{0,1},{1,0},{2,3},{3,2},{4,5},{5,4},{6,7},{7,6},{8,9},{9,8},{10,11... | collective-permute-start | bytes 983048 | tf_op jit(solution)/shard_map/ppermute | solution.py:793
  440.5 38.5 %collective-permute-start.32 = (bf16[128,512]{1,0:T(8,128)(2,1)S(1)}, bf16[128,512]{1,0:T(8,128)(2,1)S(1)}, u32[]{:S(2)}, u32[]{:S(2)}) collective-permute-start(bf16[128,512]{1,0:T(8,128)(2,1)S(1)} %constant_dynamic-slice_fusion.20), channel_id=1, source_target_pairs={{0,16},{4,20},{8,24},{12,28},{16,0},{20,4},{24,8},{28,12},{1,17},{... | collective-permute-start | bytes 393224 | tf_op jit(solution)/shard_map/ppermute | solution.py:793
  453.5 7.1 %collective-permute-start.61 = (bf16[320,512]{1,0:T(8,128)(2,1)S(1)}, bf16[320,512]{1,0:T(8,128)(2,1)S(1)}, u32[]{:S(2)}, u32[]{:S(2)}) collective-permute-start(bf16[320,512]{1,0:T(8,128)(2,1)S(1)} %pad_maximum_fusion.13), channel_id=1, source_target_pairs={{0,8},{4,12},{8,0},{12,4},{16,24},{20,28},{24,16},{28,20},{1,9},{5... | collective-permute-start | bytes 983048 | tf_op jit(solution)/shard_map/ppermute | solution.py:793
  455.9 10.6 %collective-permute-start.59 = (bf16[320,512]{1,0:T(8,128)(2,1)S(1)}, bf16[320,512]{1,0:T(8,128)(2,1)S(1)}, u32[]{:S(2)}, u32[]{:S(2)}) collective-permute-start(bf16[320,512]{1,0:T(8,128)(2,1)S(1)} %fusion.2), channel_id=1, source_target_pairs={{0,16},{4,20},{8,24},{12,28},{16,0},{20,4},{24,8},{28,12},{1,17},{... | collective-permute-start | bytes 983048 | tf_op jit(solution)/shard_map/ppermute | solution.py:793
  461.0 15.8 %collective-permute-start.62 = (bf16[640,512]{1,0:T(8,128)(2,1)S(1)}, bf16[640,512]{1,0:T(8,128)(2,1)S(1)}, u32[]{:S(2)}, u32[]{:S(2)}) collective-permute-start(bf16[640,512]{1,0:T(8,128)(2,1)S(1)} %pad_maximum_fusion.6), channel_id=1, source_target_pairs={{0,16},{4,20},{8,24},{12,28},{16,0},{20,4},{24,8},{28,12},{1,17},{... | collective-permute-start | bytes 1966088 | tf_op jit(solution)/shard_map/ppermute | solution.py:793
  466.8 10.7 %collective-permute-start.60 = (bf16[640,512]{1,0:T(8,128)(2,1)S(1)}, bf16[640,512]{1,0:T(8,128)(2,1)S(1)}, u32[]{:S(2)}, u32[]{:S(2)}) collective-permute-start(bf16[640,512]{1,0:T(8,128)(2,1)S(1)} %maximum_select_fusion.6), channel_id=1, source_target_pairs={{0,8},{4,12},{8,0},{12,4},{16,24},{20,28},{24,16},{28,20},{1,9},{5... | collective-permute-start | bytes 1966088 | tf_op jit(solution)/shard_map/ppermute | solution.py:793
  467.6 38.1 %collective-permute-start.48 = (bf16[3328,512]{1,0:T(8,128)(2,1)S(1)}, bf16[3328,512]{1,0:T(8,128)(2,1)}, u32[]{:S(2)}, u32[]{:S(2)}) collective-permute-start(bf16[3328,512]{1,0:T(8,128)(2,1)S(1)} %pad_maximum_fusion.1.refs_1_), channel_id=1, source_target_pairs={{0,4},{4,0},{8,12},{12,8},{16,20},{20,16},{24,28},{28,24},{1,5},{5... | collective-permute-start | bytes 10223624 | tf_op jit(solution)/shard_map/ppermute | solution.py:793
  478.1 34.6 %collective-permute-start.63 = (bf16[2560,512]{1,0:T(8,128)(2,1)S(1)}, bf16[2560,512]{1,0:T(8,128)(2,1)}, u32[]{:S(2)}, u32[]{:S(2)}) collective-permute-start(bf16[2560,512]{1,0:T(8,128)(2,1)S(1)} %pad_maximum_fusion.2.refs_3_), channel_id=1, source_target_pairs={{0,4},{4,0},{8,12},{12,8},{16,20},{20,16},{24,28},{28,24},{1,5},{5... | collective-permute-start | bytes 7864328 | tf_op jit(solution)/shard_map/ppermute | solution.py:793
  478.3 6.0 %collective-permute-start.36 = (bf16[128,512]{1,0:T(8,128)(2,1)S(1)}, bf16[128,512]{1,0:T(8,128)(2,1)S(1)}, u32[]{:S(2)}, u32[]{:S(2)}) collective-permute-start(bf16[128,512]{1,0:T(8,128)(2,1)S(1)} %constant_dynamic-slice_fusion.18), channel_id=1, source_target_pairs={{0,8},{4,12},{8,0},{12,4},{16,24},{20,28},{24,16},{28,20},{1,9},{5... | collective-permute-start | bytes 393224 | tf_op jit(solution)/shard_map/ppermute | solution.py:793
  479.0 6.0 %collective-permute-start.33 = (bf16[128,512]{1,0:T(8,128)(2,1)S(1)}, bf16[128,512]{1,0:T(8,128)(2,1)S(1)}, u32[]{:S(2)}, u32[]{:S(2)}) collective-permute-start(bf16[128,512]{1,0:T(8,128)(2,1)S(1)} %add_convert_fusion.21), channel_id=1, source_target_pairs={{0,16},{4,20},{8,24},{12,28},{16,0},{20,4},{24,8},{28,12},{1,17},{... | collective-permute-start | bytes 393224 | tf_op jit(solution)/shard_map/ppermute | solution.py:793
  484.3 6.5 %collective-permute-start.37 = (bf16[128,512]{1,0:T(8,128)(2,1)S(1)}, bf16[128,512]{1,0:T(8,128)(2,1)S(1)}, u32[]{:S(2)}, u32[]{:S(2)}) collective-permute-start(bf16[128,512]{1,0:T(8,128)(2,1)S(1)} %add_convert_fusion.20), channel_id=1, source_target_pairs={{0,8},{4,12},{8,0},{12,4},{16,24},{20,28},{24,16},{28,20},{1,9},{5... | collective-permute-start | bytes 393224 | tf_op jit(solution)/shard_map/ppermute | solution.py:793
  485.0 10.1 %collective-permute-start.34 = (bf16[256,512]{1,0:T(8,128)(2,1)S(1)}, bf16[256,512]{1,0:T(8,128)(2,1)S(1)}, u32[]{:S(2)}, u32[]{:S(2)}) collective-permute-start(bf16[256,512]{1,0:T(8,128)(2,1)S(1)} %maximum_select_fusion.12), channel_id=1, source_target_pairs={{0,8},{4,12},{8,0},{12,4},{16,24},{20,28},{24,16},{28,20},{1,9},{5... | collective-permute-start | bytes 786440 | tf_op jit(solution)/shard_map/ppermute | solution.py:793
  490.8 6.4 %collective-permute-start.38 = (bf16[256,512]{1,0:T(8,128)(2,1)S(1)}, bf16[256,512]{1,0:T(8,128)(2,1)S(1)}, u32[]{:S(2)}, u32[]{:S(2)}) collective-permute-start(bf16[256,512]{1,0:T(8,128)(2,1)S(1)} %maximum_select_fusion.13), channel_id=1, source_target_pairs={{0,16},{4,20},{8,24},{12,28},{16,0},{20,4},{24,8},{28,12},{1,17},{... | collective-permute-start | bytes 786440 | tf_op jit(solution)/shard_map/ppermute | solution.py:793
  498.6 2.7 collective-permute-start.39
  (41 other events, 268.6 us)

commit v2 on v1

--- a/solution.py
+++ b/solution.py
@@ -558,7 +558,6 @@
     x_ref, stat_ref, s_ref, gain_ref, amat_ref, mask_ref, ints_ref, w_hbm = refs[:8]
     y_ref, ystat_ref, ygain_ref, ybias_ref = refs[8:12]
     refs = refs[12:]
-    refs = refs[1:]
     if first:
         mid_out_ref, refs = refs[0], refs[1:]
     err_ref, v_ref, so_ref, vec_ref, msgp_ref, msgn_ref = refs[:6]
@@ -649,13 +648,12 @@
     ins = [HB] + [VM] * len(heads) + [VM] * 6 + [SM, HB] + [VM] * 4
     msg = sds((HALO + 8 if first else 8, chans), f32)
     rows = sds((pixels, chans), f32)
-    outs = [sds(token.shape, token.dtype)] + ([rows] if first else [])
+    outs = [rows] if first else []
     outs += [sds((pixels, chans), bf16), rows, sds((2 * nb, chans), f32), sds((8, chans), f32), msg, msg]
     scratch = conv_scratch(pixels, chans, nb, (chans, 9 * chans)) + [pltpu.SemaphoreType.DMA((9,))]
     flops = 18 * pixels * chans * chans
     return call(
-        functools.partial(conv_backward_kernel, nb, first), ins, [(outs[0], HB)] + [(o, VM) for o in outs[1:]], scratch,
-        operands, flops, aliases={0: 0},
+        functools.partial(conv_backward_kernel, nb, first), ins, [(o, VM) for o in outs], scratch, operands, flops
     )
 
 
@@ -775,6 +773,15 @@
     return out
 
 
+def gate_kernel(*refs):
+    pass
+
+
+def gate(passed, *tokens):
+    outs = [(sds(passed.shape, passed.dtype), HB)]
+    return call(gate_kernel, [HB] * (1 + len(tokens)), outs, [], (passed, *tokens), 0, aliases={0: 0}, light=True)[0]
+
+
 def along(array, axis, by):
     count = lax.axis_size(axis)
     return lax.ppermute(array, axis, [(i, i + by) for i in range(count) if 0 <= i + by < count])
@@ -862,9 +869,16 @@
     return lax.dynamic_slice_in_dim(x, which * (x.shape[0] // 2), x.shape[0] // 2)
 
 
+def core_send(x):
+    return partner(half_of(x, 1 - lax.axis_index("rows") % 2), "rows", 1)
+
+
+def core_half(x):
+    return half_of(x, lax.axis_index("rows") % 2)
+
+
 def core_swap(x):
-    up = lax.axis_index("rows") % 2
-    return half_of(x, up), partner(half_of(x, 1 - up), "rows", 1)
+    return core_half(x), core_send(x)
 
 
 def per_device(
@@ -967,39 +981,40 @@
     g_b_proj = jnp.sum(cot.astype(f32), axis=0, keepdims=True)
     g_b_query = jnp.sum(d_query.astype(f32), axis=0, keepdims=True)
     g_b_value = jnp.sum(d_value.astype(f32), axis=0, keepdims=True)
-    g_attn, d_mid, err_two, v_two, s_two, vec_two, msg_p, msg_n = conv_backward(
+    d_mid, err_two, v_two, s_two, vec_two, msg_p, msg_n = conv_backward(
         True, g_attn, (u_own, to_p, to_n, p_back, n_back, p_three, n_three, cot),
         resid_mid, stat_three, s_three, row(gn3_gain), amat, mask, ints, conv2_w,
         hid_one, stat_two, row(gn2_gain), row(gn2_bias),
     )
     p_four, n_four = swap(msg_p, msg_n)
     g_conv2 = tn(patch_two, err_two)
-    g_conv2, err_one, v_one, s_one, vec_one, msg_p, msg_n = conv_backward(
+    two_got, attn_got = core_send(g_conv2), core_send(g_attn)
+    err_one, v_one, s_one, vec_one, msg_p, msg_n = conv_backward(
         False, g_conv2, (v_two, p_four, n_four, p_two, n_two),
         hid_one, stat_two, s_two, row(gn2_gain), amat, mask, ints, conv1_w,
         resid_in, stat_one, row(gn1_gain), row(gn1_bias),
     )
     p_five, n_five = swap(msg_p, msg_n)
-    err_one, g_conv2, g_attn, err_in, feature_grad, vec_in = tail(
-        (err_one, g_conv2, g_attn), v_one, p_five, n_five, s_one, resid_in, stat_one, row(gn1_gain), amat, d_mid, w_in
+    err_one, two_got, attn_got, err_in, feature_grad, vec_in = tail(
+        (err_one, two_got, attn_got), v_one, p_five, n_five, s_one, resid_in, stat_one, row(gn1_gain), amat, d_mid, w_in
     )
     below, above = [feature_grad], [feature_grad]
     for _ in range(1, groups):
         below.append(along(below[-1], "chan", 1))
         above.append(along(above[-1], "chan", -1))
-    two = jnp.concatenate([add(*core_swap(g_conv2)), add(*core_swap(g_attn))])
-    g_conv1 = tn(patch_one, err_one)
+    two = jnp.concatenate([add(core_half(g_conv2), two_got), add(core_half(g_attn), attn_got)])
+    g_conv1 = tn(patch_one, gate(err_one, two))
     vectors = (vec_in, vec_one, vec_two, vec_three, g_b_query, g_b_value, g_b_proj)
-    g_conv1, begun, small = own_part(g_conv1, two, row(local[0]), feature_grad, quant, err_in, vectors, codes)
-    one = add(*core_swap(g_conv1))
-    small = add(*core_swap(small))
     both = [plan(flip, "rows", "chan") for flip in (False, True)]
     plans = both + both + both[1:] + [plan(flip, "rows") for flip in (False, True)]
     begins = [0, 0, LATE_ROUND, LATE_ROUND, LATE_ROUND, BOOK_ROUND, BOOK_ROUND]
+    work = rounds(streams(two, "rows", "chan"), plans[:2], begins, range(1))
+    g_conv1, begun, small = own_part(g_conv1, work[0], row(local[0]), feature_grad, quant, err_in, vectors, codes)
+    one = add(*core_swap(g_conv1))
+    small = add(*core_swap(small))
     pair = lambda d: (row(local[groups - d]), (below[d], above[groups - d]))
     middle = [pair(d) for d in range(1, groups) if 2 * d == groups]
     outer = [pair(d) for d in range(1, groups) if 2 * d != groups]
-    work = rounds(streams(two, "rows", "chan"), plans[:2], begins, range(1))
     book = scatter(*zip(*middle), codes, f32, begun, work)
     work = rounds(work, plans[:2], begins, range(1, 2))
     book = scatter(*zip(*outer), codes, bf16, book, work)

time: 528 us -> 519 us (0.983)
  waiting for transfers between devices: 164 us -> 140 us
  starting transfers between devices: 133 us -> 146 us
    ppermute x40, starting transfers between devices: 33.8 us -> 52.4 us  [partner(): lax.ppermute(array, axis, [(i, i ^ bit) for i in range(lax.axis_size(axis...]
    ppermute x40, waiting for transfers between devices: 122 us -> 106 us  [partner(): lax.ppermute(array, axis, [(i, i ^ bit) for i in range(lax.axis_size(axis...]
    ppermute x18, waiting for transfers between devices: 13.9 us -> 5.79 us  [along(): lax.ppermute(array, axis, [(i, i + by) for i in range(count) if 0 <= i +...]
    unnamed x82 -> x94, local copies, waits for them, and re-layouts: 15.2 us -> 18.1 us
    pallas_call x11 -> x12, Pallas kernels: 119 us -> 119 us  [call(): pl.pallas_call(body, out_shape=[o[0] for o in outs], in_specs=ins, out_sp...]
  transfers between devices with their start and end apart: 64 -> 64, of which waited for: 31 -> 28; matrix products, arithmetic and copies ran while one was open for 12% -> 10% of each run, Pallas kernels for 7% -> 10%
where the time goes in v2:
time: 519 us; the launch traced here: 512 us
  starting transfers between devices  146 us (28%)
  Pallas kernels  141 us (27%)
  waiting for transfers between devices  140 us (27%)
  local copies, waits for them, and re-layouts  29.7 us (6%)
  matrix products  25.8 us (5%)
  other arithmetic  25.7 us (5%)
    pallas_call x12, Pallas kernels, call(): pl.pallas_call(body, out_shape=[o[0] for o in outs], in_specs=ins, out_sp...  119 us
    ppermute x40, waiting for transfers between devices, partner(): lax.ppermute(array, axis, [(i, i ^ bit) for i in range(lax.axis_size(axis...  106 us
    ppermute x18, starting transfers between devices, along(): lax.ppermute(array, axis, [(i, i + by) for i in range(count) if 0 <= i +...  82.7 us
    ppermute x40, starting transfers between devices, partner(): lax.ppermute(array, axis, [(i, i ^ bit) for i in range(lax.axis_size(axis...  52.4 us
    ppermute x6, waiting for transfers between devices, around(): lax.ppermute(array, axis, [(i, (i + by) % count) for i in range(count)])  28 us
    dot_general x6, matrix products, per_device(): jnp.einsum('nk,nc->kc', a, b, preferred_element_type=f32).astype(bf16)  25.8 us
    unnamed x94, local copies, waits for them, and re-layouts  18.1 us
    pallas_call x4, Pallas kernels, lookup(): pl.pallas_call(functools.partial(lookup_kernel, len(tokens)), grid=(pixel...  12.2 us
  transfers between devices with their start and end apart: 64, of which 28 were waited for; matrix products, arithmetic and copies ran while one was open for 10% of the time, Pallas kernels for 10%

profile of v2, /device:TPU:0, one launch (start us, length us, event | category | flops | bytes accessed | tf_op | source)
XLA Modules:
  0.0 512.3 jit_solution(3236481625397123154)
XLA Ops:
  0.7 4.1 collective-permute-start.1
  14.5 3.0 shard_map.410.refs_2_
  17.5 3.0 shard_map.408.refs_0_
  22.4 3.0 shard_map.409.refs_1_
  26.6 2.7 collective-permute-start.3
  31.1 3.0 shard_map.411.refs_1_
  35.0 28.0 %collective-permute-done.4.refs_3_ = bf16[1024,256]{1,0:T(8,128)(2,1)S(1)} collective-permute-done((bf16[1024,256]{1,0:T(8,128)(2,1)S(1)}, bf16[1024,256]{1,0:T(8,128)(2,1)S(1)}, u32[]{:S(2)}, u32[]{:S(2)}) %collective-permute-start.4) | collective-permute-done | bytes 524320 | tf_op jit(solution)/shard_map/ppermute | solution.py:792
  64.1 4.1 shard_map.412
  75.3 14.3 %shard_map.413 = (f32[1024,512]{1,0:T(8,128)}, f32[32,512]{1,0:T(8,128)}, f32[32,512]{1,0:T(8,128)}, f32[72,512]{1,0:T(8,128)}, f32[72,512]{1,0:T(8,128)}, /*index=5*/bf16[1024,4608]{1,0:T(8,128)(2,1)}) custom-call(f32[1024,512]{1,0:T(8,128)} %get-tuple-element.81.refs_0_.refs_11_.refs_14_.refs_7_, f32[72,512]{1,0:T(8,128)} %copy-done.38, ...), custom_call_target="tpu_custom_call" | custom-call | flops 4831838208 | bytes 19180928 | tf_op jit(solution)/shard_map/pallas_call | solution.py:34
  89.7 5.6 %collective-permute-start.8 = (f32[72,512]{1,0:T(8,128)}, f32[72,512]{1,0:T(8,128)S(1)}, u32[]{:S(2)}, u32[]{:S(2)}) collective-permute-start(f32[72,512]{1,0:T(8,128)} %get-tuple-element.86), channel_id=1, source_target_pairs={{0,4},{4,8},{8,12},{12,16},{16,20},{20,24},{24,28},{1,5},{5,9},{9,... | collective-permute-start | bytes 442376 | tf_op jit(solution)/shard_map/ppermute | solution.py:787
  95.3 1.8 collective-permute-start.9
  99.4 16.0 %shard_map.414 = (f32[1024,512]{1,0:T(8,128)}, f32[32,512]{1,0:T(8,128)}, f32[32,512]{1,0:T(8,128)}, bf16[1104,512]{1,0:T(8,128)(2,1)}, bf16[1104,512]{1,0:T(8,128)(2,1)}, /*index=5*/bf16[1024,4608]{1,0:T(8,128)(2,1)}) custom-call(f32[1024,512]{1,0:T(8,128)} %get-tuple-element.85.refs_0_.refs_17_.refs_6_, f32[72,512]{1,0:T(8,128)} %copy-done.34, ...), custom_call_target="tpu_custom_call" | custom-call | flops 4831838208 | bytes 24292736 | tf_op jit(solution)/shard_map/pallas_call | solution.py:34
  115.5 5.9 %collective-permute-start.10 = (bf16[1104,512]{1,0:T(8,128)(2,1)}, bf16[1104,512]{1,0:T(8,128)(2,1)S(1)}, u32[]{:S(2)}, u32[]{:S(2)}) collective-permute-start(bf16[1104,512]{1,0:T(8,128)(2,1)} %get-tuple-element.90), channel_id=1, source_target_pairs={{0,4},{4,8},{8,12},{12,16},{16,20},{20,24},{24,28},{1,5},{5,9},{9,... | collective-permute-start | bytes 3391496 | tf_op jit(solution)/shard_map/ppermute | solution.py:787
  127.3 25.5 %shard_map.415 = (bf16[3072,512]{1,0:T(8,128)(2,1)}, bf16[3072,512]{1,0:T(8,128)(2,1)}, bf16[3072,512]{1,0:T(8,128)(2,1)}, bf16[1024,512]{1,0:T(8,128)(2,1)}, bf...) custom-call(f32[1024,512]{1,0:T(8,128)} %get-tuple-element.89.refs_0, ...), custom_call_target="tpu_custom_call" | custom-call | flops 12884901888 | bytes 24669728 | tf_op jit(solution)/shard_map/pallas_call | solution.py:34
  154.1 26.4 %collective-permute-start.12 = (bf16[1104,512]{1,0:T(8,128)(2,1)}, bf16[1104,512]{1,0:T(8,128)(2,1)S(1)}, u32[]{:S(2)}, u32[]{:S(2)}) collective-permute-start(bf16[1104,512]{1,0:T(8,128)(2,1)} %get-tuple-element.102.refs_3_), channel_id=1, source_target_pairs={{0,4},{4,8},{8,12},{12,16},{16,20},{20,24},{24,28},{1,5},{5,9},{9,... | collective-permute-start | bytes 3391496 | tf_op jit(solution)/shard_map/ppermute | solution.py:787
  180.5 4.8 convolution_convert_fusion.2
  188.7 1.8 convolution_convert_fusion.3
  193.4 17.4 %shard_map.416 = (f32[1024,512]{1,0:T(8,128)}, bf16[1024,512]{1,0:T(8,128)(2,1)}, f32[1024,512]{1,0:T(8,128)}, f32[32,512]{1,0:T(8,128)}, f32[8,512]{1,0:T(8,128...) custom-call(bf16[2048,512]{1,0:T(8,128)(2,1)} %pad_maximum_fusion.3.refs_0_, f32[1024,512]{1,0:T(8,128)} %get-tuple-element.100.refs_1_, ...), custom_call_target="tpu_custom_call" | custom-call | flops 4831838208 | bytes 26799488 | tf_op jit(solution)/shard_map/pallas_call | solution.py:34
  210.8 8.4 %convolution_convert_fusion.1.refs_0_ = bf16[4608,512]{1,0:T(8,128)(2,1)S(1)} fusion(bf16[1024,4608]{1,0:T(8,128)(2,1)} %get-tuple-element.94, bf16[1024,512]{1,0:T(8,128)(2,1)} %get-tuple-element.106), kind=kOutput, calls=%fused_computation.1 | convolution fusion | flops 4834197504 | bytes 15204352 | tf_op jit(solution)/shard_map/nk,nc->kc/dot_general | solution.py:974
  220.8 1.8 copy-done.11
  222.7 13.6 %collective-permute-start.16 = (bf16[2304,512]{1,0:T(8,128)(2,1)}, bf16[2304,512]{1,0:T(8,128)(2,1)}, u32[]{:S(2)}, u32[]{:S(2)}) collective-permute-start(bf16[2304,512]{1,0:T(8,128)(2,1)} %constant_dynamic-slice_fusion.28), channel_id=1, source_target_pairs={{0,4},{4,0},{8,12},{12,8},{16,20},{20,16},{24,28},{28,24},{1,5},{5... | collective-permute-start | bytes 7077896 | tf_op jit(solution)/shard_map/ppermute | solution.py:800
  237.8 2.4 collective-permute-start.14
  244.1 14.8 %shard_map.417 = (bf16[1024,512]{1,0:T(8,128)(2,1)}, f32[1024,512]{1,0:T(8,128)}, f32[32,512]{1,0:T(8,128)}, f32[8,512]{1,0:T(8,128)}, f32[8,512]{1,0:T(8,128)}, /*index=5*/f32[8,512]{1,0:T(8,128)}) custom-call(bf16[4608,512]{1,0:T(8,128)(2,1)} %copy-done.11, f32[1024,512]{1,0:T(8,128)} %get-tuple-element.107.refs_1_, f32[72,512]{1,0:T(8,128)} %copy-done.40, ...), custom_call_target="tpu_custom_call" | custom-call | flops 4831838208 | bytes 19819904 | tf_op jit(solution)/shard_map/pallas_call | solution.py:34
  258.9 5.2 %collective-permute-start.18 = (f32[8,512]{1,0:T(8,128)}, f32[8,512]{1,0:T(8,128)S(1)}, u32[]{:S(2)}, u32[]{:S(2)}) collective-permute-start(f32[8,512]{1,0:T(8,128)} %get-tuple-element.114), channel_id=1, source_target_pairs={{0,4},{4,8},{8,12},{12,16},{16,20},{20,24},{24,28},{1,5},{5,9},{9,... | collective-permute-start | bytes 49160 | tf_op jit(solution)/shard_map/ppermute | solution.py:787
  268.0 4.9 shard_map.418
  274.2 13.6 %collective-permute-start.24 = (bf16[1024,256]{1,0:T(8,128)(2,1)}, bf16[1024,256]{1,0:T(8,128)(2,1)S(1)}, u32[]{:S(2)}, u32[]{:S(2)}) collective-permute-start(bf16[1024,256]{1,0:T(8,128)(2,1)} %get-tuple-element.118.grad_ref), channel_id=1, source_target_pairs={{0,1},{1,2},{2,3},{4,5},{5,6},{6,7},{8,9},{9,10},{10,11},{12,13},{... | collective-permute-start | bytes 1572872 | tf_op jit(solution)/shard_map/ppermute | solution.py:787
  287.9 3.0 add_convert_fusion.1
  292.9 2.0 pad_maximum_fusion.refs_1_
  295.0 3.6 collective-permute-start.22
  299.5 9.4 %convolution_convert_fusion.pass_ref = bf16[4608,512]{1,0:T(8,128)(2,1)} fusion(bf16[1024,4608]{1,0:T(8,128)(2,1)} %get-tuple-element.121, bf16[1024,512]{1,0:T(8,128)(2,1)} %shard_map.419), kind=kOutput, calls=%fused_computation | convolution fusion | flops 4834197504 | bytes 15204352 | tf_op jit(solution)/shard_map/nk,nc->kc/dot_general | solution.py:974
  310.3 4.8 collective-permute-start.28
  317.5 5.5 %collective-permute-done.20 = bf16[896,512]{1,0:T(8,128)(2,1)S(1)} collective-permute-done((bf16[896,512]{1,0:T(8,128)(2,1)}, bf16[896,512]{1,0:T(8,128)(2,1)S(1)}, u32[]{:S(2)}, u32[]{:S(2)}) %collective-permute-start.20) | collective-permute-done | bytes 917536 | tf_op jit(solution)/shard_map/ppermute | solution.py:800
  324.2 6.1 %shard_map.420 = (bf16[4608,512]{1,0:T(8,128)(2,1)}, f32[2048,512]{1,0:T(8,128)}, bf16[512,512]{1,0:T(8,128)(2,1)}) custom-call(bf16[4608,512]{1,0:T(8,128)(2,1)} %convolution_convert_fusion.pass_ref, bf16[896,512]{1,0:T(8,128)(2,1)} %copy-done, s32[1,1024]{1,0:T(1,128)} %broadcast_subtract_fusion.index_ref, ...), custom_call_target="tpu_custom_call", output_to_operand_aliasing={{0}: (0, {})} | custom-call | flops 2415919104 | bytes 17246208 | tf_op jit(solution)/shard_map/pallas_call | solution.py:34
  331.6 2.9 collective-permute-done.21
  334.7 2.3 collective-permute-start.40
  336.9 2.0 constant_dynamic-slice_fusion.13
  340.3 4.8 collective-permute-start.29
  345.1 3.7 shard_map.421.refs_8_
  349.1 2.1 collective-permute-start.41
  351.3 12.6 %collective-permute-done.41 = bf16[208,512]{1,0:T(8,128)(2,1)S(1)} collective-permute-done((bf16[208,512]{1,0:T(8,128)(2,1)S(1)}, bf16[208,512]{1,0:T(8,128)(2,1)S(1)}, u32[]{:S(2)}, u32[]{:S(2)}) %collective-permute-start.41) | collective-permute-done | bytes 213024 | tf_op jit(solution)/shard_map/ppermute | solution.py:800
  364.6 6.1 %shard_map.422 = bf16[2048,512]{1,0:T(8,128)(2,1)S(1)} custom-call(bf16[448,512]{1,0:T(8,128)(2,1)S(1)} %add_convert_fusion.8.refs_0_, bf16[384,512]{1,0:T(8,128)(2,1)S(1)} %add_convert_fusion.9.refs_1_, s32[1,1024]{1,0:T(1,128)S(1)} %broadcast_subtract_fusion.1.refs_2_, s32[1,1024]{1,0:T(1,128)S(1)} %broadcast_subtract_fusion.3.refs_3_, ...), custom_call_target="tpu_custom_call" | custom-call | flops 4294967296 | bytes 8388608 | tf_op jit(solution)/shard_map/pallas_call | solution.py:208
  370.9 2.2 collective-permute-done.42
  373.3 7.3 %collective-permute-start.43 = (bf16[416,512]{1,0:T(8,128)(2,1)S(1)}, bf16[416,512]{1,0:T(8,128)(2,1)S(1)}, u32[]{:S(2)}, u32[]{:S(2)}) collective-permute-start(bf16[416,512]{1,0:T(8,128)(2,1)S(1)} %pad_maximum_fusion.8), channel_id=1, source_target_pairs={{0,1},{1,0},{2,3},{3,2},{4,5},{5,4},{6,7},{7,6},{8,9},{9,8},{10,11... | collective-permute-start | bytes 1277960 | tf_op jit(solution)/shard_map/ppermute | solution.py:800
  382.2 16.3 %collective-permute-done.50 = bf16[640,512]{1,0:T(8,128)(2,1)S(1)} collective-permute-done((bf16[640,512]{1,0:T(8,128)(2,1)S(1)}, bf16[640,512]{1,0:T(8,128)(2,1)S(1)}, u32[]{:S(2)}, u32[]{:S(2)}) %collective-permute-start.50) | collective-permute-done | bytes 655392 | tf_op jit(solution)/shard_map/ppermute | solution.py:800
  399.0 1.6 collective-permute-start.54
  400.7 7.0 %collective-permute-done.51 = bf16[320,512]{1,0:T(8,128)(2,1)S(1)} collective-permute-done((bf16[320,512]{1,0:T(8,128)(2,1)S(1)}, bf16[320,512]{1,0:T(8,128)(2,1)S(1)}, u32[]{:S(2)}, u32[]{:S(2)}) %collective-permute-start.51) | collective-permute-done | bytes 327712 | tf_op jit(solution)/shard_map/ppermute | solution.py:800
  413.1 3.3 collective-permute-done.55
  418.4 5.8 %collective-permute-done.46 = bf16[384,512]{1,0:T(8,128)(2,1)S(1)} collective-permute-done((bf16[384,512]{1,0:T(8,128)(2,1)S(1)}, bf16[384,512]{1,0:T(8,128)(2,1)S(1)}, u32[]{:S(2)}, u32[]{:S(2)}) %collective-permute-start.46) | collective-permute-done | bytes 393248 | tf_op jit(solution)/shard_map/ppermute | solution.py:800
  426.3 2.7 collective-permute-done.44
  430.2 4.1 collective-permute-done.57
  435.2 10.0 %collective-permute-done.47 = bf16[768,512]{1,0:T(8,128)(2,1)S(1)} collective-permute-done((bf16[768,512]{1,0:T(8,128)(2,1)S(1)}, bf16[768,512]{1,0:T(8,128)(2,1)S(1)}, u32[]{:S(2)}, u32[]{:S(2)}) %collective-permute-start.47) | collective-permute-done | bytes 786464 | tf_op jit(solution)/shard_map/ppermute | solution.py:800
  449.2 4.1 collective-permute-done.61
  454.7 2.1 collective-permute-done.59
  458.5 10.5 %collective-permute-done.62 = bf16[640,512]{1,0:T(8,128)(2,1)S(1)} collective-permute-done((bf16[640,512]{1,0:T(8,128)(2,1)S(1)}, bf16[640,512]{1,0:T(8,128)(2,1)S(1)}, u32[]{:S(2)}, u32[]{:S(2)}) %collective-permute-start.62) | collective-permute-done | bytes 655392 | tf_op jit(solution)/shard_map/ppermute | solution.py:800
  471.5 2.0 collective-permute-start.33
  473.5 2.9 collective-permute-done.36
  478.7 4.2 collective-permute-done.37
  484.4 2.9 collective-permute-done.34
  487.5 2.0 collective-permute-done.38
  490.7 2.7 collective-permute-done.39.refs_2_
  494.4 3.6 shard_map.423.refs_1_
  498.0 6.9 %shard_map.424 = (f32[4608,512]{1,0:T(8,128)}, f32[512,512]{1,0:T(8,128)}, f32[512,512]{1,0:T(8,128)}, f32[512,512]{1,0:T(8,128)}, f32[512,512]{1,0:T(8,128)}) custom-call(s32[1]{0:T(128)} %bitcast.38.refs_0_.refs_2_, bf16[3328,512]{1,0:T(8,128)(2,1)} %copy-done.7, bf16[3328,512]{1,0:T(8,128)(2,1)} %collective-permute-done.48.refs_2_), custom_call_target="tpu_custom_call" | custom-call | bytes 20447236 | tf_op jit(solution)/shard_map/pallas_call | solution.py:34
  504.9 5.4 %shard_map.425 = (f32[4608,512]{1,0:T(8,128)}, f32[256,512]{1,0:T(8,128)}, f32[256,512]{1,0:T(8,128)}) custom-call(f32[4608,512]{1,0:T(8,128)} %get-tuple-element.130.refs_0_, f32[4096,256]{1,0:T(8,128)} %shard_map.423.refs_1_, s32[1]{0:T(128)} %bitcast.38.refs_0_.refs_2_, bf16[2560,512]{1,0:T(8,128)(2,1)} %copy-done.8, ...), custom_call_target="tpu_custom_call" | custom-call | bytes 29360132 | tf_op jit(solution)/shard_map/pallas_call | solution.py:34
  510.4 1.6 fusion.11
  (347 shorter events, 91.0 us)
Async XLA Ops:
  0.7 19.9 %collective-permute-start.1 = (s32[1,1024]{1,0:T(1,128)}, s32[1,1024]{1,0:T(1,128)S(1)}, u32[]{:S(2)}, u32[]{:S(2)}) collective-permute-start(s32[1,1024]{1,0:T(1,128)} %param.26), channel_id=1, source_target_pairs={{0,2},{1,3},{2,0},{3,1},{4,6},{5,7},{6,4},{7,5},{8,10},{9,11},{10,... | collective-permute-start | bytes 12296 | tf_op jit(solution)/shard_map/ppermute | solution.py:792
  4.8 7.9 %collective-permute-start = (s32[1,1024]{1,0:T(1,128)}, s32[1,1024]{1,0:T(1,128)S(1)}, u32[]{:S(2)}, u32[]{:S(2)}) collective-permute-start(s32[1,1024]{1,0:T(1,128)} %param.26), channel_id=1, source_target_pairs={{0,3},{1,0},{2,1},{3,2},{4,7},{5,4},{6,5},{7,6},{8,11},{9,8},{10,9... | collective-permute-start | bytes 12296 | tf_op jit(solution)/shard_map/ppermute | solution.py:792
  6.1 6.3 %collective-permute-start.2 = (s32[1,1024]{1,0:T(1,128)}, s32[1,1024]{1,0:T(1,128)S(1)}, u32[]{:S(2)}, u32[]{:S(2)}) collective-permute-start(s32[1,1024]{1,0:T(1,128)} %param.26), channel_id=1, source_target_pairs={{0,1},{1,2},{2,3},{3,0},{4,5},{5,6},{6,7},{7,4},{8,9},{9,10},{10,1... | collective-permute-start | bytes 12296 | tf_op jit(solution)/shard_map/ppermute | solution.py:792
  25.5 37.5 %collective-permute-start.4 = (bf16[1024,256]{1,0:T(8,128)(2,1)S(1)}, bf16[1024,256]{1,0:T(8,128)(2,1)S(1)}, u32[]{:S(2)}, u32[]{:S(2)}) collective-permute-start(bf16[1024,256]{1,0:T(8,128)(2,1)S(1)} %shard_map.409.refs_1_), channel_id=1, source_target_pairs={{0,2},{1,3},{2,0},{3,1},{4,6},{5,7},{6,4},{7,5},{8,10},{9,11},{10,... | collective-permute-start | bytes 1572872 | tf_op jit(solution)/shard_map/ppermute | solution.py:792
  26.6 36.4 %collective-permute-start.3 = (bf16[1024,256]{1,0:T(8,128)(2,1)S(1)}, bf16[1024,256]{1,0:T(8,128)(2,1)S(1)}, u32[]{:S(2)}, u32[]{:S(2)}) collective-permute-start(bf16[1024,256]{1,0:T(8,128)(2,1)S(1)} %shard_map.408.refs_0_), channel_id=1, source_target_pairs={{0,1},{1,2},{2,3},{3,0},{4,5},{5,6},{6,7},{7,4},{8,9},{9,10},{10,1... | collective-permute-start | bytes 1572872 | tf_op jit(solution)/shard_map/ppermute | solution.py:792
  29.3 33.7 %collective-permute-start.5 = (bf16[1024,256]{1,0:T(8,128)(2,1)S(1)}, bf16[1024,256]{1,0:T(8,128)(2,1)S(1)}, u32[]{:S(2)}, u32[]{:S(2)}) collective-permute-start(bf16[1024,256]{1,0:T(8,128)(2,1)S(1)} %shard_map.410.refs_2_), channel_id=1, source_target_pairs={{0,3},{1,0},{2,1},{3,2},{4,7},{5,4},{6,5},{7,6},{8,11},{9,8},{10,9... | collective-permute-start | bytes 1572872 | tf_op jit(solution)/shard_map/ppermute | solution.py:792
  68.2 5.0 collective-permute-start.6
  69.5 5.2 %collective-permute-start.7 = (f32[72,512]{1,0:T(8,128)}, f32[72,512]{1,0:T(8,128)S(1)}, u32[]{:S(2)}, u32[]{:S(2)}) collective-permute-start(f32[72,512]{1,0:T(8,128)} %get-tuple-element.83), channel_id=1, source_target_pairs={{4,0},{8,4},{12,8},{16,12},{20,16},{24,20},{28,24},{5,1},{9,5},{13... | collective-permute-start | bytes 442376 | tf_op jit(solution)/shard_map/ppermute | solution.py:787
  89.7 7.4 %collective-permute-start.8 = (f32[72,512]{1,0:T(8,128)}, f32[72,512]{1,0:T(8,128)S(1)}, u32[]{:S(2)}, u32[]{:S(2)}) collective-permute-start(f32[72,512]{1,0:T(8,128)} %get-tuple-element.86), channel_id=1, source_target_pairs={{0,4},{4,8},{8,12},{12,16},{16,20},{20,24},{24,28},{1,5},{5,9},{9,... | collective-permute-start | bytes 442376 | tf_op jit(solution)/shard_map/ppermute | solution.py:787
  95.3 3.5 collective-permute-start.9
  115.5 10.0 %collective-permute-start.10 = (bf16[1104,512]{1,0:T(8,128)(2,1)}, bf16[1104,512]{1,0:T(8,128)(2,1)S(1)}, u32[]{:S(2)}, u32[]{:S(2)}) collective-permute-start(bf16[1104,512]{1,0:T(8,128)(2,1)} %get-tuple-element.90), channel_id=1, source_target_pairs={{0,4},{4,8},{8,12},{12,16},{16,20},{20,24},{24,28},{1,5},{5,9},{9,... | collective-permute-start | bytes 3391496 | tf_op jit(solution)/shard_map/ppermute | solution.py:787
  121.4 4.9 collective-permute-start.11
  152.8 39.2 %collective-permute-start.13 = (bf16[1104,512]{1,0:T(8,128)(2,1)}, bf16[1104,512]{1,0:T(8,128)(2,1)S(1)}, u32[]{:S(2)}, u32[]{:S(2)}) collective-permute-start(bf16[1104,512]{1,0:T(8,128)(2,1)} %get-tuple-element.101.refs_2_), channel_id=1, source_target_pairs={{4,0},{8,4},{12,8},{16,12},{20,16},{24,20},{28,24},{5,1},{9,5},{13... | collective-permute-start | bytes 3391496 | tf_op jit(solution)/shard_map/ppermute | solution.py:787
  154.1 37.9 %collective-permute-start.12 = (bf16[1104,512]{1,0:T(8,128)(2,1)}, bf16[1104,512]{1,0:T(8,128)(2,1)S(1)}, u32[]{:S(2)}, u32[]{:S(2)}) collective-permute-start(bf16[1104,512]{1,0:T(8,128)(2,1)} %get-tuple-element.102.refs_3_), channel_id=1, source_target_pairs={{0,4},{4,8},{8,12},{12,16},{16,20},{20,24},{24,28},{1,5},{5,9},{9,... | collective-permute-start | bytes 3391496 | tf_op jit(solution)/shard_map/ppermute | solution.py:787
  222.7 44.7 %collective-permute-start.16 = (bf16[2304,512]{1,0:T(8,128)(2,1)}, bf16[2304,512]{1,0:T(8,128)(2,1)}, u32[]{:S(2)}, u32[]{:S(2)}) collective-permute-start(bf16[2304,512]{1,0:T(8,128)(2,1)} %constant_dynamic-slice_fusion.28), channel_id=1, source_target_pairs={{0,4},{4,0},{8,12},{12,8},{16,20},{20,16},{24,28},{28,24},{1,5},{5... | collective-permute-start | bytes 7077896 | tf_op jit(solution)/shard_map/ppermute | solution.py:800
  237.7 28.7 %collective-permute-start.17 = (bf16[1024,512]{1,0:T(8,128)(2,1)S(1)}, bf16[1024,512]{1,0:T(8,128)(2,1)S(1)}, u32[]{:S(2)}, u32[]{:S(2)}) collective-permute-start(bf16[1024,512]{1,0:T(8,128)(2,1)S(1)} %constant_dynamic-slice_fusion.27), channel_id=1, source_target_pairs={{0,4},{4,0},{8,12},{12,8},{16,20},{20,16},{24,28},{28,24},{1,5},{5... | collective-permute-start | bytes 3145736 | tf_op jit(solution)/shard_map/ppermute | solution.py:800
  237.8 4.8 collective-permute-start.14
  240.2 3.3 collective-permute-start.15
  258.9 7.5 %collective-permute-start.18 = (f32[8,512]{1,0:T(8,128)}, f32[8,512]{1,0:T(8,128)S(1)}, u32[]{:S(2)}, u32[]{:S(2)}) collective-permute-start(f32[8,512]{1,0:T(8,128)} %get-tuple-element.114), channel_id=1, source_target_pairs={{0,4},{4,8},{8,12},{12,16},{16,20},{20,24},{24,28},{1,5},{5,9},{9,... | collective-permute-start | bytes 49160 | tf_op jit(solution)/shard_map/ppermute | solution.py:787
  264.1 3.3 collective-permute-start.19
  272.9 36.0 %collective-permute-start.25 = (bf16[1024,256]{1,0:T(8,128)(2,1)}, bf16[1024,256]{1,0:T(8,128)(2,1)S(1)}, u32[]{:S(2)}, u32[]{:S(2)}) collective-permute-start(bf16[1024,256]{1,0:T(8,128)(2,1)} %get-tuple-element.118.grad_ref), channel_id=1, source_target_pairs={{1,0},{2,1},{3,2},{5,4},{6,5},{7,6},{9,8},{10,9},{11,10},{13,12},{... | collective-permute-start | bytes 1572872 | tf_op jit(solution)/shard_map/ppermute | solution.py:787
  274.2 36.1 %collective-permute-start.24 = (bf16[1024,256]{1,0:T(8,128)(2,1)}, bf16[1024,256]{1,0:T(8,128)(2,1)S(1)}, u32[]{:S(2)}, u32[]{:S(2)}) collective-permute-start(bf16[1024,256]{1,0:T(8,128)(2,1)} %get-tuple-element.118.grad_ref), channel_id=1, source_target_pairs={{0,1},{1,2},{2,3},{4,5},{5,6},{6,7},{8,9},{9,10},{10,11},{12,13},{... | collective-permute-start | bytes 1572872 | tf_op jit(solution)/shard_map/ppermute | solution.py:787
  295.0 21.8 %collective-permute-start.22 = (bf16[768,512]{1,0:T(8,128)(2,1)S(1)}, bf16[768,512]{1,0:T(8,128)(2,1)S(1)}, u32[]{:S(2)}, u32[]{:S(2)}) collective-permute-start(bf16[768,512]{1,0:T(8,128)(2,1)S(1)} %constant_dynamic-slice_fusion.24), channel_id=1, source_target_pairs={{0,16},{4,20},{8,24},{12,28},{16,0},{20,4},{24,8},{28,12},{1,17},{... | collective-permute-start | bytes 2359304 | tf_op jit(solution)/shard_map/ppermute | solution.py:800
  299.5 23.5 %collective-permute-start.20 = (bf16[896,512]{1,0:T(8,128)(2,1)}, bf16[896,512]{1,0:T(8,128)(2,1)S(1)}, u32[]{:S(2)}, u32[]{:S(2)}) collective-permute-start(bf16[896,512]{1,0:T(8,128)(2,1)} %constant_dynamic-slice_fusion.26), channel_id=1, source_target_pairs={{0,8},{4,12},{8,0},{12,4},{16,24},{20,28},{24,16},{28,20},{1,9},{5... | collective-permute-start | bytes 2752520 | tf_op jit(solution)/shard_map/ppermute | solution.py:800
  308.9 30.1 %collective-permute-start.26 = (bf16[1024,256]{1,0:T(8,128)(2,1)S(1)}, bf16[1024,256]{1,0:T(8,128)(2,1)S(1)}, u32[]{:S(2)}, u32[]{:S(2)}) collective-permute-start(bf16[1024,256]{1,0:T(8,128)(2,1)S(1)} %collective-permute-done.25.refs_7_), channel_id=1, source_target_pairs={{1,0},{2,1},{3,2},{5,4},{6,5},{7,6},{9,8},{10,9},{11,10},{13,12},{... | collective-permute-start | bytes 1572872 | tf_op jit(solution)/shard_map/ppermute | solution.py:787
  310.3 30.0 %collective-permute-start.28 = (bf16[1024,256]{1,0:T(8,128)(2,1)S(1)}, bf16[1024,256]{1,0:T(8,128)(2,1)S(1)}, u32[]{:S(2)}, u32[]{:S(2)}) collective-permute-start(bf16[1024,256]{1,0:T(8,128)(2,1)S(1)} %collective-permute-done.24.refs_4_), channel_id=1, source_target_pairs={{0,1},{1,2},{2,3},{4,5},{5,6},{6,7},{8,9},{9,10},{10,11},{12,13},{... | collective-permute-start | bytes 1572872 | tf_op jit(solution)/shard_map/ppermute | solution.py:787
  317.0 14.4 %collective-permute-start.23 = (bf16[384,512]{1,0:T(8,128)(2,1)S(1)}, bf16[384,512]{1,0:T(8,128)(2,1)S(1)}, u32[]{:S(2)}, u32[]{:S(2)}) collective-permute-start(bf16[384,512]{1,0:T(8,128)(2,1)S(1)} %constant_dynamic-slice_fusion.23), channel_id=1, source_target_pairs={{0,8},{4,12},{8,0},{12,4},{16,24},{20,28},{24,16},{28,20},{1,9},{5... | collective-permute-start | bytes 1179656 | tf_op jit(solution)/shard_map/ppermute | solution.py:800
  323.4 11.1 %collective-permute-start.21 = (bf16[448,512]{1,0:T(8,128)(2,1)S(1)}, bf16[448,512]{1,0:T(8,128)(2,1)S(1)}, u32[]{:S(2)}, u32[]{:S(2)}) collective-permute-start(bf16[448,512]{1,0:T(8,128)(2,1)S(1)} %constant_dynamic-slice_fusion.25), channel_id=1, source_target_pairs={{0,16},{4,20},{8,24},{12,28},{16,0},{20,4},{24,8},{28,12},{1,17},{... | collective-permute-start | bytes 1376264 | tf_op jit(solution)/shard_map/ppermute | solution.py:800
  331.4 19.8 %collective-permute-start.52 = (bf16[256,512]{1,0:T(8,128)(2,1)S(1)}, bf16[256,512]{1,0:T(8,128)(2,1)S(1)}, u32[]{:S(2)}, u32[]{:S(2)}) collective-permute-start(bf16[256,512]{1,0:T(8,128)(2,1)S(1)} %constant_dynamic-slice_fusion.8), channel_id=1, source_target_pairs={{0,4},{4,0},{8,12},{12,8},{16,20},{20,16},{24,28},{28,24},{1,5},{5... | collective-permute-start | bytes 786440 | tf_op jit(solution)/shard_map/ppermute | solution.py:800
  334.7 14.2 %collective-permute-start.40 = (bf16[416,512]{1,0:T(8,128)(2,1)S(1)}, bf16[416,512]{1,0:T(8,128)(2,1)S(1)}, u32[]{:S(2)}, u32[]{:S(2)}) collective-permute-start(bf16[416,512]{1,0:T(8,128)(2,1)S(1)} %pad_maximum_fusion.7), channel_id=1, source_target_pairs={{0,1},{1,0},{2,3},{3,2},{4,5},{5,4},{6,7},{7,6},{8,9},{9,8},{10,11... | collective-permute-start | bytes 1277960 | tf_op jit(solution)/shard_map/ppermute | solution.py:800
  338.9 41.7 %collective-permute-start.49 = (bf16[2304,512]{1,0:T(8,128)(2,1)S(1)}, bf16[2304,512]{1,0:T(8,128)(2,1)S(1)}, u32[]{:S(2)}, u32[]{:S(2)}) collective-permute-start(bf16[2304,512]{1,0:T(8,128)(2,1)S(1)} %constant_dynamic-slice_fusion.13), channel_id=1, source_target_pairs={{0,4},{4,0},{8,12},{12,8},{16,20},{20,16},{24,28},{28,24},{1,5},{5... | collective-permute-start | bytes 7077896 | tf_op jit(solution)/shard_map/ppermute | solution.py:800
  339.0 25.6 %collective-permute-start.27 = (bf16[1024,256]{1,0:T(8,128)(2,1)S(1)}, bf16[1024,256]{1,0:T(8,128)(2,1)S(1)}, u32[]{:S(2)}, u32[]{:S(2)}) collective-permute-start(bf16[1024,256]{1,0:T(8,128)(2,1)S(1)} %collective-permute-done.26.refs_4_), channel_id=1, source_target_pairs={{1,0},{2,1},{3,2},{5,4},{6,5},{7,6},{9,8},{10,9},{11,10},{13,12},{... | collective-permute-start | bytes 1572872 | tf_op jit(solution)/shard_map/ppermute | solution.py:787
  340.3 24.3 %collective-permute-start.29 = (bf16[1024,256]{1,0:T(8,128)(2,1)S(1)}, bf16[1024,256]{1,0:T(8,128)(2,1)S(1)}, u32[]{:S(2)}, u32[]{:S(2)}) collective-permute-start(bf16[1024,256]{1,0:T(8,128)(2,1)S(1)} %collective-permute-done.28.refs_3_), channel_id=1, source_target_pairs={{0,1},{1,2},{2,3},{4,5},{5,6},{6,7},{8,9},{9,10},{10,11},{12,13},{... | collective-permute-start | bytes 1572872 | tf_op jit(solution)/shard_map/ppermute | solution.py:787
  349.1 14.8 %collective-permute-start.41 = (bf16[208,512]{1,0:T(8,128)(2,1)S(1)}, bf16[208,512]{1,0:T(8,128)(2,1)S(1)}, u32[]{:S(2)}, u32[]{:S(2)}) collective-permute-start(bf16[208,512]{1,0:T(8,128)(2,1)S(1)} %pad_maximum_fusion.14), channel_id=1, source_target_pairs={{0,2},{1,3},{2,0},{3,1},{4,6},{5,7},{6,4},{7,5},{8,10},{9,11},{10,... | collective-permute-start | bytes 638984 | tf_op jit(solution)/shard_map/ppermute | solution.py:800
  364.0 9.1 %collective-permute-start.42 = (bf16[208,512]{1,0:T(8,128)(2,1)S(1)}, bf16[208,512]{1,0:T(8,128)(2,1)S(1)}, u32[]{:S(2)}, u32[]{:S(2)}) collective-permute-start(bf16[208,512]{1,0:T(8,128)(2,1)S(1)} %pad_maximum_fusion.15), channel_id=1, source_target_pairs={{0,2},{1,3},{2,0},{3,1},{4,6},{5,7},{6,4},{7,5},{8,10},{9,11},{10,... | collective-permute-start | bytes 638984 | tf_op jit(solution)/shard_map/ppermute | solution.py:800
  370.8 11.0 %collective-permute-start.30 = (bf16[1024,512]{1,0:T(8,128)(2,1)S(1)}, bf16[1024,512]{1,0:T(8,128)(2,1)S(1)}, u32[]{:S(2)}, u32[]{:S(2)}) collective-permute-start(bf16[1024,512]{1,0:T(8,128)(2,1)S(1)} %constant_dynamic-slice_fusion.22), channel_id=1, source_target_pairs={{0,4},{4,0},{8,12},{12,8},{16,20},{20,16},{24,28},{28,24},{1,5},{5... | collective-permute-start | bytes 3145736 | tf_op jit(solution)/shard_map/ppermute | solution.py:800
  373.3 38.1 %collective-permute-start.43 = (bf16[416,512]{1,0:T(8,128)(2,1)S(1)}, bf16[416,512]{1,0:T(8,128)(2,1)S(1)}, u32[]{:S(2)}, u32[]{:S(2)}) collective-permute-start(bf16[416,512]{1,0:T(8,128)(2,1)S(1)} %pad_maximum_fusion.8), channel_id=1, source_target_pairs={{0,1},{1,0},{2,3},{3,2},{4,5},{5,4},{6,7},{7,6},{8,9},{9,8},{10,11... | collective-permute-start | bytes 1277960 | tf_op jit(solution)/shard_map/ppermute | solution.py:800
  381.5 16.9 %collective-permute-start.50 = (bf16[640,512]{1,0:T(8,128)(2,1)S(1)}, bf16[640,512]{1,0:T(8,128)(2,1)S(1)}, u32[]{:S(2)}, u32[]{:S(2)}) collective-permute-start(bf16[640,512]{1,0:T(8,128)(2,1)S(1)} %constant_dynamic-slice_fusion.12), channel_id=1, source_target_pairs={{0,8},{4,12},{8,0},{12,4},{16,24},{20,28},{24,16},{28,20},{1,9},{5... | collective-permute-start | bytes 1966088 | tf_op jit(solution)/shard_map/ppermute | solution.py:800
  381.7 17.0 %collective-permute-start.53 = (bf16[640,512]{1,0:T(8,128)(2,1)S(1)}, bf16[640,512]{1,0:T(8,128)(2,1)S(1)}, u32[]{:S(2)}, u32[]{:S(2)}) collective-permute-start(bf16[640,512]{1,0:T(8,128)(2,1)S(1)} %pad_maximum_fusion.5), channel_id=1, source_target_pairs={{0,16},{4,20},{8,24},{12,28},{16,0},{20,4},{24,8},{28,12},{1,17},{... | collective-permute-start | bytes 1966088 | tf_op jit(solution)/shard_map/ppermute | solution.py:800
  398.6 9.1 %collective-permute-start.51 = (bf16[320,512]{1,0:T(8,128)(2,1)S(1)}, bf16[320,512]{1,0:T(8,128)(2,1)S(1)}, u32[]{:S(2)}, u32[]{:S(2)}) collective-permute-start(bf16[320,512]{1,0:T(8,128)(2,1)S(1)} %constant_dynamic-slice_fusion.11), channel_id=1, source_target_pairs={{0,16},{4,20},{8,24},{12,28},{16,0},{20,4},{24,8},{28,12},{1,17},{... | collective-permute-start | bytes 983048 | tf_op jit(solution)/shard_map/ppermute | solution.py:800
  399.0 9.1 %collective-permute-start.54 = (bf16[320,512]{1,0:T(8,128)(2,1)S(1)}, bf16[320,512]{1,0:T(8,128)(2,1)S(1)}, u32[]{:S(2)}, u32[]{:S(2)}) collective-permute-start(bf16[320,512]{1,0:T(8,128)(2,1)S(1)} %pad_maximum_fusion.11), channel_id=1, source_target_pairs={{0,8},{4,12},{8,0},{12,4},{16,24},{20,28},{24,16},{28,20},{1,9},{5... | collective-permute-start | bytes 983048 | tf_op jit(solution)/shard_map/ppermute | solution.py:800
  408.3 8.2 %collective-permute-start.55 = (bf16[320,512]{1,0:T(8,128)(2,1)S(1)}, bf16[320,512]{1,0:T(8,128)(2,1)S(1)}, u32[]{:S(2)}, u32[]{:S(2)}) collective-permute-start(bf16[320,512]{1,0:T(8,128)(2,1)S(1)} %pad_maximum_fusion.12), channel_id=1, source_target_pairs={{0,1},{1,0},{2,3},{3,2},{4,5},{5,4},{6,7},{7,6},{8,9},{9,8},{10,11... | collective-permute-start | bytes 983048 | tf_op jit(solution)/shard_map/ppermute | solution.py:800
  409.0 17.2 %collective-permute-start.31 = (bf16[256,512]{1,0:T(8,128)(2,1)S(1)}, bf16[256,512]{1,0:T(8,128)(2,1)S(1)}, u32[]{:S(2)}, u32[]{:S(2)}) collective-permute-start(bf16[256,512]{1,0:T(8,128)(2,1)S(1)} %constant_dynamic-slice_fusion.21), channel_id=1, source_target_pairs={{0,8},{4,12},{8,0},{12,4},{16,24},{20,28},{24,16},{28,20},{1,9},{5... | collective-permute-start | bytes 786440 | tf_op jit(solution)/shard_map/ppermute | solution.py:800
  410.4 60.0 %collective-permute-start.35 = (bf16[256,512]{1,0:T(8,128)(2,1)S(1)}, bf16[256,512]{1,0:T(8,128)(2,1)S(1)}, u32[]{:S(2)}, u32[]{:S(2)}) collective-permute-start(bf16[256,512]{1,0:T(8,128)(2,1)S(1)} %constant_dynamic-slice_fusion.19), channel_id=1, source_target_pairs={{0,16},{4,20},{8,24},{12,28},{16,0},{20,4},{24,8},{28,12},{1,17},{... | collective-permute-start | bytes 786440 | tf_op jit(solution)/shard_map/ppermute | solution.py:800
  411.5 12.7 %collective-permute-start.46 = (bf16[384,512]{1,0:T(8,128)(2,1)S(1)}, bf16[384,512]{1,0:T(8,128)(2,1)S(1)}, u32[]{:S(2)}, u32[]{:S(2)}) collective-permute-start(bf16[384,512]{1,0:T(8,128)(2,1)S(1)} %maximum_select_fusion.11), channel_id=1, source_target_pairs={{0,8},{4,12},{8,0},{12,4},{16,24},{20,28},{24,16},{28,20},{1,9},{5... | collective-permute-start | bytes 1179656 | tf_op jit(solution)/shard_map/ppermute | solution.py:800
  416.6 9.4 %collective-permute-start.56 = (bf16[160,512]{1,0:T(8,128)(2,1)S(1)}, bf16[160,512]{1,0:T(8,128)(2,1)S(1)}, u32[]{:S(2)}, u32[]{:S(2)}) collective-permute-start(bf16[160,512]{1,0:T(8,128)(2,1)S(1)} %pad_maximum_fusion.18), channel_id=1, source_target_pairs={{0,2},{1,3},{2,0},{3,1},{4,6},{5,7},{6,4},{7,5},{8,10},{9,11},{10,... | collective-permute-start | bytes 491528 | tf_op jit(solution)/shard_map/ppermute | solution.py:800
  416.9 12.1 %collective-permute-start.44 = (bf16[448,512]{1,0:T(8,128)(2,1)S(1)}, bf16[448,512]{1,0:T(8,128)(2,1)S(1)}, u32[]{:S(2)}, u32[]{:S(2)}) collective-permute-start(bf16[448,512]{1,0:T(8,128)(2,1)S(1)} %maximum_select_fusion.10), channel_id=1, source_target_pairs={{0,16},{4,20},{8,24},{12,28},{16,0},{20,4},{24,8},{28,12},{1,17},{... | collective-permute-start | bytes 1376264 | tf_op jit(solution)/shard_map/ppermute | solution.py:800
  424.6 20.6 %collective-permute-start.47 = (bf16[768,512]{1,0:T(8,128)(2,1)S(1)}, bf16[768,512]{1,0:T(8,128)(2,1)S(1)}, u32[]{:S(2)}, u32[]{:S(2)}) collective-permute-start(bf16[768,512]{1,0:T(8,128)(2,1)S(1)} %maximum_select_fusion.5), channel_id=1, source_target_pairs={{0,16},{4,20},{8,24},{12,28},{16,0},{20,4},{24,8},{28,12},{1,17},{... | collective-permute-start | bytes 2359304 | tf_op jit(solution)/shard_map/ppermute | solution.py:800
  426.1 8.1 %collective-permute-start.57 = (bf16[160,512]{1,0:T(8,128)(2,1)S(1)}, bf16[160,512]{1,0:T(8,128)(2,1)S(1)}, u32[]{:S(2)}, u32[]{:S(2)}) collective-permute-start(bf16[160,512]{1,0:T(8,128)(2,1)S(1)} %fusion.5), channel_id=1, source_target_pairs={{0,2},{1,3},{2,0},{3,1},{4,6},{5,7},{6,4},{7,5},{8,10},{9,11},{10,... | collective-permute-start | bytes 491528 | tf_op jit(solution)/shard_map/ppermute | solution.py:800
  429.4 17.8 %collective-permute-start.45 = (bf16[896,512]{1,0:T(8,128)(2,1)S(1)}, bf16[896,512]{1,0:T(8,128)(2,1)S(1)}, u32[]{:S(2)}, u32[]{:S(2)}) collective-permute-start(bf16[896,512]{1,0:T(8,128)(2,1)S(1)} %maximum_select_fusion.4), channel_id=1, source_target_pairs={{0,8},{4,12},{8,0},{12,4},{16,24},{20,28},{24,16},{28,20},{1,9},{5... | collective-permute-start | bytes 2752520 | tf_op jit(solution)/shard_map/ppermute | solution.py:800
  434.4 11.4 %collective-permute-start.58 = (bf16[320,512]{1,0:T(8,128)(2,1)S(1)}, bf16[320,512]{1,0:T(8,128)(2,1)S(1)}, u32[]{:S(2)}, u32[]{:S(2)}) collective-permute-start(bf16[320,512]{1,0:T(8,128)(2,1)S(1)} %fusion.3), channel_id=1, source_target_pairs={{0,1},{1,0},{2,3},{3,2},{4,5},{5,4},{6,7},{7,6},{8,9},{9,8},{10,11... | collective-permute-start | bytes 983048 | tf_op jit(solution)/shard_map/ppermute | solution.py:800
  434.5 36.9 %collective-permute-start.32 = (bf16[128,512]{1,0:T(8,128)(2,1)S(1)}, bf16[128,512]{1,0:T(8,128)(2,1)S(1)}, u32[]{:S(2)}, u32[]{:S(2)}) collective-permute-start(bf16[128,512]{1,0:T(8,128)(2,1)S(1)} %constant_dynamic-slice_fusion.20), channel_id=1, source_target_pairs={{0,16},{4,20},{8,24},{12,28},{16,0},{20,4},{24,8},{28,12},{1,17},{... | collective-permute-start | bytes 393224 | tf_op jit(solution)/shard_map/ppermute | solution.py:800
  446.0 7.3 %collective-permute-start.61 = (bf16[320,512]{1,0:T(8,128)(2,1)S(1)}, bf16[320,512]{1,0:T(8,128)(2,1)S(1)}, u32[]{:S(2)}, u32[]{:S(2)}) collective-permute-start(bf16[320,512]{1,0:T(8,128)(2,1)S(1)} %pad_maximum_fusion.13), channel_id=1, source_target_pairs={{0,8},{4,12},{8,0},{12,4},{16,24},{20,28},{24,16},{28,20},{1,9},{5... | collective-permute-start | bytes 983048 | tf_op jit(solution)/shard_map/ppermute | solution.py:800
  447.8 9.0 %collective-permute-start.59 = (bf16[320,512]{1,0:T(8,128)(2,1)S(1)}, bf16[320,512]{1,0:T(8,128)(2,1)S(1)}, u32[]{:S(2)}, u32[]{:S(2)}) collective-permute-start(bf16[320,512]{1,0:T(8,128)(2,1)S(1)} %fusion.2), channel_id=1, source_target_pairs={{0,16},{4,20},{8,24},{12,28},{16,0},{20,4},{24,8},{28,12},{1,17},{... | collective-permute-start | bytes 983048 | tf_op jit(solution)/shard_map/ppermute | solution.py:800
  453.6 15.4 %collective-permute-start.62 = (bf16[640,512]{1,0:T(8,128)(2,1)S(1)}, bf16[640,512]{1,0:T(8,128)(2,1)S(1)}, u32[]{:S(2)}, u32[]{:S(2)}) collective-permute-start(bf16[640,512]{1,0:T(8,128)(2,1)S(1)} %pad_maximum_fusion.6), channel_id=1, source_target_pairs={{0,16},{4,20},{8,24},{12,28},{16,0},{20,4},{24,8},{28,12},{1,17},{... | collective-permute-start | bytes 1966088 | tf_op jit(solution)/shard_map/ppermute | solution.py:800
  457.1 12.5 %collective-permute-start.60 = (bf16[640,512]{1,0:T(8,128)(2,1)S(1)}, bf16[640,512]{1,0:T(8,128)(2,1)S(1)}, u32[]{:S(2)}, u32[]{:S(2)}) collective-permute-start(bf16[640,512]{1,0:T(8,128)(2,1)S(1)} %maximum_select_fusion.6), channel_id=1, source_target_pairs={{0,8},{4,12},{8,0},{12,4},{16,24},{20,28},{24,16},{28,20},{1,9},{5... | collective-permute-start | bytes 1966088 | tf_op jit(solution)/shard_map/ppermute | solution.py:800
  458.4 39.5 %collective-permute-start.48 = (bf16[3328,512]{1,0:T(8,128)(2,1)S(1)}, bf16[3328,512]{1,0:T(8,128)(2,1)}, u32[]{:S(2)}, u32[]{:S(2)}) collective-permute-start(bf16[3328,512]{1,0:T(8,128)(2,1)S(1)} %pad_maximum_fusion.1.refs_1_), channel_id=1, source_target_pairs={{0,4},{4,0},{8,12},{12,8},{16,20},{20,16},{24,28},{28,24},{1,5},{5... | collective-permute-start | bytes 10223624 | tf_op jit(solution)/shard_map/ppermute | solution.py:800
  470.3 34.7 %collective-permute-start.63 = (bf16[2560,512]{1,0:T(8,128)(2,1)S(1)}, bf16[2560,512]{1,0:T(8,128)(2,1)}, u32[]{:S(2)}, u32[]{:S(2)}) collective-permute-start(bf16[2560,512]{1,0:T(8,128)(2,1)S(1)} %pad_maximum_fusion.2.refs_3_), channel_id=1, source_target_pairs={{0,4},{4,0},{8,12},{12,8},{16,20},{20,16},{24,28},{28,24},{1,5},{5... | collective-permute-start | bytes 7864328 | tf_op jit(solution)/shard_map/ppermute | solution.py:800
  470.5 6.0 %collective-permute-start.36 = (bf16[128,512]{1,0:T(8,128)(2,1)S(1)}, bf16[128,512]{1,0:T(8,128)(2,1)S(1)}, u32[]{:S(2)}, u32[]{:S(2)}) collective-permute-start(bf16[128,512]{1,0:T(8,128)(2,1)S(1)} %constant_dynamic-slice_fusion.18), channel_id=1, source_target_pairs={{0,8},{4,12},{8,0},{12,4},{16,24},{20,28},{24,16},{28,20},{1,9},{5... | collective-permute-start | bytes 393224 | tf_op jit(solution)/shard_map/ppermute | solution.py:800
  471.5 6.0 %collective-permute-start.33 = (bf16[128,512]{1,0:T(8,128)(2,1)S(1)}, bf16[128,512]{1,0:T(8,128)(2,1)S(1)}, u32[]{:S(2)}, u32[]{:S(2)}) collective-permute-start(bf16[128,512]{1,0:T(8,128)(2,1)S(1)} %add_convert_fusion.21), channel_id=1, source_target_pairs={{0,16},{4,20},{8,24},{12,28},{16,0},{20,4},{24,8},{28,12},{1,17},{... | collective-permute-start | bytes 393224 | tf_op jit(solution)/shard_map/ppermute | solution.py:800
  476.5 6.5 %collective-permute-start.37 = (bf16[128,512]{1,0:T(8,128)(2,1)S(1)}, bf16[128,512]{1,0:T(8,128)(2,1)S(1)}, u32[]{:S(2)}, u32[]{:S(2)}) collective-permute-start(bf16[128,512]{1,0:T(8,128)(2,1)S(1)} %add_convert_fusion.20), channel_id=1, source_target_pairs={{0,8},{4,12},{8,0},{12,4},{16,24},{20,28},{24,16},{28,20},{1,9},{5... | collective-permute-start | bytes 393224 | tf_op jit(solution)/shard_map/ppermute | solution.py:800
  477.5 9.7 %collective-permute-start.34 = (bf16[256,512]{1,0:T(8,128)(2,1)S(1)}, bf16[256,512]{1,0:T(8,128)(2,1)S(1)}, u32[]{:S(2)}, u32[]{:S(2)}) collective-permute-start(bf16[256,512]{1,0:T(8,128)(2,1)S(1)} %maximum_select_fusion.12), channel_id=1, source_target_pairs={{0,8},{4,12},{8,0},{12,4},{16,24},{20,28},{24,16},{28,20},{1,9},{5... | collective-permute-start | bytes 786440 | tf_op jit(solution)/shard_map/ppermute | solution.py:800
  483.0 6.4 %collective-permute-start.38 = (bf16[256,512]{1,0:T(8,128)(2,1)S(1)}, bf16[256,512]{1,0:T(8,128)(2,1)S(1)}, u32[]{:S(2)}, u32[]{:S(2)}) collective-permute-start(bf16[256,512]{1,0:T(8,128)(2,1)S(1)} %maximum_select_fusion.13), channel_id=1, source_target_pairs={{0,16},{4,20},{8,24},{12,28},{16,0},{20,4},{24,8},{28,12},{1,17},{... | collective-permute-start | bytes 786440 | tf_op jit(solution)/shard_map/ppermute | solution.py:800
  490.7 2.7 collective-permute-start.39
  (47 other events, 309.6 us)

commit v3 on v2

--- a/solution.py
+++ b/solution.py
@@ -170,7 +170,7 @@
 
 def lookup(index, book, tokens=()):
     pixels, emb = index.shape[0], book.shape[1]
-    step = 256
+    step = 512
     return pl.pallas_call(
         functools.partial(lookup_kernel, len(tokens)),
         grid=(pixels // step,),

time: 519 us -> 518 us (level)
  starting transfers between devices: 146 us -> 139 us
  waiting for transfers between devices: 140 us -> 146 us
    ppermute x40, starting transfers between devices: 52.4 us -> 47.2 us  [partner(): lax.ppermute(array, axis, [(i, i ^ bit) for i in range(lax.axis_size(axis...]
where the time goes in v3:
time: 518 us; the launch traced here: 509 us
  waiting for transfers between devices  146 us (28%)
  starting transfers between devices  139 us (27%)
  Pallas kernels  139 us (27%)
  local copies, waits for them, and re-layouts  29.7 us (6%)
  other arithmetic  25.7 us (5%)
  matrix products  25.6 us (5%)
    pallas_call x12, Pallas kernels, call(): pl.pallas_call(body, out_shape=[o[0] for o in outs], in_specs=ins, out_sp...  119 us
    ppermute x40, waiting for transfers between devices, partner(): lax.ppermute(array, axis, [(i, i ^ bit) for i in range(lax.axis_size(axis...  107 us
    ppermute x18, starting transfers between devices, along(): lax.ppermute(array, axis, [(i, i + by) for i in range(count) if 0 <= i +...  81.2 us
    ppermute x40, starting transfers between devices, partner(): lax.ppermute(array, axis, [(i, i ^ bit) for i in range(lax.axis_size(axis...  47.2 us
    ppermute x6, waiting for transfers between devices, around(): lax.ppermute(array, axis, [(i, (i + by) % count) for i in range(count)])  28.4 us
    dot_general x6, matrix products, per_device(): jnp.einsum('nk,nc->kc', a, b, preferred_element_type=f32).astype(bf16)  25.6 us
    unnamed x94, local copies, waits for them, and re-layouts  18.1 us
    ppermute x6, starting transfers between devices, around(): lax.ppermute(array, axis, [(i, (i + by) % count) for i in range(count)])  11 us
  transfers between devices with their start and end apart: 64, of which 28 were waited for; matrix products, arithmetic and copies ran while one was open for 10% of the time, Pallas kernels for 10%

profile of v3, /device:TPU:0, one launch (start us, length us, event | category | flops | bytes accessed | tf_op | source)
XLA Modules:
  0.0 509.2 jit_solution(2464620147886989488)
XLA Ops:
  0.7 4.1 collective-permute-start.1
  14.5 2.6 shard_map.410.refs_2_
  17.1 2.6 shard_map.408.refs_0_
  21.6 2.6 shard_map.409.refs_1_
  25.3 2.7 collective-permute-start.3
  29.8 2.6 shard_map.411.refs_1_
  33.3 28.4 %collective-permute-done.4.refs_3_ = bf16[1024,256]{1,0:T(8,128)(2,1)S(1)} collective-permute-done((bf16[1024,256]{1,0:T(8,128)(2,1)S(1)}, bf16[1024,256]{1,0:T(8,128)(2,1)S(1)}, u32[]{:S(2)}, u32[]{:S(2)}) %collective-permute-start.4) | collective-permute-done | bytes 524320 | tf_op jit(solution)/shard_map/ppermute | solution.py:792
  62.8 4.1 shard_map.412
  68.2 1.8 collective-permute-start.7
  74.0 14.4 %shard_map.413 = (f32[1024,512]{1,0:T(8,128)}, f32[32,512]{1,0:T(8,128)}, f32[32,512]{1,0:T(8,128)}, f32[72,512]{1,0:T(8,128)}, f32[72,512]{1,0:T(8,128)}, /*index=5*/bf16[1024,4608]{1,0:T(8,128)(2,1)}) custom-call(f32[1024,512]{1,0:T(8,128)} %get-tuple-element.81.refs_0_.refs_11_.refs_14_.refs_7_, f32[72,512]{1,0:T(8,128)} %copy-done.38, ...), custom_call_target="tpu_custom_call" | custom-call | flops 4831838208 | bytes 19180928 | tf_op jit(solution)/shard_map/pallas_call | solution.py:34
  88.4 5.6 %collective-permute-start.8 = (f32[72,512]{1,0:T(8,128)}, f32[72,512]{1,0:T(8,128)S(1)}, u32[]{:S(2)}, u32[]{:S(2)}) collective-permute-start(f32[72,512]{1,0:T(8,128)} %get-tuple-element.86), channel_id=1, source_target_pairs={{0,4},{4,8},{8,12},{12,16},{16,20},{20,24},{24,28},{1,5},{5,9},{9,... | collective-permute-start | bytes 442376 | tf_op jit(solution)/shard_map/ppermute | solution.py:787
  95.5 2.0 collective-permute-done.9.refs_2_.refs_5_
  98.1 16.0 %shard_map.414 = (f32[1024,512]{1,0:T(8,128)}, f32[32,512]{1,0:T(8,128)}, f32[32,512]{1,0:T(8,128)}, bf16[1104,512]{1,0:T(8,128)(2,1)}, bf16[1104,512]{1,0:T(8,128)(2,1)}, /*index=5*/bf16[1024,4608]{1,0:T(8,128)(2,1)}) custom-call(f32[1024,512]{1,0:T(8,128)} %get-tuple-element.85.refs_0_.refs_17_.refs_6_, f32[72,512]{1,0:T(8,128)} %copy-done.34, ...), custom_call_target="tpu_custom_call" | custom-call | flops 4831838208 | bytes 24292736 | tf_op jit(solution)/shard_map/pallas_call | solution.py:34
  114.2 5.9 %collective-permute-start.10 = (bf16[1104,512]{1,0:T(8,128)(2,1)}, bf16[1104,512]{1,0:T(8,128)(2,1)S(1)}, u32[]{:S(2)}, u32[]{:S(2)}) collective-permute-start(bf16[1104,512]{1,0:T(8,128)(2,1)} %get-tuple-element.90), channel_id=1, source_target_pairs={{0,4},{4,8},{8,12},{12,16},{16,20},{20,24},{24,28},{1,5},{5,9},{9,... | collective-permute-start | bytes 3391496 | tf_op jit(solution)/shard_map/ppermute | solution.py:787
  126.0 25.5 %shard_map.415 = (bf16[3072,512]{1,0:T(8,128)(2,1)}, bf16[3072,512]{1,0:T(8,128)(2,1)}, bf16[3072,512]{1,0:T(8,128)(2,1)}, bf16[1024,512]{1,0:T(8,128)(2,1)}, bf...) custom-call(f32[1024,512]{1,0:T(8,128)} %get-tuple-element.89.refs_0, ...), custom_call_target="tpu_custom_call" | custom-call | flops 12884901888 | bytes 24669728 | tf_op jit(solution)/shard_map/pallas_call | solution.py:34
  152.8 26.4 %collective-permute-start.12 = (bf16[1104,512]{1,0:T(8,128)(2,1)}, bf16[1104,512]{1,0:T(8,128)(2,1)S(1)}, u32[]{:S(2)}, u32[]{:S(2)}) collective-permute-start(bf16[1104,512]{1,0:T(8,128)(2,1)} %get-tuple-element.102.refs_3_), channel_id=1, source_target_pairs={{0,4},{4,8},{8,12},{12,16},{16,20},{20,24},{24,28},{1,5},{5,9},{9,... | collective-permute-start | bytes 3391496 | tf_op jit(solution)/shard_map/ppermute | solution.py:787
  179.2 4.8 convolution_convert_fusion.2
  192.1 17.4 %shard_map.416 = (f32[1024,512]{1,0:T(8,128)}, bf16[1024,512]{1,0:T(8,128)(2,1)}, f32[1024,512]{1,0:T(8,128)}, f32[32,512]{1,0:T(8,128)}, f32[8,512]{1,0:T(8,128...) custom-call(bf16[2048,512]{1,0:T(8,128)(2,1)} %pad_maximum_fusion.3.refs_0_, f32[1024,512]{1,0:T(8,128)} %get-tuple-element.100.refs_1_, ...), custom_call_target="tpu_custom_call" | custom-call | flops 4831838208 | bytes 26799488 | tf_op jit(solution)/shard_map/pallas_call | solution.py:34
  209.6 8.2 %convolution_convert_fusion.1.refs_0_ = bf16[4608,512]{1,0:T(8,128)(2,1)S(1)} fusion(bf16[1024,4608]{1,0:T(8,128)(2,1)} %get-tuple-element.94, bf16[1024,512]{1,0:T(8,128)(2,1)} %get-tuple-element.106), kind=kOutput, calls=%fused_computation.1 | convolution fusion | flops 4834197504 | bytes 15204352 | tf_op jit(solution)/shard_map/nk,nc->kc/dot_general | solution.py:974
  219.3 1.8 copy-done.11
  221.2 9.7 %collective-permute-start.16 = (bf16[2304,512]{1,0:T(8,128)(2,1)}, bf16[2304,512]{1,0:T(8,128)(2,1)}, u32[]{:S(2)}, u32[]{:S(2)}) collective-permute-start(bf16[2304,512]{1,0:T(8,128)(2,1)} %constant_dynamic-slice_fusion.28), channel_id=1, source_target_pairs={{0,4},{4,0},{8,12},{12,8},{16,20},{20,16},{24,28},{28,24},{1,5},{5... | collective-permute-start | bytes 7077896 | tf_op jit(solution)/shard_map/ppermute | solution.py:800
  232.4 2.4 collective-permute-start.14
  237.2 5.5 %collective-permute-done.15.refs_3_ = f32[72,512]{1,0:T(8,128)S(1)} collective-permute-done((f32[72,512]{1,0:T(8,128)S(1)}, f32[72,512]{1,0:T(8,128)S(1)}, u32[]{:S(2)}, u32[]{:S(2)}) %collective-permute-start.15) | collective-permute-done | bytes 147488 | tf_op jit(solution)/shard_map/ppermute | solution.py:787
  243.3 14.8 %shard_map.417 = (bf16[1024,512]{1,0:T(8,128)(2,1)}, f32[1024,512]{1,0:T(8,128)}, f32[32,512]{1,0:T(8,128)}, f32[8,512]{1,0:T(8,128)}, f32[8,512]{1,0:T(8,128)}, /*index=5*/f32[8,512]{1,0:T(8,128)}) custom-call(bf16[4608,512]{1,0:T(8,128)(2,1)} %copy-done.11, f32[1024,512]{1,0:T(8,128)} %get-tuple-element.107.refs_1_, f32[72,512]{1,0:T(8,128)} %copy-done.40, ...), custom_call_target="tpu_custom_call" | custom-call | flops 4831838208 | bytes 19819904 | tf_op jit(solution)/shard_map/pallas_call | solution.py:34
  258.1 5.6 %collective-permute-start.18 = (f32[8,512]{1,0:T(8,128)}, f32[8,512]{1,0:T(8,128)S(1)}, u32[]{:S(2)}, u32[]{:S(2)}) collective-permute-start(f32[8,512]{1,0:T(8,128)} %get-tuple-element.114), channel_id=1, source_target_pairs={{0,4},{4,8},{8,12},{12,16},{16,20},{20,24},{24,28},{1,5},{5,9},{9,... | collective-permute-start | bytes 49160 | tf_op jit(solution)/shard_map/ppermute | solution.py:787
  267.6 4.9 shard_map.418
  273.8 11.8 %collective-permute-start.24 = (bf16[1024,256]{1,0:T(8,128)(2,1)}, bf16[1024,256]{1,0:T(8,128)(2,1)S(1)}, u32[]{:S(2)}, u32[]{:S(2)}) collective-permute-start(bf16[1024,256]{1,0:T(8,128)(2,1)} %get-tuple-element.118.grad_ref), channel_id=1, source_target_pairs={{0,1},{1,2},{2,3},{4,5},{5,6},{6,7},{8,9},{9,10},{10,11},{12,13},{... | collective-permute-start | bytes 1572872 | tf_op jit(solution)/shard_map/ppermute | solution.py:787
  285.6 3.0 add_convert_fusion.1
  290.7 2.0 pad_maximum_fusion.refs_1_
  292.7 5.0 collective-permute-start.22
  298.7 9.4 %convolution_convert_fusion.pass_ref = bf16[4608,512]{1,0:T(8,128)(2,1)} fusion(bf16[1024,4608]{1,0:T(8,128)(2,1)} %get-tuple-element.121, bf16[1024,512]{1,0:T(8,128)(2,1)} %shard_map.419), kind=kOutput, calls=%fused_computation | convolution fusion | flops 4834197504 | bytes 15204352 | tf_op jit(solution)/shard_map/nk,nc->kc/dot_general | solution.py:974
  309.4 4.6 collective-permute-start.28
  314.0 1.8 collective-permute-done.22
  316.4 5.7 %collective-permute-done.20 = bf16[896,512]{1,0:T(8,128)(2,1)S(1)} collective-permute-done((bf16[896,512]{1,0:T(8,128)(2,1)}, bf16[896,512]{1,0:T(8,128)(2,1)S(1)}, u32[]{:S(2)}, u32[]{:S(2)}) %collective-permute-start.20) | collective-permute-done | bytes 917536 | tf_op jit(solution)/shard_map/ppermute | solution.py:800
  323.3 6.1 %shard_map.420 = (bf16[4608,512]{1,0:T(8,128)(2,1)}, f32[2048,512]{1,0:T(8,128)}, bf16[512,512]{1,0:T(8,128)(2,1)}) custom-call(bf16[4608,512]{1,0:T(8,128)(2,1)} %convolution_convert_fusion.pass_ref, bf16[896,512]{1,0:T(8,128)(2,1)} %copy-done, s32[1,1024]{1,0:T(1,128)} %broadcast_subtract_fusion.index_ref, ...), custom_call_target="tpu_custom_call", output_to_operand_aliasing={{0}: (0, {})} | custom-call | flops 2415919104 | bytes 17246208 | tf_op jit(solution)/shard_map/pallas_call | solution.py:34
  330.7 2.9 collective-permute-done.21
  335.6 2.0 constant_dynamic-slice_fusion.13
  338.9 5.0 collective-permute-start.29
  344.0 3.7 shard_map.421.refs_8_
  349.6 13.1 %collective-permute-done.41 = bf16[208,512]{1,0:T(8,128)(2,1)S(1)} collective-permute-done((bf16[208,512]{1,0:T(8,128)(2,1)S(1)}, bf16[208,512]{1,0:T(8,128)(2,1)S(1)}, u32[]{:S(2)}, u32[]{:S(2)}) %collective-permute-start.41) | collective-permute-done | bytes 213024 | tf_op jit(solution)/shard_map/ppermute | solution.py:800
  363.3 6.1 %shard_map.422 = bf16[2048,512]{1,0:T(8,128)(2,1)S(1)} custom-call(bf16[448,512]{1,0:T(8,128)(2,1)S(1)} %add_convert_fusion.8.refs_0_, bf16[384,512]{1,0:T(8,128)(2,1)S(1)} %add_convert_fusion.9.refs_1_, s32[1,1024]{1,0:T(1,128)S(1)} %broadcast_subtract_fusion.1.refs_2_, s32[1,1024]{1,0:T(1,128)S(1)} %broadcast_subtract_fusion.3.refs_3_, ...), custom_call_target="tpu_custom_call" | custom-call | flops 4294967296 | bytes 8388608 | tf_op jit(solution)/shard_map/pallas_call | solution.py:208
  369.5 5.7 %collective-permute-done.42 = bf16[208,512]{1,0:T(8,128)(2,1)S(1)} collective-permute-done((bf16[208,512]{1,0:T(8,128)(2,1)S(1)}, bf16[208,512]{1,0:T(8,128)(2,1)S(1)}, u32[]{:S(2)}, u32[]{:S(2)}) %collective-permute-start.42) | collective-permute-done | bytes 213024 | tf_op jit(solution)/shard_map/ppermute | solution.py:800
  378.9 13.5 %collective-permute-done.50 = bf16[640,512]{1,0:T(8,128)(2,1)S(1)} collective-permute-done((bf16[640,512]{1,0:T(8,128)(2,1)S(1)}, bf16[640,512]{1,0:T(8,128)(2,1)S(1)}, u32[]{:S(2)}, u32[]{:S(2)}) %collective-permute-start.50) | collective-permute-done | bytes 655392 | tf_op jit(solution)/shard_map/ppermute | solution.py:800
  395.4 6.3 %collective-permute-done.51 = bf16[320,512]{1,0:T(8,128)(2,1)S(1)} collective-permute-done((bf16[320,512]{1,0:T(8,128)(2,1)S(1)}, bf16[320,512]{1,0:T(8,128)(2,1)S(1)}, u32[]{:S(2)}, u32[]{:S(2)}) %collective-permute-start.51) | collective-permute-done | bytes 327712 | tf_op jit(solution)/shard_map/ppermute | solution.py:800
  406.6 5.0 collective-permute-done.55
  414.9 3.8 collective-permute-done.46
  419.8 2.6 collective-permute-start.57
  422.5 2.9 collective-permute-done.44
  425.8 3.9 collective-permute-start.45
  430.5 10.1 %collective-permute-done.47 = bf16[768,512]{1,0:T(8,128)(2,1)S(1)} collective-permute-done((bf16[768,512]{1,0:T(8,128)(2,1)S(1)}, bf16[768,512]{1,0:T(8,128)(2,1)S(1)}, u32[]{:S(2)}, u32[]{:S(2)}) %collective-permute-start.47) | collective-permute-done | bytes 786464 | tf_op jit(solution)/shard_map/ppermute | solution.py:800
  441.4 2.6 collective-permute-start.61
  445.3 4.1 collective-permute-done.61
  450.0 5.2 %collective-permute-done.59 = bf16[320,512]{1,0:T(8,128)(2,1)S(1)} collective-permute-done((bf16[320,512]{1,0:T(8,128)(2,1)S(1)}, bf16[320,512]{1,0:T(8,128)(2,1)S(1)}, u32[]{:S(2)}, u32[]{:S(2)}) %collective-permute-start.59) | collective-permute-done | bytes 327712 | tf_op jit(solution)/shard_map/ppermute | solution.py:800
  455.5 2.4 collective-permute-start.60
  458.2 7.1 %collective-permute-done.62 = bf16[640,512]{1,0:T(8,128)(2,1)S(1)} collective-permute-done((bf16[640,512]{1,0:T(8,128)(2,1)S(1)}, bf16[640,512]{1,0:T(8,128)(2,1)S(1)}, u32[]{:S(2)}, u32[]{:S(2)}) %collective-permute-start.62) | collective-permute-done | bytes 655392 | tf_op jit(solution)/shard_map/ppermute | solution.py:800
  467.3 2.1 collective-permute-start.36
  469.5 4.0 collective-permute-done.36
  473.6 1.8 collective-permute-start.37
  475.8 4.2 collective-permute-done.37
  480.2 4.4 collective-permute-done.34
  487.8 2.7 collective-permute-done.39.refs_2_
  491.4 3.5 shard_map.423.refs_1_
  495.0 6.9 %shard_map.424 = (f32[4608,512]{1,0:T(8,128)}, f32[512,512]{1,0:T(8,128)}, f32[512,512]{1,0:T(8,128)}, f32[512,512]{1,0:T(8,128)}, f32[512,512]{1,0:T(8,128)}) custom-call(s32[1]{0:T(128)} %bitcast.38.refs_0_.refs_2_, bf16[3328,512]{1,0:T(8,128)(2,1)} %copy-done.7, bf16[3328,512]{1,0:T(8,128)(2,1)} %collective-permute-done.48.refs_2_), custom_call_target="tpu_custom_call" | custom-call | bytes 20447236 | tf_op jit(solution)/shard_map/pallas_call | solution.py:34
  502.0 5.4 %shard_map.425 = (f32[4608,512]{1,0:T(8,128)}, f32[256,512]{1,0:T(8,128)}, f32[256,512]{1,0:T(8,128)}) custom-call(f32[4608,512]{1,0:T(8,128)} %get-tuple-element.130.refs_0_, f32[4096,256]{1,0:T(8,128)} %shard_map.423.refs_1_, s32[1]{0:T(128)} %bitcast.38.refs_0_.refs_2_, bf16[2560,512]{1,0:T(8,128)(2,1)} %copy-done.8, ...), custom_call_target="tpu_custom_call" | custom-call | bytes 29360132 | tf_op jit(solution)/shard_map/pallas_call | solution.py:34
  (347 shorter events, 90.6 us)
Async XLA Ops:
  0.7 19.1 %collective-permute-start.1 = (s32[1,1024]{1,0:T(1,128)}, s32[1,1024]{1,0:T(1,128)S(1)}, u32[]{:S(2)}, u32[]{:S(2)}) collective-permute-start(s32[1,1024]{1,0:T(1,128)} %param.26), channel_id=1, source_target_pairs={{0,2},{1,3},{2,0},{3,1},{4,6},{5,7},{6,4},{7,5},{8,10},{9,11},{10,... | collective-permute-start | bytes 12296 | tf_op jit(solution)/shard_map/ppermute | solution.py:792
  4.8 7.9 %collective-permute-start = (s32[1,1024]{1,0:T(1,128)}, s32[1,1024]{1,0:T(1,128)S(1)}, u32[]{:S(2)}, u32[]{:S(2)}) collective-permute-start(s32[1,1024]{1,0:T(1,128)} %param.26), channel_id=1, source_target_pairs={{0,3},{1,0},{2,1},{3,2},{4,7},{5,4},{6,5},{7,6},{8,11},{9,8},{10,9... | collective-permute-start | bytes 12296 | tf_op jit(solution)/shard_map/ppermute | solution.py:792
  6.1 6.3 %collective-permute-start.2 = (s32[1,1024]{1,0:T(1,128)}, s32[1,1024]{1,0:T(1,128)S(1)}, u32[]{:S(2)}, u32[]{:S(2)}) collective-permute-start(s32[1,1024]{1,0:T(1,128)} %param.26), channel_id=1, source_target_pairs={{0,1},{1,2},{2,3},{3,0},{4,5},{5,6},{6,7},{7,4},{8,9},{9,10},{10,1... | collective-permute-start | bytes 12296 | tf_op jit(solution)/shard_map/ppermute | solution.py:792
  24.2 37.5 %collective-permute-start.4 = (bf16[1024,256]{1,0:T(8,128)(2,1)S(1)}, bf16[1024,256]{1,0:T(8,128)(2,1)S(1)}, u32[]{:S(2)}, u32[]{:S(2)}) collective-permute-start(bf16[1024,256]{1,0:T(8,128)(2,1)S(1)} %shard_map.409.refs_1_), channel_id=1, source_target_pairs={{0,2},{1,3},{2,0},{3,1},{4,6},{5,7},{6,4},{7,5},{8,10},{9,11},{10,... | collective-permute-start | bytes 1572872 | tf_op jit(solution)/shard_map/ppermute | solution.py:792
  25.3 36.4 %collective-permute-start.3 = (bf16[1024,256]{1,0:T(8,128)(2,1)S(1)}, bf16[1024,256]{1,0:T(8,128)(2,1)S(1)}, u32[]{:S(2)}, u32[]{:S(2)}) collective-permute-start(bf16[1024,256]{1,0:T(8,128)(2,1)S(1)} %shard_map.408.refs_0_), channel_id=1, source_target_pairs={{0,1},{1,2},{2,3},{3,0},{4,5},{5,6},{6,7},{7,4},{8,9},{9,10},{10,1... | collective-permute-start | bytes 1572872 | tf_op jit(solution)/shard_map/ppermute | solution.py:792
  28.0 33.7 %collective-permute-start.5 = (bf16[1024,256]{1,0:T(8,128)(2,1)S(1)}, bf16[1024,256]{1,0:T(8,128)(2,1)S(1)}, u32[]{:S(2)}, u32[]{:S(2)}) collective-permute-start(bf16[1024,256]{1,0:T(8,128)(2,1)S(1)} %shard_map.410.refs_2_), channel_id=1, source_target_pairs={{0,3},{1,0},{2,1},{3,2},{4,7},{5,4},{6,5},{7,6},{8,11},{9,8},{10,9... | collective-permute-start | bytes 1572872 | tf_op jit(solution)/shard_map/ppermute | solution.py:792
  66.9 5.3 %collective-permute-start.6 = (f32[72,512]{1,0:T(8,128)}, f32[72,512]{1,0:T(8,128)S(1)}, u32[]{:S(2)}, u32[]{:S(2)}) collective-permute-start(f32[72,512]{1,0:T(8,128)} %get-tuple-element.82), channel_id=1, source_target_pairs={{0,4},{4,8},{8,12},{12,16},{16,20},{20,24},{24,28},{1,5},{5,9},{9,... | collective-permute-start | bytes 442376 | tf_op jit(solution)/shard_map/ppermute | solution.py:787
  68.2 5.2 %collective-permute-start.7 = (f32[72,512]{1,0:T(8,128)}, f32[72,512]{1,0:T(8,128)S(1)}, u32[]{:S(2)}, u32[]{:S(2)}) collective-permute-start(f32[72,512]{1,0:T(8,128)} %get-tuple-element.83), channel_id=1, source_target_pairs={{4,0},{8,4},{12,8},{16,12},{20,16},{24,20},{28,24},{5,1},{9,5},{13... | collective-permute-start | bytes 442376 | tf_op jit(solution)/shard_map/ppermute | solution.py:787
  88.4 7.1 %collective-permute-start.8 = (f32[72,512]{1,0:T(8,128)}, f32[72,512]{1,0:T(8,128)S(1)}, u32[]{:S(2)}, u32[]{:S(2)}) collective-permute-start(f32[72,512]{1,0:T(8,128)} %get-tuple-element.86), channel_id=1, source_target_pairs={{0,4},{4,8},{8,12},{12,16},{16,20},{20,24},{24,28},{1,5},{5,9},{9,... | collective-permute-start | bytes 442376 | tf_op jit(solution)/shard_map/ppermute | solution.py:787
  94.0 3.5 collective-permute-start.9
  114.2 10.0 %collective-permute-start.10 = (bf16[1104,512]{1,0:T(8,128)(2,1)}, bf16[1104,512]{1,0:T(8,128)(2,1)S(1)}, u32[]{:S(2)}, u32[]{:S(2)}) collective-permute-start(bf16[1104,512]{1,0:T(8,128)(2,1)} %get-tuple-element.90), channel_id=1, source_target_pairs={{0,4},{4,8},{8,12},{12,16},{16,20},{20,24},{24,28},{1,5},{5,9},{9,... | collective-permute-start | bytes 3391496 | tf_op jit(solution)/shard_map/ppermute | solution.py:787
  120.1 4.9 collective-permute-start.11
  151.5 39.2 %collective-permute-start.13 = (bf16[1104,512]{1,0:T(8,128)(2,1)}, bf16[1104,512]{1,0:T(8,128)(2,1)S(1)}, u32[]{:S(2)}, u32[]{:S(2)}) collective-permute-start(bf16[1104,512]{1,0:T(8,128)(2,1)} %get-tuple-element.101.refs_2_), channel_id=1, source_target_pairs={{4,0},{8,4},{12,8},{16,12},{20,16},{24,20},{28,24},{5,1},{9,5},{13... | collective-permute-start | bytes 3391496 | tf_op jit(solution)/shard_map/ppermute | solution.py:787
  152.8 37.9 %collective-permute-start.12 = (bf16[1104,512]{1,0:T(8,128)(2,1)}, bf16[1104,512]{1,0:T(8,128)(2,1)S(1)}, u32[]{:S(2)}, u32[]{:S(2)}) collective-permute-start(bf16[1104,512]{1,0:T(8,128)(2,1)} %get-tuple-element.102.refs_3_), channel_id=1, source_target_pairs={{0,4},{4,8},{8,12},{12,16},{16,20},{20,24},{24,28},{1,5},{5,9},{9,... | collective-permute-start | bytes 3391496 | tf_op jit(solution)/shard_map/ppermute | solution.py:787
  221.2 45.8 %collective-permute-start.16 = (bf16[2304,512]{1,0:T(8,128)(2,1)}, bf16[2304,512]{1,0:T(8,128)(2,1)}, u32[]{:S(2)}, u32[]{:S(2)}) collective-permute-start(bf16[2304,512]{1,0:T(8,128)(2,1)} %constant_dynamic-slice_fusion.28), channel_id=1, source_target_pairs={{0,4},{4,0},{8,12},{12,8},{16,20},{20,16},{24,28},{28,24},{1,5},{5... | collective-permute-start | bytes 7077896 | tf_op jit(solution)/shard_map/ppermute | solution.py:800
  232.3 33.7 %collective-permute-start.17 = (bf16[1024,512]{1,0:T(8,128)(2,1)S(1)}, bf16[1024,512]{1,0:T(8,128)(2,1)S(1)}, u32[]{:S(2)}, u32[]{:S(2)}) collective-permute-start(bf16[1024,512]{1,0:T(8,128)(2,1)S(1)} %constant_dynamic-slice_fusion.27), channel_id=1, source_target_pairs={{0,4},{4,0},{8,12},{12,8},{16,20},{20,16},{24,28},{28,24},{1,5},{5... | collective-permute-start | bytes 3145736 | tf_op jit(solution)/shard_map/ppermute | solution.py:800
  232.4 4.8 collective-permute-start.14
  234.8 7.8 %collective-permute-start.15 = (f32[72,512]{1,0:T(8,128)S(1)}, f32[72,512]{1,0:T(8,128)S(1)}, u32[]{:S(2)}, u32[]{:S(2)}) collective-permute-start(f32[72,512]{1,0:T(8,128)S(1)} %copy-done.36), channel_id=1, source_target_pairs={{4,0},{8,4},{12,8},{16,12},{20,16},{24,20},{28,24},{5,1},{9,5},{13... | collective-permute-start | bytes 442376 | tf_op jit(solution)/shard_map/ppermute | solution.py:787
  258.1 7.9 %collective-permute-start.18 = (f32[8,512]{1,0:T(8,128)}, f32[8,512]{1,0:T(8,128)S(1)}, u32[]{:S(2)}, u32[]{:S(2)}) collective-permute-start(f32[8,512]{1,0:T(8,128)} %get-tuple-element.114), channel_id=1, source_target_pairs={{0,4},{4,8},{8,12},{12,16},{16,20},{20,24},{24,28},{1,5},{5,9},{9,... | collective-permute-start | bytes 49160 | tf_op jit(solution)/shard_map/ppermute | solution.py:787
  263.7 3.3 collective-permute-start.19
  272.5 35.5 %collective-permute-start.25 = (bf16[1024,256]{1,0:T(8,128)(2,1)}, bf16[1024,256]{1,0:T(8,128)(2,1)S(1)}, u32[]{:S(2)}, u32[]{:S(2)}) collective-permute-start(bf16[1024,256]{1,0:T(8,128)(2,1)} %get-tuple-element.118.grad_ref), channel_id=1, source_target_pairs={{1,0},{2,1},{3,2},{5,4},{6,5},{7,6},{9,8},{10,9},{11,10},{13,12},{... | collective-permute-start | bytes 1572872 | tf_op jit(solution)/shard_map/ppermute | solution.py:787
  273.8 35.6 %collective-permute-start.24 = (bf16[1024,256]{1,0:T(8,128)(2,1)}, bf16[1024,256]{1,0:T(8,128)(2,1)S(1)}, u32[]{:S(2)}, u32[]{:S(2)}) collective-permute-start(bf16[1024,256]{1,0:T(8,128)(2,1)} %get-tuple-element.118.grad_ref), channel_id=1, source_target_pairs={{0,1},{1,2},{2,3},{4,5},{5,6},{6,7},{8,9},{9,10},{10,11},{12,13},{... | collective-permute-start | bytes 1572872 | tf_op jit(solution)/shard_map/ppermute | solution.py:787
  292.7 23.2 %collective-permute-start.22 = (bf16[768,512]{1,0:T(8,128)(2,1)S(1)}, bf16[768,512]{1,0:T(8,128)(2,1)S(1)}, u32[]{:S(2)}, u32[]{:S(2)}) collective-permute-start(bf16[768,512]{1,0:T(8,128)(2,1)S(1)} %constant_dynamic-slice_fusion.24), channel_id=1, source_target_pairs={{0,16},{4,20},{8,24},{12,28},{16,0},{20,4},{24,8},{28,12},{1,17},{... | collective-permute-start | bytes 2359304 | tf_op jit(solution)/shard_map/ppermute | solution.py:800
  298.6 23.5 %collective-permute-start.20 = (bf16[896,512]{1,0:T(8,128)(2,1)}, bf16[896,512]{1,0:T(8,128)(2,1)S(1)}, u32[]{:S(2)}, u32[]{:S(2)}) collective-permute-start(bf16[896,512]{1,0:T(8,128)(2,1)} %constant_dynamic-slice_fusion.26), channel_id=1, source_target_pairs={{0,8},{4,12},{8,0},{12,4},{16,24},{20,28},{24,16},{28,20},{1,9},{5... | collective-permute-start | bytes 2752520 | tf_op jit(solution)/shard_map/ppermute | solution.py:800
  308.0 29.6 %collective-permute-start.26 = (bf16[1024,256]{1,0:T(8,128)(2,1)S(1)}, bf16[1024,256]{1,0:T(8,128)(2,1)S(1)}, u32[]{:S(2)}, u32[]{:S(2)}) collective-permute-start(bf16[1024,256]{1,0:T(8,128)(2,1)S(1)} %collective-permute-done.25.refs_7_), channel_id=1, source_target_pairs={{1,0},{2,1},{3,2},{5,4},{6,5},{7,6},{9,8},{10,9},{11,10},{13,12},{... | collective-permute-start | bytes 1572872 | tf_op jit(solution)/shard_map/ppermute | solution.py:787
  309.4 29.5 %collective-permute-start.28 = (bf16[1024,256]{1,0:T(8,128)(2,1)S(1)}, bf16[1024,256]{1,0:T(8,128)(2,1)S(1)}, u32[]{:S(2)}, u32[]{:S(2)}) collective-permute-start(bf16[1024,256]{1,0:T(8,128)(2,1)S(1)} %collective-permute-done.24.refs_4_), channel_id=1, source_target_pairs={{0,1},{1,2},{2,3},{4,5},{5,6},{6,7},{8,9},{9,10},{10,11},{12,13},{... | collective-permute-start | bytes 1572872 | tf_op jit(solution)/shard_map/ppermute | solution.py:787
  316.1 14.4 %collective-permute-start.23 = (bf16[384,512]{1,0:T(8,128)(2,1)S(1)}, bf16[384,512]{1,0:T(8,128)(2,1)S(1)}, u32[]{:S(2)}, u32[]{:S(2)}) collective-permute-start(bf16[384,512]{1,0:T(8,128)(2,1)S(1)} %constant_dynamic-slice_fusion.23), channel_id=1, source_target_pairs={{0,8},{4,12},{8,0},{12,4},{16,24},{20,28},{24,16},{28,20},{1,9},{5... | collective-permute-start | bytes 1179656 | tf_op jit(solution)/shard_map/ppermute | solution.py:800
  322.5 11.1 %collective-permute-start.21 = (bf16[448,512]{1,0:T(8,128)(2,1)S(1)}, bf16[448,512]{1,0:T(8,128)(2,1)S(1)}, u32[]{:S(2)}, u32[]{:S(2)}) collective-permute-start(bf16[448,512]{1,0:T(8,128)(2,1)S(1)} %constant_dynamic-slice_fusion.25), channel_id=1, source_target_pairs={{0,16},{4,20},{8,24},{12,28},{16,0},{20,4},{24,8},{28,12},{1,17},{... | collective-permute-start | bytes 1376264 | tf_op jit(solution)/shard_map/ppermute | solution.py:800
  330.5 19.0 %collective-permute-start.52 = (bf16[256,512]{1,0:T(8,128)(2,1)S(1)}, bf16[256,512]{1,0:T(8,128)(2,1)S(1)}, u32[]{:S(2)}, u32[]{:S(2)}) collective-permute-start(bf16[256,512]{1,0:T(8,128)(2,1)S(1)} %constant_dynamic-slice_fusion.8), channel_id=1, source_target_pairs={{0,4},{4,0},{8,12},{12,8},{16,20},{20,16},{24,28},{28,24},{1,5},{5... | collective-permute-start | bytes 786440 | tf_op jit(solution)/shard_map/ppermute | solution.py:800
  333.8 13.9 %collective-permute-start.40 = (bf16[416,512]{1,0:T(8,128)(2,1)S(1)}, bf16[416,512]{1,0:T(8,128)(2,1)S(1)}, u32[]{:S(2)}, u32[]{:S(2)}) collective-permute-start(bf16[416,512]{1,0:T(8,128)(2,1)S(1)} %pad_maximum_fusion.7), channel_id=1, source_target_pairs={{0,1},{1,0},{2,3},{3,2},{4,5},{5,4},{6,7},{7,6},{8,9},{9,8},{10,11... | collective-permute-start | bytes 1277960 | tf_op jit(solution)/shard_map/ppermute | solution.py:800
  337.5 37.9 %collective-permute-start.49 = (bf16[2304,512]{1,0:T(8,128)(2,1)S(1)}, bf16[2304,512]{1,0:T(8,128)(2,1)S(1)}, u32[]{:S(2)}, u32[]{:S(2)}) collective-permute-start(bf16[2304,512]{1,0:T(8,128)(2,1)S(1)} %constant_dynamic-slice_fusion.13), channel_id=1, source_target_pairs={{0,4},{4,0},{8,12},{12,8},{16,20},{20,16},{24,28},{28,24},{1,5},{5... | collective-permute-start | bytes 7077896 | tf_op jit(solution)/shard_map/ppermute | solution.py:800
  337.6 25.6 %collective-permute-start.27 = (bf16[1024,256]{1,0:T(8,128)(2,1)S(1)}, bf16[1024,256]{1,0:T(8,128)(2,1)S(1)}, u32[]{:S(2)}, u32[]{:S(2)}) collective-permute-start(bf16[1024,256]{1,0:T(8,128)(2,1)S(1)} %collective-permute-done.26.refs_4_), channel_id=1, source_target_pairs={{1,0},{2,1},{3,2},{5,4},{6,5},{7,6},{9,8},{10,9},{11,10},{13,12},{... | collective-permute-start | bytes 1572872 | tf_op jit(solution)/shard_map/ppermute | solution.py:787
  338.9 24.3 %collective-permute-start.29 = (bf16[1024,256]{1,0:T(8,128)(2,1)S(1)}, bf16[1024,256]{1,0:T(8,128)(2,1)S(1)}, u32[]{:S(2)}, u32[]{:S(2)}) collective-permute-start(bf16[1024,256]{1,0:T(8,128)(2,1)S(1)} %collective-permute-done.28.refs_3_), channel_id=1, source_target_pairs={{0,1},{1,2},{2,3},{4,5},{5,6},{6,7},{8,9},{9,10},{10,11},{12,13},{... | collective-permute-start | bytes 1572872 | tf_op jit(solution)/shard_map/ppermute | solution.py:787
  347.9 14.8 %collective-permute-start.41 = (bf16[208,512]{1,0:T(8,128)(2,1)S(1)}, bf16[208,512]{1,0:T(8,128)(2,1)S(1)}, u32[]{:S(2)}, u32[]{:S(2)}) collective-permute-start(bf16[208,512]{1,0:T(8,128)(2,1)S(1)} %pad_maximum_fusion.14), channel_id=1, source_target_pairs={{0,2},{1,3},{2,0},{3,1},{4,6},{5,7},{6,4},{7,5},{8,10},{9,11},{10,... | collective-permute-start | bytes 638984 | tf_op jit(solution)/shard_map/ppermute | solution.py:800
  362.8 12.4 %collective-permute-start.42 = (bf16[208,512]{1,0:T(8,128)(2,1)S(1)}, bf16[208,512]{1,0:T(8,128)(2,1)S(1)}, u32[]{:S(2)}, u32[]{:S(2)}) collective-permute-start(bf16[208,512]{1,0:T(8,128)(2,1)S(1)} %pad_maximum_fusion.15), channel_id=1, source_target_pairs={{0,2},{1,3},{2,0},{3,1},{4,6},{5,7},{6,4},{7,5},{8,10},{9,11},{10,... | collective-permute-start | bytes 638984 | tf_op jit(solution)/shard_map/ppermute | solution.py:800
  369.4 9.2 %collective-permute-start.30 = (bf16[1024,512]{1,0:T(8,128)(2,1)S(1)}, bf16[1024,512]{1,0:T(8,128)(2,1)S(1)}, u32[]{:S(2)}, u32[]{:S(2)}) collective-permute-start(bf16[1024,512]{1,0:T(8,128)(2,1)S(1)} %constant_dynamic-slice_fusion.22), channel_id=1, source_target_pairs={{0,4},{4,0},{8,12},{12,8},{16,20},{20,16},{24,28},{28,24},{1,5},{5... | collective-permute-start | bytes 3145736 | tf_op jit(solution)/shard_map/ppermute | solution.py:800
  375.4 30.7 %collective-permute-start.43 = (bf16[416,512]{1,0:T(8,128)(2,1)S(1)}, bf16[416,512]{1,0:T(8,128)(2,1)S(1)}, u32[]{:S(2)}, u32[]{:S(2)}) collective-permute-start(bf16[416,512]{1,0:T(8,128)(2,1)S(1)} %pad_maximum_fusion.8), channel_id=1, source_target_pairs={{0,1},{1,0},{2,3},{3,2},{4,5},{5,4},{6,7},{7,6},{8,9},{9,8},{10,11... | collective-permute-start | bytes 1277960 | tf_op jit(solution)/shard_map/ppermute | solution.py:800
  376.4 16.1 %collective-permute-start.50 = (bf16[640,512]{1,0:T(8,128)(2,1)S(1)}, bf16[640,512]{1,0:T(8,128)(2,1)S(1)}, u32[]{:S(2)}, u32[]{:S(2)}) collective-permute-start(bf16[640,512]{1,0:T(8,128)(2,1)S(1)} %constant_dynamic-slice_fusion.12), channel_id=1, source_target_pairs={{0,8},{4,12},{8,0},{12,4},{16,24},{20,28},{24,16},{28,20},{1,9},{5... | collective-permute-start | bytes 1966088 | tf_op jit(solution)/shard_map/ppermute | solution.py:800
  377.5 17.0 %collective-permute-start.53 = (bf16[640,512]{1,0:T(8,128)(2,1)S(1)}, bf16[640,512]{1,0:T(8,128)(2,1)S(1)}, u32[]{:S(2)}, u32[]{:S(2)}) collective-permute-start(bf16[640,512]{1,0:T(8,128)(2,1)S(1)} %pad_maximum_fusion.5), channel_id=1, source_target_pairs={{0,16},{4,20},{8,24},{12,28},{16,0},{20,4},{24,8},{28,12},{1,17},{... | collective-permute-start | bytes 1966088 | tf_op jit(solution)/shard_map/ppermute | solution.py:800
  392.7 9.0 %collective-permute-start.51 = (bf16[320,512]{1,0:T(8,128)(2,1)S(1)}, bf16[320,512]{1,0:T(8,128)(2,1)S(1)}, u32[]{:S(2)}, u32[]{:S(2)}) collective-permute-start(bf16[320,512]{1,0:T(8,128)(2,1)S(1)} %constant_dynamic-slice_fusion.11), channel_id=1, source_target_pairs={{0,16},{4,20},{8,24},{12,28},{16,0},{20,4},{24,8},{28,12},{1,17},{... | collective-permute-start | bytes 983048 | tf_op jit(solution)/shard_map/ppermute | solution.py:800
  394.8 8.8 %collective-permute-start.54 = (bf16[320,512]{1,0:T(8,128)(2,1)S(1)}, bf16[320,512]{1,0:T(8,128)(2,1)S(1)}, u32[]{:S(2)}, u32[]{:S(2)}) collective-permute-start(bf16[320,512]{1,0:T(8,128)(2,1)S(1)} %pad_maximum_fusion.11), channel_id=1, source_target_pairs={{0,8},{4,12},{8,0},{12,4},{16,24},{20,28},{24,16},{28,20},{1,9},{5... | collective-permute-start | bytes 983048 | tf_op jit(solution)/shard_map/ppermute | solution.py:800
  403.7 7.9 %collective-permute-start.55 = (bf16[320,512]{1,0:T(8,128)(2,1)S(1)}, bf16[320,512]{1,0:T(8,128)(2,1)S(1)}, u32[]{:S(2)}, u32[]{:S(2)}) collective-permute-start(bf16[320,512]{1,0:T(8,128)(2,1)S(1)} %pad_maximum_fusion.12), channel_id=1, source_target_pairs={{0,1},{1,0},{2,3},{3,2},{4,5},{5,4},{6,7},{7,6},{8,9},{9,8},{10,11... | collective-permute-start | bytes 983048 | tf_op jit(solution)/shard_map/ppermute | solution.py:800
  403.8 18.5 %collective-permute-start.31 = (bf16[256,512]{1,0:T(8,128)(2,1)S(1)}, bf16[256,512]{1,0:T(8,128)(2,1)S(1)}, u32[]{:S(2)}, u32[]{:S(2)}) collective-permute-start(bf16[256,512]{1,0:T(8,128)(2,1)S(1)} %constant_dynamic-slice_fusion.21), channel_id=1, source_target_pairs={{0,8},{4,12},{8,0},{12,4},{16,24},{20,28},{24,16},{28,20},{1,9},{5... | collective-permute-start | bytes 786440 | tf_op jit(solution)/shard_map/ppermute | solution.py:800
  404.3 62.9 %collective-permute-start.35 = (bf16[256,512]{1,0:T(8,128)(2,1)S(1)}, bf16[256,512]{1,0:T(8,128)(2,1)S(1)}, u32[]{:S(2)}, u32[]{:S(2)}) collective-permute-start(bf16[256,512]{1,0:T(8,128)(2,1)S(1)} %constant_dynamic-slice_fusion.19), channel_id=1, source_target_pairs={{0,16},{4,20},{8,24},{12,28},{16,0},{20,4},{24,8},{28,12},{1,17},{... | collective-permute-start | bytes 786440 | tf_op jit(solution)/shard_map/ppermute | solution.py:800
  406.2 12.5 %collective-permute-start.46 = (bf16[384,512]{1,0:T(8,128)(2,1)S(1)}, bf16[384,512]{1,0:T(8,128)(2,1)S(1)}, u32[]{:S(2)}, u32[]{:S(2)}) collective-permute-start(bf16[384,512]{1,0:T(8,128)(2,1)S(1)} %maximum_select_fusion.11), channel_id=1, source_target_pairs={{0,8},{4,12},{8,0},{12,4},{16,24},{20,28},{24,16},{28,20},{1,9},{5... | collective-permute-start | bytes 1179656 | tf_op jit(solution)/shard_map/ppermute | solution.py:800
  411.8 7.8 %collective-permute-start.56 = (bf16[160,512]{1,0:T(8,128)(2,1)S(1)}, bf16[160,512]{1,0:T(8,128)(2,1)S(1)}, u32[]{:S(2)}, u32[]{:S(2)}) collective-permute-start(bf16[160,512]{1,0:T(8,128)(2,1)S(1)} %pad_maximum_fusion.18), channel_id=1, source_target_pairs={{0,2},{1,3},{2,0},{3,1},{4,6},{5,7},{6,4},{7,5},{8,10},{9,11},{10,... | collective-permute-start | bytes 491528 | tf_op jit(solution)/shard_map/ppermute | solution.py:800
  413.3 12.1 %collective-permute-start.44 = (bf16[448,512]{1,0:T(8,128)(2,1)S(1)}, bf16[448,512]{1,0:T(8,128)(2,1)S(1)}, u32[]{:S(2)}, u32[]{:S(2)}) collective-permute-start(bf16[448,512]{1,0:T(8,128)(2,1)S(1)} %maximum_select_fusion.10), channel_id=1, source_target_pairs={{0,16},{4,20},{8,24},{12,28},{16,0},{20,4},{24,8},{28,12},{1,17},{... | collective-permute-start | bytes 1376264 | tf_op jit(solution)/shard_map/ppermute | solution.py:800
  419.1 21.6 %collective-permute-start.47 = (bf16[768,512]{1,0:T(8,128)(2,1)S(1)}, bf16[768,512]{1,0:T(8,128)(2,1)S(1)}, u32[]{:S(2)}, u32[]{:S(2)}) collective-permute-start(bf16[768,512]{1,0:T(8,128)(2,1)S(1)} %maximum_select_fusion.5), channel_id=1, source_target_pairs={{0,16},{4,20},{8,24},{12,28},{16,0},{20,4},{24,8},{28,12},{1,17},{... | collective-permute-start | bytes 2359304 | tf_op jit(solution)/shard_map/ppermute | solution.py:800
  419.8 9.9 %collective-permute-start.57 = (bf16[160,512]{1,0:T(8,128)(2,1)S(1)}, bf16[160,512]{1,0:T(8,128)(2,1)S(1)}, u32[]{:S(2)}, u32[]{:S(2)}) collective-permute-start(bf16[160,512]{1,0:T(8,128)(2,1)S(1)} %fusion.5), channel_id=1, source_target_pairs={{0,2},{1,3},{2,0},{3,1},{4,6},{5,7},{6,4},{7,5},{8,10},{9,11},{10,... | collective-permute-start | bytes 491528 | tf_op jit(solution)/shard_map/ppermute | solution.py:800
  425.8 18.2 %collective-permute-start.45 = (bf16[896,512]{1,0:T(8,128)(2,1)S(1)}, bf16[896,512]{1,0:T(8,128)(2,1)S(1)}, u32[]{:S(2)}, u32[]{:S(2)}) collective-permute-start(bf16[896,512]{1,0:T(8,128)(2,1)S(1)} %maximum_select_fusion.4), channel_id=1, source_target_pairs={{0,8},{4,12},{8,0},{12,4},{16,24},{20,28},{24,16},{28,20},{1,9},{5... | collective-permute-start | bytes 2752520 | tf_op jit(solution)/shard_map/ppermute | solution.py:800
  429.8 11.4 %collective-permute-start.58 = (bf16[320,512]{1,0:T(8,128)(2,1)S(1)}, bf16[320,512]{1,0:T(8,128)(2,1)S(1)}, u32[]{:S(2)}, u32[]{:S(2)}) collective-permute-start(bf16[320,512]{1,0:T(8,128)(2,1)S(1)} %fusion.3), channel_id=1, source_target_pairs={{0,1},{1,0},{2,3},{3,2},{4,5},{5,4},{6,7},{7,6},{8,9},{9,8},{10,11... | collective-permute-start | bytes 983048 | tf_op jit(solution)/shard_map/ppermute | solution.py:800
  430.2 39.3 %collective-permute-start.32 = (bf16[128,512]{1,0:T(8,128)(2,1)S(1)}, bf16[128,512]{1,0:T(8,128)(2,1)S(1)}, u32[]{:S(2)}, u32[]{:S(2)}) collective-permute-start(bf16[128,512]{1,0:T(8,128)(2,1)S(1)} %constant_dynamic-slice_fusion.20), channel_id=1, source_target_pairs={{0,16},{4,20},{8,24},{12,28},{16,0},{20,4},{24,8},{28,12},{1,17},{... | collective-permute-start | bytes 393224 | tf_op jit(solution)/shard_map/ppermute | solution.py:800
  441.4 8.0 %collective-permute-start.61 = (bf16[320,512]{1,0:T(8,128)(2,1)S(1)}, bf16[320,512]{1,0:T(8,128)(2,1)S(1)}, u32[]{:S(2)}, u32[]{:S(2)}) collective-permute-start(bf16[320,512]{1,0:T(8,128)(2,1)S(1)} %pad_maximum_fusion.13), channel_id=1, source_target_pairs={{0,8},{4,12},{8,0},{12,4},{16,24},{20,28},{24,16},{28,20},{1,9},{5... | collective-permute-start | bytes 983048 | tf_op jit(solution)/shard_map/ppermute | solution.py:800
  444.6 10.6 %collective-permute-start.59 = (bf16[320,512]{1,0:T(8,128)(2,1)S(1)}, bf16[320,512]{1,0:T(8,128)(2,1)S(1)}, u32[]{:S(2)}, u32[]{:S(2)}) collective-permute-start(bf16[320,512]{1,0:T(8,128)(2,1)S(1)} %fusion.2), channel_id=1, source_target_pairs={{0,16},{4,20},{8,24},{12,28},{16,0},{20,4},{24,8},{28,12},{1,17},{... | collective-permute-start | bytes 983048 | tf_op jit(solution)/shard_map/ppermute | solution.py:800
  449.8 15.5 %collective-permute-start.62 = (bf16[640,512]{1,0:T(8,128)(2,1)S(1)}, bf16[640,512]{1,0:T(8,128)(2,1)S(1)}, u32[]{:S(2)}, u32[]{:S(2)}) collective-permute-start(bf16[640,512]{1,0:T(8,128)(2,1)S(1)} %pad_maximum_fusion.6), channel_id=1, source_target_pairs={{0,16},{4,20},{8,24},{12,28},{16,0},{20,4},{24,8},{28,12},{1,17},{... | collective-permute-start | bytes 1966088 | tf_op jit(solution)/shard_map/ppermute | solution.py:800
  455.5 10.9 %collective-permute-start.60 = (bf16[640,512]{1,0:T(8,128)(2,1)S(1)}, bf16[640,512]{1,0:T(8,128)(2,1)S(1)}, u32[]{:S(2)}, u32[]{:S(2)}) collective-permute-start(bf16[640,512]{1,0:T(8,128)(2,1)S(1)} %maximum_select_fusion.6), channel_id=1, source_target_pairs={{0,8},{4,12},{8,0},{12,4},{16,24},{20,28},{24,16},{28,20},{1,9},{5... | collective-permute-start | bytes 1966088 | tf_op jit(solution)/shard_map/ppermute | solution.py:800
  458.1 36.9 %collective-permute-start.48 = (bf16[3328,512]{1,0:T(8,128)(2,1)S(1)}, bf16[3328,512]{1,0:T(8,128)(2,1)}, u32[]{:S(2)}, u32[]{:S(2)}) collective-permute-start(bf16[3328,512]{1,0:T(8,128)(2,1)S(1)} %pad_maximum_fusion.1.refs_1_), channel_id=1, source_target_pairs={{0,4},{4,0},{8,12},{12,8},{16,20},{20,16},{24,28},{28,24},{1,5},{5... | collective-permute-start | bytes 10223624 | tf_op jit(solution)/shard_map/ppermute | solution.py:800
  467.1 34.8 %collective-permute-start.63 = (bf16[2560,512]{1,0:T(8,128)(2,1)S(1)}, bf16[2560,512]{1,0:T(8,128)(2,1)}, u32[]{:S(2)}, u32[]{:S(2)}) collective-permute-start(bf16[2560,512]{1,0:T(8,128)(2,1)S(1)} %pad_maximum_fusion.2.refs_3_), channel_id=1, source_target_pairs={{0,4},{4,0},{8,12},{12,8},{16,20},{20,16},{24,28},{28,24},{1,5},{5... | collective-permute-start | bytes 7864328 | tf_op jit(solution)/shard_map/ppermute | solution.py:800
  467.3 6.2 %collective-permute-start.36 = (bf16[128,512]{1,0:T(8,128)(2,1)S(1)}, bf16[128,512]{1,0:T(8,128)(2,1)S(1)}, u32[]{:S(2)}, u32[]{:S(2)}) collective-permute-start(bf16[128,512]{1,0:T(8,128)(2,1)S(1)} %constant_dynamic-slice_fusion.18), channel_id=1, source_target_pairs={{0,8},{4,12},{8,0},{12,4},{16,24},{20,28},{24,16},{28,20},{1,9},{5... | collective-permute-start | bytes 393224 | tf_op jit(solution)/shard_map/ppermute | solution.py:800
  469.4 6.0 %collective-permute-start.33 = (bf16[128,512]{1,0:T(8,128)(2,1)S(1)}, bf16[128,512]{1,0:T(8,128)(2,1)S(1)}, u32[]{:S(2)}, u32[]{:S(2)}) collective-permute-start(bf16[128,512]{1,0:T(8,128)(2,1)S(1)} %add_convert_fusion.21), channel_id=1, source_target_pairs={{0,16},{4,20},{8,24},{12,28},{16,0},{20,4},{24,8},{28,12},{1,17},{... | collective-permute-start | bytes 393224 | tf_op jit(solution)/shard_map/ppermute | solution.py:800
  473.6 6.4 %collective-permute-start.37 = (bf16[128,512]{1,0:T(8,128)(2,1)S(1)}, bf16[128,512]{1,0:T(8,128)(2,1)S(1)}, u32[]{:S(2)}, u32[]{:S(2)}) collective-permute-start(bf16[128,512]{1,0:T(8,128)(2,1)S(1)} %add_convert_fusion.20), channel_id=1, source_target_pairs={{0,8},{4,12},{8,0},{12,4},{16,24},{20,28},{24,16},{28,20},{1,9},{5... | collective-permute-start | bytes 393224 | tf_op jit(solution)/shard_map/ppermute | solution.py:800
  475.5 9.1 %collective-permute-start.34 = (bf16[256,512]{1,0:T(8,128)(2,1)S(1)}, bf16[256,512]{1,0:T(8,128)(2,1)S(1)}, u32[]{:S(2)}, u32[]{:S(2)}) collective-permute-start(bf16[256,512]{1,0:T(8,128)(2,1)S(1)} %maximum_select_fusion.12), channel_id=1, source_target_pairs={{0,8},{4,12},{8,0},{12,4},{16,24},{20,28},{24,16},{28,20},{1,9},{5... | collective-permute-start | bytes 786440 | tf_op jit(solution)/shard_map/ppermute | solution.py:800
  480.1 6.4 %collective-permute-start.38 = (bf16[256,512]{1,0:T(8,128)(2,1)S(1)}, bf16[256,512]{1,0:T(8,128)(2,1)S(1)}, u32[]{:S(2)}, u32[]{:S(2)}) collective-permute-start(bf16[256,512]{1,0:T(8,128)(2,1)S(1)} %maximum_select_fusion.13), channel_id=1, source_target_pairs={{0,16},{4,20},{8,24},{12,28},{16,0},{20,4},{24,8},{28,12},{1,17},{... | collective-permute-start | bytes 786440 | tf_op jit(solution)/shard_map/ppermute | solution.py:800
  487.8 2.7 collective-permute-start.39
  (47 other events, 285.9 us)
